TPU v7x, 128 devices: a whole 4x4x4 slice. The times are simulated.
128 devices in a mesh: region: 4 (over y_hi, core), tile: 32 (over x, z, y_lo).
Axes of the slice: x: 4, y: 4 (y_hi: 2, y_lo: 2; y = y_hi * 2 + y_lo), z: 4, core: 2. Of those that a mesh axis runs over, the one named last changes fastest.
Arguments:
- fields: float32 [9, 32, 64, 4096], P(None, None, 'region', 'tile'), may hold values from -6 to 6
- buoyancy: float32 [32, 64, 4096], P(None, 'region', 'tile'), may hold values from 0.5 to 1.5
- lame_first: float32 [32, 64, 4096], P(None, 'region', 'tile'), may hold values from 0.5 to 2
- shear_modulus: float32 [32, 64, 4096], P(None, 'region', 'tile'), may hold values from 0.3 to 1.5
- observed: float32 [3, 4096], P(None, ('region', 'tile')), may hold values from -6 to 6
- station_weight: float32 [4096], P(('region', 'tile')), may hold values from 0.2 to 2
- depth_profile: float32 [3, 32], replicated, may hold values from 0.1 to 1
- station_cell: int32 [4096], P(('region', 'tile')), may hold values from 0 to 2047
- station_count: int32 [128], P(('region', 'tile')), may hold values from 1 to 32, as said below
- influence: int32 [128, 64], P(('region', 'tile')), may hold values from 0 to 4095, as said below
- influence_count: int32 [128], P(('region', 'tile')), may hold values from 1 to 64, as said below
Outputs:
- analysis: float32 [9, 32, 64, 4096], P(None, None, 'region', 'tile')
Inputs may be any that keep to these rules, and one draw needn't show every extreme that they name: Slots k < station_count[g] of tile g are live; the others are empty and ignored. `influence`: row g holds 64 distinct slot numbers; the tile s // 32 of each lies at a region index and a tile index that each differ from those of tile g by at most one, without wrapping. Only the first influence_count[g] entries of row g of influence are used.
All inputs are finite; a program needn't handle non-finite values.
Results may differ from a plain program's by a relative error of at most 0.0003.
Values sent between devices are 32-bit elements; how exact they have to be, the bound alone decides.
No kernel may reach another device: no remote copies, remote signals or barrier semaphores. Data moves between devices by JAX's collectives and lax.ppermute only.
A program may use at most 128 MiB of HBM per device.

v0:
```python
import jax
import jax.numpy as jnp
from jax import lax
from jax.sharding import PartitionSpec as P

ITERS = 4


near_coef = 1.125
far_coef = -1.0 / 24.0
time_step = 0.15


def extended(block, sides, width):
    for axis, dim in sides:
        count = lax.axis_size(axis)
        forward = [(i, i + 1) for i in range(count - 1)]
        backward = [(target, source) for source, target in forward]
        low = lax.ppermute(
            lax.slice_in_dim(block, block.shape[dim] - width, None, axis=dim), axis, forward
        )
        high = lax.ppermute(lax.slice_in_dim(block, 0, width, axis=dim), axis, backward)
        block = jnp.concatenate([low, block, high], axis=dim)
    return block


def shifted(field, along, offset, length):
    return lax.slice_in_dim(field, offset, offset + length, axis=along)


def differ(field, along, forward):
    for other_axis in range(3):
        if other_axis != along:
            field = shifted(field, other_axis, 2, field.shape[other_axis] - 4)
    length = field.shape[along] - 4
    if forward:
        near_term = shifted(field, along, 3, length) - shifted(field, along, 2, length)
        far_term = shifted(field, along, 4, length) - shifted(field, along, 1, length)
    else:
        near_term = shifted(field, along, 2, length) - shifted(field, along, 1, length)
        far_term = shifted(field, along, 3, length) - shifted(field, along, 0, length)
    return near_coef * near_term + far_coef * far_term


def move_velocity(velocity, stress, buoyancy):
    force_x = differ(stress[0], 1, True) + differ(stress[3], 2, False) + differ(stress[4], 0, False)
    force_y = differ(stress[3], 1, False) + differ(stress[1], 2, True) + differ(stress[5], 0, False)
    force_z = differ(stress[4], 1, False) + differ(stress[5], 2, False) + differ(stress[2], 0, True)
    factor = time_step * buoyancy
    return velocity + factor[None] * jnp.stack([force_x, force_y, force_z])


def move_stress(stress, velocity, lame_first, shear_modulus):
    grad_x = differ(velocity[0], 1, False)
    grad_y = differ(velocity[1], 2, False)
    grad_z = differ(velocity[2], 0, False)
    modulus = lame_first + 2.0 * shear_modulus
    rates = jnp.stack(
        [
            modulus * grad_x + lame_first * (grad_y + grad_z),
            modulus * grad_y + lame_first * (grad_x + grad_z),
            modulus * grad_z + lame_first * (grad_x + grad_y),
            shear_modulus * (differ(velocity[0], 2, True) + differ(velocity[1], 1, True)),
            shear_modulus * (differ(velocity[0], 0, True) + differ(velocity[2], 1, True)),
            shear_modulus * (differ(velocity[1], 0, True) + differ(velocity[2], 2, True)),
        ]
    )
    return stress + time_step * rates


def pad_depth(field):
    return jnp.pad(field, ((0, 0), (2, 2), (0, 0), (0, 0)))


def per_device(
    fields,
    buoyancy,
    lame_first,
    shear_modulus,
    observed,
    station_weight,
    depth_profile,
    station_cell,
    station_count,
    influence,
    influence_count,
):
    velocity = fields[:3]
    stress = fields[3:]
    for iteration in range(ITERS):
        stress_wide = extended(stress, (("region", 2), ("tile", 3)), 2)
        velocity = move_velocity(velocity, pad_depth(stress_wide), buoyancy)
        velocity_wide = extended(velocity, (("region", 2), ("tile", 3)), 2)
        stress = move_stress(stress, pad_depth(velocity_wide), lame_first, shear_modulus)
    span_x = velocity.shape[2]
    span_y = velocity.shape[3]
    slot_total = station_cell.shape[0]
    list_length = influence.shape[1]
    region_index = lax.axis_index("region")
    tile_index = lax.axis_index("tile")
    live_slot = jnp.arange(slot_total, dtype=jnp.int32) < station_count[0]
    surface = velocity[:, 0].reshape(3, span_x * span_y)
    sample = jnp.take(surface, station_cell, axis=1)
    weight = jnp.where(live_slot[None], station_weight[None] * (observed - sample), 0.0)
    station_x = (region_index * span_x + station_cell // span_y).astype(jnp.float32)
    station_y = (tile_index * span_y + station_cell % span_y).astype(jnp.float32)
    packet = jnp.concatenate([weight, station_x[None], station_y[None]], axis=0)
    listed = influence[0]
    owner_tile = listed // slot_total
    slot_place = listed % slot_total
    gathered = lax.all_gather(packet[None], ("region", "tile"), axis=0, tiled=True)
    picked = gathered[owner_tile, :, slot_place]
    used_entry = jnp.arange(list_length, dtype=jnp.int32) < influence_count[0]
    width_x = 2.0 * (0.5 * span_x) ** 2
    width_y = 2.0 * (0.25 * span_y) ** 2
    cell_x = (region_index * span_x + jnp.arange(span_x, dtype=jnp.int32)).astype(jnp.float32)
    cell_y = (tile_index * span_y + jnp.arange(span_y, dtype=jnp.int32)).astype(jnp.float32)
    dist_x = cell_x[:, None] - picked[:, 3][None]
    dist_y = cell_y[:, None] - picked[:, 4][None]
    along_x = jnp.exp(-(dist_x * dist_x) / width_x)
    along_y = jnp.exp(-(dist_y * dist_y) / width_y)
    scaled = jnp.where(used_entry[None, None], picked[:, :3].T[:, None, :] * along_x[None], 0.0)
    increment = jnp.einsum("cxl,yl->cxy", scaled, along_y, precision=lax.Precision.HIGHEST)
    velocity = velocity + depth_profile[:, :, None, None] * increment[:, None]
    return jnp.concatenate([velocity, stress], axis=0)


def solution(mesh):
    in_specs = (
        P(None, None, "region", "tile"),
        P(None, "region", "tile"),
        P(None, "region", "tile"),
        P(None, "region", "tile"),
        P(None, ("region", "tile")),
        P(("region", "tile")),
        P(),
        P(("region", "tile")),
        P(("region", "tile")),
        P(("region", "tile"), None),
        P(("region", "tile")),
    )
    out_specs = P(None, None, "region", "tile")
    return jax.shard_map(
        per_device, mesh=mesh, in_specs=in_specs, out_specs=out_specs, check_vma=False
    )
```

profile of v0, /device:TPU:8, one launch (start us, length us, event | category | flops | bytes accessed | tf_op | source)
XLA Modules:
  0.0 657.8 jit_solution(5435431754785393210)
XLA Ops:
  6.3 2.4 collective-permute-done.1
  9.3 2.9 fusion.372
  12.2 2.5 copy.444
  14.7 4.6 collective-permute-start.2
  19.3 2.5 copy.445
  23.7 2.3 copy.446
  26.0 3.4 collective-permute-done.3
  29.4 2.3 copy.447
  31.7 5.1 pad_maximum_fusion
  41.5 6.1 collective-permute-start.4
  54.7 3.0 collective-permute-start.6
  59.4 3.1 collective-permute-start.7
  63.9 2.6 collective-permute-done.7
  68.1 3.0 pad_maximum_fusion.5
  76.2 5.0 collective-permute-start.8
  86.0 2.9 fusion.371
  88.9 2.5 copy.456
  91.4 4.5 collective-permute-start.10
  95.9 3.1 copy.457
  99.0 2.2 collective-permute-start.11
  101.2 3.2 copy.458
  104.4 2.6 collective-permute-done.11
  107.0 3.2 copy.459
  110.2 5.2 pad_maximum_fusion.1
  120.1 6.1 collective-permute-start.12
  131.6 2.4 copy.460
  134.0 2.9 collective-permute-start.14
  136.9 2.3 copy.461
  139.2 4.0 collective-permute-start.15
  143.3 2.3 copy.462
  146.5 2.3 copy.463
  148.9 3.1 pad_maximum_fusion.7
  155.6 5.2 collective-permute-start.16
  167.8 2.5 copy.468
  170.3 4.3 collective-permute-start.18
  176.1 2.3 collective-permute-start.19
  178.5 3.3 copy.470
  181.7 2.9 collective-permute-done.19
  184.6 2.3 copy.471
  186.9 5.2 pad_maximum_fusion.2
  197.4 5.4 collective-permute-start.20
  209.9 3.4 collective-permute-start.22
  215.0 2.6 collective-permute-start.23
  219.8 2.5 collective-permute-done.23
  223.8 3.0 pad_maximum_fusion.9
  230.6 4.9 collective-permute-start.24
  240.5 2.9 fusion.369
  243.4 3.3 copy.480
  246.7 4.5 collective-permute-start.26
  251.2 3.2 copy.481
  254.4 2.2 collective-permute-start.27
  257.3 3.2 copy.482
  260.5 3.1 collective-permute-done.27
  263.5 3.2 copy.483
  266.8 5.3 pad_maximum_fusion.3
  281.6 332.3 %all-gather.1 = f32[128,5,32]{2,1,0:T(8,128)} all-gather(f32[1,5,32]{2,1,0:T(8,128)S(1)} %maximum_bitcast_fusion), channel_id=2, replica_groups=mesh['region'=4,'tile'=32] {'region','tile'}, dimensions={0}, use_global_device_ids=true | all-gather | bytes 82560 | tf_op jit(solution)/shard_map/all_gather | solution.py:111
  613.8 3.2 copy.487
  629.2 2.3 copy.489
  633.4 2.3 copy.490
  635.7 4.8 collective-permute-start.31
  640.5 2.9 multiply_add_fusion.4
  643.5 2.4 copy.491
  645.9 2.3 copy.492
  648.2 3.0 pad_maximum_fusion.11
  (262 shorter events, 112.6 us)
Async XLA Ops:
  1.6 4.6 collective-permute-start
  3.3 5.4 collective-permute-start.1
  12.2 11.5 %copy-start.42 = (f32[32,16,128]{2,1,0:T(8,128)S(1)}, f32[32,16,128]{2,1,0:T(8,128)}, u32[]{:S(2)}) copy-start(f32[32,16,128]{2,1,0:T(8,128)} %param.12) | copy-start | bytes 786436
  14.7 9.0 %collective-permute-start.2 = (f32[6,32,20,2]{1,3,2,0:T(2,128)S(1)}, f32[6,32,20,2]{1,3,2,0:T(2,128)S(1)}, u32[]{:S(2)}, u32[]{:S(2)}) collective-permute-start(f32[6,32,20,2]{1,3,2,0:T(2,128)S(1)} %copy.444), channel_id=1, source_target_pairs={{0,1},{1,2},{2,3},{3,4},{4,5},{5,6},{6,7},{7,8},{8,9},{9,10},{10,1... | collective-permute-start | bytes 92168 | tf_op jit(solution)/shard_map/ppermute | solution.py:19
  21.7 7.7 %collective-permute-start.3 = (f32[6,32,20,2]{1,3,2,0:T(2,128)S(1)}, f32[6,32,20,2]{1,3,2,0:T(2,128)S(1)}, u32[]{:S(2)}, u32[]{:S(2)}) collective-permute-start(f32[6,32,20,2]{1,3,2,0:T(2,128)S(1)} %copy.445), channel_id=1, source_target_pairs={{1,0},{2,1},{3,2},{4,3},{5,4},{6,5},{7,6},{8,7},{9,8},{10,9},{11,1... | collective-permute-start | bytes 92168 | tf_op jit(solution)/shard_map/ppermute | solution.py:22
  39.2 79.4 %copy-start.6 = (f32[1,32,16,128]{3,2,1,0:T(8,128)}, f32[1,32,16,128]{3,2,1,0:T(8,128)S(1)}, u32[]{:S(2)}) copy-start(f32[1,32,16,128]{3,2,1,0:T(8,128)S(1)} %fusion.307) | copy-start | bytes 786436
  40.1 78.6 %copy-start.8 = (f32[1,32,16,128]{3,2,1,0:T(8,128)}, f32[1,32,16,128]{3,2,1,0:T(8,128)S(1)}, u32[]{:S(2)}) copy-start(f32[1,32,16,128]{3,2,1,0:T(8,128)S(1)} %fusion.295) | copy-start | bytes 786436
  41.5 7.4 %collective-permute-start.4 = (f32[3,32,2,128]{3,2,1,0:T(2,128)S(1)}, f32[3,32,2,128]{3,2,1,0:T(2,128)S(1)}, u32[]{:S(2)}, u32[]{:S(2)}) collective-permute-start(f32[3,32,2,128]{3,2,1,0:T(2,128)S(1)} %get-tuple-element.109), channel_id=1, source_target_pairs={{0,32},{32,64},{64,96},{1,33},{33,65},{65,97},{2,34},{34,66},{66,9... | collective-permute-start | bytes 294920 | tf_op jit(solution)/shard_map/ppermute | solution.py:19
  47.6 3.4 collective-permute-start.5
  54.7 7.8 %collective-permute-start.6 = (f32[3,32,20,2]{1,3,2,0:T(2,128)S(1)}, f32[3,32,20,2]{1,3,2,0:T(2,128)S(1)}, u32[]{:S(2)}, u32[]{:S(2)}) collective-permute-start(f32[3,32,20,2]{1,3,2,0:T(2,128)S(1)} %copy.448), channel_id=1, source_target_pairs={{0,1},{1,2},{2,3},{3,4},{4,5},{5,6},{6,7},{7,8},{8,9},{9,10},{10,1... | collective-permute-start | bytes 46088 | tf_op jit(solution)/shard_map/ppermute | solution.py:19
  59.4 7.2 %collective-permute-start.7 = (f32[3,32,20,2]{1,3,2,0:T(2,128)S(1)}, f32[3,32,20,2]{1,3,2,0:T(2,128)S(1)}, u32[]{:S(2)}, u32[]{:S(2)}) collective-permute-start(f32[3,32,20,2]{1,3,2,0:T(2,128)S(1)} %copy.449), channel_id=1, source_target_pairs={{1,0},{2,1},{3,2},{4,3},{5,4},{6,5},{7,6},{8,7},{9,8},{10,9},{11,1... | collective-permute-start | bytes 46088 | tf_op jit(solution)/shard_map/ppermute | solution.py:22
  74.0 1.7 copy-start.5
  76.2 6.4 collective-permute-start.8
  81.3 3.6 collective-permute-start.9
  91.4 9.8 %collective-permute-start.10 = (f32[6,32,20,2]{1,3,2,0:T(2,128)S(1)}, f32[6,32,20,2]{1,3,2,0:T(2,128)}, u32[]{:S(2)}, u32[]{:S(2)}) collective-permute-start(f32[6,32,20,2]{1,3,2,0:T(2,128)S(1)} %copy.456), channel_id=1, source_target_pairs={{0,1},{1,2},{2,3},{3,4},{4,5},{5,6},{6,7},{7,8},{8,9},{9,10},{10,1... | collective-permute-start | bytes 92168 | tf_op jit(solution)/shard_map/ppermute | solution.py:19
  99.0 8.0 %collective-permute-start.11 = (f32[6,32,20,2]{1,3,2,0:T(2,128)}, f32[6,32,20,2]{1,3,2,0:T(2,128)}, u32[]{:S(2)}, u32[]{:S(2)}) collective-permute-start(f32[6,32,20,2]{1,3,2,0:T(2,128)} %copy.457), channel_id=1, source_target_pairs={{1,0},{2,1},{3,2},{4,3},{5,4},{6,5},{7,6},{8,7},{9,8},{10,9},{11,1... | collective-permute-start | bytes 92168 | tf_op jit(solution)/shard_map/ppermute | solution.py:22
  116.9 1.7 copy-start.14
  117.8 2.3 copy-start.16
  118.6 11.2 %copy-start.19 = (f32[1,32,16,128]{3,2,1,0:T(8,128)}, f32[1,32,16,128]{3,2,1,0:T(8,128)S(1)}, u32[]{:S(2)}) copy-start(f32[1,32,16,128]{3,2,1,0:T(8,128)S(1)} %fusion.220) | copy-start | bytes 786436
  120.1 9.6 %copy-start.12 = (f32[3,32,16,128]{3,2,1,0:T(8,128)}, f32[3,32,16,128]{3,2,1,0:T(8,128)S(1)}, u32[]{:S(2)}) copy-start(f32[3,32,16,128]{3,2,1,0:T(8,128)S(1)} %fusion.25) | copy-start | bytes 2359300
  120.1 8.1 %collective-permute-start.12 = (f32[3,32,2,128]{3,2,1,0:T(2,128)S(1)}, f32[3,32,2,128]{3,2,1,0:T(2,128)S(1)}, u32[]{:S(2)}, u32[]{:S(2)}) collective-permute-start(f32[3,32,2,128]{3,2,1,0:T(2,128)S(1)} %get-tuple-element.107), channel_id=1, source_target_pairs={{0,32},{32,64},{64,96},{1,33},{33,65},{65,97},{2,34},{34,66},{66,9... | collective-permute-start | bytes 294920 | tf_op jit(solution)/shard_map/ppermute | solution.py:19
  126.3 3.4 collective-permute-start.13
  129.7 2.0 copy-start.41
  131.6 11.6 %copy-start.45 = (s32[32]{0:T(128)S(1)}, s32[32]{0:T(128)}, u32[]{:S(2)}) copy-start(s32[32]{0:T(128)} %param.18) | copy-start | bytes 388
  131.6 17.2 %copy-start.13 = (f32[3,32,16,128]{3,2,1,0:T(8,128)S(1)}, f32[3,32,16,128]{3,2,1,0:T(8,128)}, u32[]{:S(2)}) copy-start(f32[3,32,16,128]{3,2,1,0:T(8,128)} %copy-done.12) | copy-start | bytes 2359300
  134.0 9.3 %collective-permute-start.14 = (f32[3,32,20,2]{1,3,2,0:T(2,128)}, f32[3,32,20,2]{1,3,2,0:T(2,128)}, u32[]{:S(2)}, u32[]{:S(2)}) collective-permute-start(f32[3,32,20,2]{1,3,2,0:T(2,128)} %copy.460), channel_id=1, source_target_pairs={{0,1},{1,2},{2,3},{3,4},{4,5},{5,6},{6,7},{7,8},{8,9},{9,10},{10,1... | collective-permute-start | bytes 46088 | tf_op jit(solution)/shard_map/ppermute | solution.py:19
  139.2 7.3 %collective-permute-start.15 = (f32[3,32,20,2]{1,3,2,0:T(2,128)}, f32[3,32,20,2]{1,3,2,0:T(2,128)}, u32[]{:S(2)}, u32[]{:S(2)}) collective-permute-start(f32[3,32,20,2]{1,3,2,0:T(2,128)} %copy.461), channel_id=1, source_target_pairs={{1,0},{2,1},{3,2},{4,3},{5,4},{6,5},{7,6},{8,7},{9,8},{10,9},{11,1... | collective-permute-start | bytes 46088 | tf_op jit(solution)/shard_map/ppermute | solution.py:22
  155.4 9.2 %copy-start.2 = (f32[6,32,16,128]{3,2,1,0:T(8,128)}, f32[6,32,16,128]{3,2,1,0:T(8,128)S(1)}, u32[]{:S(2)}) copy-start(f32[6,32,16,128]{3,2,1,0:T(8,128)S(1)} %multiply_add_fusion.2) | copy-start | bytes 4718596
  155.6 6.6 %collective-permute-start.16 = (f32[6,32,2,128]{3,1,2,0:T(8,128)S(1)}, f32[6,32,2,128]{3,1,2,0:T(8,128)S(1)}, u32[]{:S(2)}, u32[]{:S(2)}) collective-permute-start(f32[6,32,2,128]{3,1,2,0:T(8,128)S(1)} %copy.464), channel_id=1, source_target_pairs={{0,32},{32,64},{64,96},{1,33},{33,65},{65,97},{2,34},{34,66},{66,9... | collective-permute-start | bytes 589832 | tf_op jit(solution)/shard_map/ppermute | solution.py:19
  160.9 3.6 collective-permute-start.17
  162.4 2.2 copy-start.33
  170.3 8.1 %collective-permute-start.18 = (f32[6,32,20,2]{1,3,2,0:T(2,128)S(1)}, f32[6,32,20,2]{1,3,2,0:T(2,128)}, u32[]{:S(2)}, u32[]{:S(2)}) collective-permute-start(f32[6,32,20,2]{1,3,2,0:T(2,128)S(1)} %copy.468), channel_id=1, source_target_pairs={{0,1},{1,2},{2,3},{3,4},{4,5},{5,6},{6,7},{7,8},{8,9},{9,10},{10,1... | collective-permute-start | bytes 92168 | tf_op jit(solution)/shard_map/ppermute | solution.py:19
  176.1 8.6 %collective-permute-start.19 = (f32[6,32,20,2]{1,3,2,0:T(2,128)}, f32[6,32,20,2]{1,3,2,0:T(2,128)S(1)}, u32[]{:S(2)}, u32[]{:S(2)}) collective-permute-start(f32[6,32,20,2]{1,3,2,0:T(2,128)} %copy.469), channel_id=1, source_target_pairs={{1,0},{2,1},{3,2},{4,3},{5,4},{6,5},{7,6},{8,7},{9,8},{10,9},{11,1... | collective-permute-start | bytes 92168 | tf_op jit(solution)/shard_map/ppermute | solution.py:22
  178.4 8.5 %copy-start.3 = (f32[6,32,16,128]{3,2,1,0:T(8,128)S(1)}, f32[6,32,16,128]{3,2,1,0:T(8,128)}, u32[]{:S(2)}) copy-start(f32[6,32,16,128]{3,2,1,0:T(8,128)} %copy-done.2) | copy-start | bytes 4718596
  178.4 8.5 %copy-start.34 = (f32[6,32,2,128]{3,2,1,0:T(2,128)S(1)}, f32[6,32,2,128]{3,2,1,0:T(2,128)}, u32[]{:S(2)}) copy-start(f32[6,32,2,128]{3,2,1,0:T(2,128)} %copy-done.33) | copy-start | bytes 589828
  178.4 8.5 %copy-start.37 = (f32[6,32,2,128]{3,2,1,0:T(2,128)S(1)}, f32[6,32,2,128]{3,2,1,0:T(2,128)}, u32[]{:S(2)}) copy-start(f32[6,32,2,128]{3,2,1,0:T(2,128)} %copy-done.36) | copy-start | bytes 589828
  193.6 1.8 copy-start.22
  194.5 2.8 copy-start.24
  194.5 1.3 copy-start.20
  195.9 10.5 %copy-start.26 = (f32[1,32,16,128]{3,2,1,0:T(8,128)}, f32[1,32,16,128]{3,2,1,0:T(8,128)S(1)}, u32[]{:S(2)}) copy-start(f32[1,32,16,128]{3,2,1,0:T(8,128)S(1)} %fusion.145) | copy-start | bytes 786436
  197.4 6.7 %collective-permute-start.20 = (f32[3,32,2,128]{3,2,1,0:T(2,128)S(1)}, f32[3,32,2,128]{3,2,1,0:T(2,128)S(1)}, u32[]{:S(2)}, u32[]{:S(2)}) collective-permute-start(f32[3,32,2,128]{3,2,1,0:T(2,128)S(1)} %get-tuple-element.105), channel_id=1, source_target_pairs={{0,32},{32,64},{64,96},{1,33},{33,65},{65,97},{2,34},{34,66},{66,9... | collective-permute-start | bytes 294920 | tf_op jit(solution)/shard_map/ppermute | solution.py:19
  202.8 3.4 collective-permute-start.21
  209.9 8.4 %collective-permute-start.22 = (f32[3,32,20,2]{1,3,2,0:T(2,128)S(1)}, f32[3,32,20,2]{1,3,2,0:T(2,128)S(1)}, u32[]{:S(2)}, u32[]{:S(2)}) collective-permute-start(f32[3,32,20,2]{1,3,2,0:T(2,128)S(1)} %copy.472), channel_id=1, source_target_pairs={{0,1},{1,2},{2,3},{3,4},{4,5},{5,6},{6,7},{7,8},{8,9},{9,10},{10,1... | collective-permute-start | bytes 46088 | tf_op jit(solution)/shard_map/ppermute | solution.py:19
  215.0 7.3 %collective-permute-start.23 = (f32[3,32,20,2]{1,3,2,0:T(2,128)S(1)}, f32[3,32,20,2]{1,3,2,0:T(2,128)S(1)}, u32[]{:S(2)}, u32[]{:S(2)}) collective-permute-start(f32[3,32,20,2]{1,3,2,0:T(2,128)S(1)} %copy.473), channel_id=1, source_target_pairs={{1,0},{2,1},{3,2},{4,3},{5,4},{6,5},{7,6},{8,7},{9,8},{10,9},{11,1... | collective-permute-start | bytes 46088 | tf_op jit(solution)/shard_map/ppermute | solution.py:22
  228.8 1.4 copy-start.4
  230.2 6.6 %copy-start.47 = (s32[1,64]{1,0:T(1,128)S(1)}, s32[1,64]{1,0:T(1,128)}, u32[]{:S(2)}) copy-start(s32[1,64]{1,0:T(1,128)} %param.20) | copy-start | bytes 772
  230.6 6.3 collective-permute-start.24
  235.6 3.7 collective-permute-start.25
  237.1 2.3 copy-start.32
  243.4 13.8 %copy-start.44 = (f32[3,32]{1,0:T(4,128)S(1)}, f32[3,32]{1,0:T(4,128)}, u32[]{:S(2)}) copy-start(f32[3,32]{1,0:T(4,128)} %param.15) | copy-start | bytes 1156
  246.7 10.6 %collective-permute-start.26 = (f32[6,32,20,2]{1,2,3,0:T(8,128)}, f32[6,32,20,2]{1,2,3,0:T(8,128)}, u32[]{:S(2)}, u32[]{:S(2)}) collective-permute-start(f32[6,32,20,2]{1,2,3,0:T(8,128)} %copy.480), channel_id=1, source_target_pairs={{0,1},{1,2},{2,3},{3,4},{4,5},{5,6},{6,7},{7,8},{8,9},{9,10},{10,1... | collective-permute-start | bytes 92168 | tf_op jit(solution)/shard_map/ppermute | solution.py:19
  254.4 9.1 %collective-permute-start.27 = (f32[6,32,20,2]{1,2,3,0:T(8,128)}, f32[6,32,20,2]{1,2,3,0:T(8,128)}, u32[]{:S(2)}, u32[]{:S(2)}) collective-permute-start(f32[6,32,20,2]{1,2,3,0:T(8,128)} %copy.481), channel_id=1, source_target_pairs={{1,0},{2,1},{3,2},{4,3},{5,4},{6,5},{7,6},{8,7},{9,8},{10,9},{11,1... | collective-permute-start | bytes 92168 | tf_op jit(solution)/shard_map/ppermute | solution.py:22
  273.5 1.8 copy-start.29
  274.4 2.9 copy-start.30
  274.5 1.3 copy-start.27
  275.8 1.5 copy-start.31
  275.8 5.6 copy-start.46
  620.7 3.6 collective-permute-start.28
  622.0 3.4 collective-permute-start.29
  629.2 11.4 %copy-start.43 = (f32[3,32]{1,0:T(4,128)S(1)}, f32[3,32]{1,0:T(4,128)}, u32[]{:S(2)}) copy-start(f32[3,32]{1,0:T(4,128)} %param.17) | copy-start | bytes 1156
  631.5 12.0 %collective-permute-start.30 = (f32[3,32,20,2]{1,3,2,0:T(2,128)}, f32[3,32,20,2]{1,3,2,0:T(2,128)}, u32[]{:S(2)}, u32[]{:S(2)}) collective-permute-start(f32[3,32,20,2]{1,3,2,0:T(2,128)} %copy.489), channel_id=1, source_target_pairs={{0,1},{1,2},{2,3},{3,4},{4,5},{5,6},{6,7},{7,8},{8,9},{9,10},{10,1... | collective-permute-start | bytes 46088 | tf_op jit(solution)/shard_map/ppermute | solution.py:19
  635.7 10.2 %collective-permute-start.31 = (f32[3,32,20,2]{1,3,2,0:T(2,128)}, f32[3,32,20,2]{1,3,2,0:T(2,128)}, u32[]{:S(2)}, u32[]{:S(2)}) collective-permute-start(f32[3,32,20,2]{1,3,2,0:T(2,128)} %copy.490), channel_id=1, source_target_pairs={{1,0},{2,1},{3,2},{4,3},{5,4},{6,5},{7,6},{8,7},{9,8},{10,9},{11,1... | collective-permute-start | bytes 46088 | tf_op jit(solution)/shard_map/ppermute | solution.py:22
  643.5 4.7 copy-start.11
  643.5 4.7 copy-start.40
  (16 other events, 15.8 us)
where the time goes:
time: 668 us; the launch traced here: 658 us
  blocking collectives  332 us (50%)
  local copies, waits for them, and re-layouts  120 us (18%)
  starting transfers between devices  98.5 us (15%)
  other arithmetic  69.8 us (10%)
  waiting for transfers between devices  33.5 us (5%)
    all_gather x1, blocking collectives, per_device(): lax.all_gather(packet[None], ('region', 'tile'), axis=0, tiled=True)  332 us
    ppermute x16, starting transfers between devices, extended(): lax.ppermute(lax.slice_in_dim(block, block.shape[dim] - width, None, axis...  65 us
    slice x27, local copies, waits for them, and re-layouts, extended(): lax.slice_in_dim(block, block.shape[dim] - width, None, axis=dim)  40.8 us
    concatenate x16, other arithmetic, extended(): block = jnp.concatenate([low, block, high], axis=dim)  36.2 us
    ppermute x16, starting transfers between devices, extended(): lax.ppermute(lax.slice_in_dim(block, 0, width, axis=dim), axis, backward)  33.5 us
    ppermute x16, waiting for transfers between devices, extended(): lax.ppermute(lax.slice_in_dim(block, 0, width, axis=dim), axis, backward)  33.4 us
    ppermute x12, local copies, waits for them, and re-layouts, extended(): lax.ppermute(lax.slice_in_dim(block, block.shape[dim] - width, None, axis...  20.3 us
    ppermute x12, local copies, waits for them, and re-layouts, extended(): lax.ppermute(lax.slice_in_dim(block, 0, width, axis=dim), axis, backward)  19.2 us
  transfers between devices with their start and end apart: 32, of which 15 were waited for; matrix products, arithmetic and copies ran while one was open for 7% of the time, Pallas kernels for 0%

commit v1 on v0

v1 whole, which is shorter than its diff:
```python
import jax
import jax.numpy as jnp
from jax import lax
from jax.experimental import pallas as pl
from jax.experimental.pallas import tpu as pltpu
from jax.sharding import PartitionSpec as P

ITERS = 4
NEAR = 1.125
FAR = -1.0 / 24.0
DT = 0.15

CX, CY, NZ = 16, 128, 32
S, LIST = 32, 64
GROUPS = 4
WIDE = 16
PACK = NZ // GROUPS
DEPTH = NZ + PACK
LOW = 4
PLANES = LOW + CX + 4
ZROWS = 72

VX, VY, VZ, SXX, SYY, SZZ, SXY, SXZ, SYZ = range(9)
BELOW = [(f, r) for f in (SXX, SXY, SXZ) for r in (-3, -2, -1)] + [
    (SYY, -1), (SYZ, -1), (SZZ, -1), (VX, -2), (VX, -1), (VY, -1), (VZ, -1)]
ABOVE = [(f, r) for f in (SXX, SXY, SXZ) for r in (16, 17, 18)] + [
    (f, r) for f in (SYY, SYZ, SZZ) for r in (16, 17)] + [
    (VX, 16), (VY, 16), (VY, 17), (VZ, 16), (VZ, 17)]
BUOY_ROWS = 2

VMEM_BYTES = 40 * 1024 * 1024


def lanes(rows):
    return lax.broadcasted_iota(jnp.int32, (rows, 128), 1)


def edge_pack(main):
    lane = lanes(PACK)
    out = pltpu.roll(main[0:8], WIDE, 1)
    for g in range(1, GROUPS):
        rolled = pltpu.roll(main[8 * g:8 * g + 8], (WIDE + 32 * g) % 128, 1)
        out = jnp.where(lane >= 32 * g, rolled, out)
    return out


def y_shifts(a, offsets):
    main, halo = a[:NZ], a[NZ:]
    near = [pltpu.roll(halo, (128 - WIDE - 32 * g) % 128, 1) for g in range(GROUPS)]
    other = jnp.concatenate(near + [edge_pack(main)], axis=0)
    lane = lanes(DEPTH)
    is_main = lax.broadcasted_iota(jnp.int32, (DEPTH, 128), 0) < NZ
    spot = jnp.where(is_main, lane, (lane + WIDE) % 32)
    last = jnp.where(is_main, 128, 32)
    out = []
    for o in offsets:
        if o > 0:
            mixed = jnp.where(spot < o, other, a)
        else:
            mixed = jnp.where(spot >= last + o, other, a)
        out.append(pltpu.roll(mixed, (-o) % 128, 1))
    return out


def combine(m1, c0, p1, p2):
    return NEAR * (p1 - c0) + FAR * (p2 - m1)


def load(ref, f, x, dz=0):
    return jnp.concatenate(
        [ref[f, x, 8 + dz:8 + NZ + dz, :], ref[f, x, 56 + dz:64 + dz, :]], axis=0)


def store(ref, f, x, value, z_pads):
    ref[f, x, 8:8 + NZ, :] = value[:NZ]
    halo = value[NZ:]
    ref[f, x, 56:64, :] = halo
    if z_pads:
        lane = lanes(PACK)
        ref[f, x, 48:56, :] = jnp.where(lane < 32, 0.0, pltpu.roll(halo, 32, 1))
        ref[f, x, 64:72, :] = jnp.where(lane >= 96, 0.0, pltpu.roll(halo, 96, 1))


def diff_x(ref, f, x, forward):
    first = -1 if forward else -2
    return combine(*[load(ref, f, x + first + k) for k in range(4)])


def diff_z(ref, f, x, forward):
    first = -1 if forward else -2
    return combine(*[load(ref, f, x, first + k) for k in range(4)])


def diff_y(ref, f, x, forward):
    here = load(ref, f, x)
    if forward:
        m1, p1, p2 = y_shifts(here, (-1, 1, 2))
        return combine(m1, here, p1, p2)
    m2, m1, p1 = y_shifts(here, (-2, -1, 1))
    return combine(m2, m1, here, p1)


Z_PADDED = (VX, VY, VZ, SZZ, SXZ, SYZ)


def fill(x_ref, main_ref, halo_ref, below_ref, above_ref):
    zero = jnp.zeros((8, 128), jnp.float32)

    def zero_pads(x, _):
        for f in Z_PADDED:
            x_ref[f, x, 0:8, :] = zero
            x_ref[f, x, 40:48, :] = zero
        return 0

    lax.fori_loop(0, PLANES, zero_pads, 0)

    def copy_in(x, _):
        for f in range(9):
            value = jnp.concatenate([main_ref[f, x], halo_ref[f, x]], axis=0)
            store(x_ref, f, x + LOW, value, f in Z_PADDED)
        return 0

    lax.fori_loop(0, CX, copy_in, 0)
    for n, (f, r) in enumerate(BELOW):
        store(x_ref, f, r + LOW, below_ref[n], f in Z_PADDED)
    for n, (f, r) in enumerate(ABOVE):
        store(x_ref, f, r + LOW, above_ref[n], f in Z_PADDED)


def param(main_ref, halo_ref, f, x):
    return jnp.concatenate([main_ref[9 + f, x], halo_ref[9 + f, x]], axis=0)


def fill_buoyancy(b_ref, par_main, par_halo, below_first, above_first):
    def copy_in(x, _):
        b_ref[x + BUOY_ROWS] = DT * param(par_main, par_halo, 0, x)
        return 0

    lax.fori_loop(0, CX, copy_in, 0)
    for k in range(BUOY_ROWS):
        b_ref[k] = DT * below_first[len(BELOW) + k]
        b_ref[CX + BUOY_ROWS + k] = DT * above_first[len(ABOVE) + k]


def velocity_pass(x_ref, b_ref):
    def body(j, _):
        x = j - 2 + LOW
        force = (diff_x(x_ref, SXX, x, True) + diff_y(x_ref, SXY, x, False)
                 + diff_z(x_ref, SXZ, x, False))
        store(x_ref, VX, x, load(x_ref, VX, x) + b_ref[j] * force, True)
        x = x + 1
        b = b_ref[j + 1]
        force = (diff_x(x_ref, SXY, x, False) + diff_y(x_ref, SYY, x, True)
                 + diff_z(x_ref, SYZ, x, False))
        store(x_ref, VY, x, load(x_ref, VY, x) + b * force, True)
        force = (diff_x(x_ref, SXZ, x, False) + diff_y(x_ref, SYZ, x, False)
                 + diff_z(x_ref, SZZ, x, True))
        store(x_ref, VZ, x, load(x_ref, VZ, x) + b * force, True)
        return 0

    lax.fori_loop(0, CX + 3, body, 0)


def stress_rates(x_ref, x, lame, mu):
    grad_x = diff_x(x_ref, VX, x, False)
    grad_y = diff_y(x_ref, VY, x, False)
    grad_z = diff_z(x_ref, VZ, x, False)
    modulus = lame + 2.0 * mu
    return {
        SXX: modulus * grad_x + lame * (grad_y + grad_z),
        SYY: modulus * grad_y + lame * (grad_x + grad_z),
        SZZ: modulus * grad_z + lame * (grad_x + grad_y),
        SXY: mu * (diff_y(x_ref, VX, x, True) + diff_x(x_ref, VY, x, True)),
        SXZ: mu * (diff_z(x_ref, VX, x, True) + diff_x(x_ref, VZ, x, True)),
        SYZ: mu * (diff_z(x_ref, VY, x, True) + diff_y(x_ref, VZ, x, True)),
    }


def step_kernel(main_ref, halo_ref, par_main, par_halo, below_ref, above_ref, below_first,
                above_first, new_main, new_halo, send_down, send_up, x_ref, b_ref):
    fill(x_ref, main_ref, halo_ref, below_ref, above_ref)
    fill_buoyancy(b_ref, par_main, par_halo, below_first, above_first)
    velocity_pass(x_ref, b_ref)

    def body(r, _):
        x = r + LOW
        lame, mu = param(par_main, par_halo, 1, r), param(par_main, par_halo, 2, r)
        for f, rate in stress_rates(x_ref, x, lame, mu).items():
            value = load(x_ref, f, x) + DT * rate
            new_main[f, r] = value[:NZ]
            new_halo[f, r] = value[NZ:]
        for f in (VX, VY, VZ):
            value = load(x_ref, f, x)
            new_main[f, r] = value[:NZ]
            new_halo[f, r] = value[NZ:]
        return 0

    lax.fori_loop(0, CX, body, 0)
    write_sends(new_main, new_halo, send_down, send_up)


def write_sends(main_ref, halo_ref, send_down, send_up):
    for n, (f, r) in enumerate(ABOVE):
        send_down[n, 0:NZ] = main_ref[f, r - CX]
        send_down[n, NZ:DEPTH] = halo_ref[f, r - CX]
    for n, (f, r) in enumerate(BELOW):
        send_up[n, 0:NZ] = main_ref[f, r + CX]
        send_up[n, NZ:DEPTH] = halo_ref[f, r + CX]


def pack_kernel(fields_ref, buoy_ref, lame_ref, mu_ref, main_ref, right_ref, left_ref):
    lane = lanes(PACK)
    low = lane % 32 < WIDE

    def pair(read, a, p):
        edges = []
        for k in range(2):
            x = 2 * p + k
            value = read(x)
            main_ref[a, x] = value
            edges.append(edge_pack(value))
        right_ref[a, p] = jnp.where(low, edges[0], pltpu.roll(edges[1], WIDE, 1))
        left_ref[a, p] = jnp.where(low, pltpu.roll(edges[1], 128 - WIDE, 1), edges[0])

    def body(p, _):
        for a in range(9):
            pair(lambda x: fields_ref[pl.ds(a * NZ * CX + x, NZ, stride=CX), :], a, p)
        for a, ref in ((9, buoy_ref), (10, lame_ref), (11, mu_ref)):
            pair(lambda x: ref[pl.ds(x, NZ, stride=CX), :], a, p)
        return 0

    lax.fori_loop(0, CX // 2, body, 0)


def halo_kernel(main_ref, from_left, from_right, halo_ref, send_down, send_up):
    lane = lanes(PACK)
    low = lane % 32 < WIDE

    def body(p, _):
        for a in range(12):
            one, two = from_left[a, p], from_right[a, p]
            halo_ref[a, 2 * p] = jnp.where(low, one, two)
            halo_ref[a, 2 * p + 1] = jnp.where(
                low, pltpu.roll(one, 128 - WIDE, 1), pltpu.roll(two, WIDE, 1))
        return 0

    lax.fori_loop(0, CX // 2, body, 0)
    write_sends(main_ref, halo_ref, send_down, send_up)
    for k in range(BUOY_ROWS):
        for ref, n, r in ((send_down, len(ABOVE) + k, k), (send_up, len(BELOW) + k, CX - BUOY_ROWS + k)):
            ref[n, 0:NZ] = main_ref[9, r]
            ref[n, NZ:DEPTH] = halo_ref[9, r]


def last_velocity_kernel(place_ref, count_ref, main_ref, halo_ref, par_main, par_halo, below_ref,
                         above_ref, below_first, above_first, observed_ref, gain_ref, cell_ref,
                         v_ref, packet_ref, x_ref, b_ref, slot_ref):
    fill(x_ref, main_ref, halo_ref, below_ref, above_ref)
    fill_buoyancy(b_ref, par_main, par_halo, below_first, above_first)
    velocity_pass(x_ref, b_ref)

    def copy_out(x, _):
        v_ref[0, x] = x_ref[0, x]
        v_ref[1, x] = x_ref[1, x]
        v_ref[2, x] = x_ref[2, x]
        return 0

    lax.fori_loop(0, PLANES, copy_out, 0)
    slot_ref[...] = jnp.zeros((16, 128), jnp.float32)
    slot_ref[0:3, 0:S] = observed_ref[...]
    slot_ref[3:4, 0:S] = gain_ref[...]
    slot_ref[4:5, 0:S] = cell_ref[...].astype(jnp.float32)
    cell = slot_ref[4:5, :].astype(jnp.int32)
    cell_x, cell_y = cell // CY, cell % CY
    pick_y = (lax.broadcasted_iota(jnp.int32, (CY, 128), 0) == cell_y).astype(jnp.float32)
    pick_x = lax.broadcasted_iota(jnp.int32, (CX, 128), 0) == cell_x
    live = lanes(1) < count_ref[0]
    gain = slot_ref[3:4, :]
    region, tile = place_ref[0], place_ref[1]
    for c in range(3):
        surface = jnp.concatenate([x_ref[c, r + LOW, 8:9, :] for r in range(CX)], axis=0)
        rows = jnp.dot(surface, pick_y, precision=lax.Precision.HIGHEST,
                       preferred_element_type=jnp.float32)
        sample = jnp.sum(jnp.where(pick_x, rows, 0.0), axis=0, keepdims=True)
        slot_ref[8 + c:9 + c, :] = jnp.where(live, gain * (slot_ref[c:c + 1, :] - sample), 0.0)
    slot_ref[11:12, :] = (region * CX + cell_x).astype(jnp.float32)
    slot_ref[12:13, :] = (tile * CY + cell_y).astype(jnp.float32)
    own = jnp.where(lanes(8) < S, slot_ref[8:16, :], 0.0)
    packet_ref[...] = pltpu.roll(own, region * S, 1)


def last_kernel(place_ref, influence_ref, count_ref, profile_ref, main_ref, par_main, v_ref,
                before_ref, here_ref, after_ref, par_halo, out_ref, profile_rows):
    region, tile = place_ref[0], place_ref[1]
    lane = lanes(8)
    column = lax.broadcasted_iota(jnp.int32, (8, 128), 0) + tile - 1
    slot_id = (lane // S * 32 + column) * S + lane % S
    slot_id = jnp.where((column >= 0) & (column < 32), slot_id, -1)
    used = jnp.zeros((8, 128), jnp.int32)
    for k in range(LIST):
        hit = (slot_id == influence_ref[0, k]) & (k < count_ref[0])
        used = jnp.where(hit, 1, used)
    cell_x = (lax.broadcasted_iota(jnp.int32, (CX, 128), 0) + region * CX).astype(jnp.float32)
    cell_y = (lax.broadcasted_iota(jnp.int32, (CY, 128), 0) + tile * CY).astype(jnp.float32)
    increment = jnp.zeros((3 * CX, CY), jnp.float32)
    for d, ref in enumerate((before_ref, here_ref, after_ref)):
        packet = ref[0] + ref[1] + ref[2] + ref[3]
        dist_x = cell_x - packet[3:4]
        dist_y = cell_y - packet[4:5]
        along_x = jnp.exp(-(dist_x * dist_x) / (2.0 * (0.5 * CX) ** 2))
        along_y = jnp.exp(-(dist_y * dist_y) / (2.0 * (0.25 * CY) ** 2))
        keep = used[d:d + 1] > 0
        scaled = jnp.concatenate(
            [jnp.where(keep, packet[c:c + 1] * along_x, 0.0) for c in range(3)], axis=0)
        increment += lax.dot_general(
            scaled, along_y, (((1,), (1,)), ((), ())), precision=lax.Precision.HIGHEST,
            preferred_element_type=jnp.float32)
    for c in range(3):
        for z in range(NZ):
            profile_rows[c, z:z + 1, :] = jnp.full((1, 128), profile_ref[c, z], jnp.float32)
    for c in range(3):
        for r in range(CX):
            value = v_ref[c, r + LOW, 8:8 + NZ, :]
            value = value + profile_rows[c] * increment[c * CX + r:c * CX + r + 1, :]
            out_ref[pl.ds(c * NZ * CX + r, NZ, stride=CX), :] = value

    def body(r, _):
        lame, mu = param(par_main, par_halo, 1, r), param(par_main, par_halo, 2, r)
        for f, rate in stress_rates(v_ref, r + LOW, lame, mu).items():
            out_ref[pl.ds(f * NZ * CX + r, NZ, stride=CX), :] = main_ref[f, r] + DT * rate[:NZ]
        return 0

    lax.fori_loop(0, CX, body, 0)


def struct(*shape):
    return jax.ShapeDtypeStruct(shape, jnp.float32)


VM = pl.BlockSpec(memory_space=pltpu.VMEM)
SM = pl.BlockSpec(memory_space=pltpu.SMEM)


def call(kernel, out_shape, specs, scratch=()):
    many = isinstance(out_shape, (list, tuple))
    return pl.pallas_call(
        kernel, out_shape=out_shape, in_specs=specs,
        out_specs=[VM] * len(out_shape) if many else VM, scratch_shapes=list(scratch),
        compiler_params=pltpu.CompilerParams(vmem_limit_bytes=VMEM_BYTES))


def neighbours(up, down, axis):
    count = lax.axis_size(axis)
    forward = [(i, i + 1) for i in range(count - 1)]
    backward = [(b, a) for a, b in forward]
    return lax.ppermute(up, axis, forward), lax.ppermute(down, axis, backward)


def per_device(fields, buoyancy, lame_first, shear_modulus, observed, station_weight, depth_profile,
               station_cell, station_count, influence, influence_count):
    place = jnp.stack([lax.axis_index("region"), lax.axis_index("tile")]).astype(jnp.int32)
    main, right, left = call(
        pack_kernel,
        (struct(12, CX, NZ, 128), struct(12, CX // 2, PACK, 128), struct(12, CX // 2, PACK, 128)),
        [VM] * 4,
    )(fields.reshape(9 * NZ * CX, CY), buoyancy.reshape(NZ * CX, CY),
      lame_first.reshape(NZ * CX, CY), shear_modulus.reshape(NZ * CX, CY))
    from_left, from_right = neighbours(right, left, "tile")
    n_down, n_up = len(ABOVE), len(BELOW)
    halo, send_down, send_up = call(
        halo_kernel,
        (struct(12, CX, PACK, 128), struct(n_down + BUOY_ROWS, DEPTH, 128),
         struct(n_up + BUOY_ROWS, DEPTH, 128)),
        [VM] * 3,
    )(main, from_left, from_right)
    par_main, par_halo = main, halo
    below, above = neighbours(send_up, send_down, "region")
    below_first, above_first = below, above
    scratch = [pltpu.VMEM((9, PLANES, ZROWS, 128), jnp.float32),
               pltpu.VMEM((CX + 2 * BUOY_ROWS, DEPTH, 128), jnp.float32)]
    for _ in range(ITERS - 1):
        main, halo, send_down, send_up = call(
            step_kernel,
            (struct(9, CX, NZ, 128), struct(9, CX, PACK, 128), struct(n_down, DEPTH, 128),
             struct(n_up, DEPTH, 128)),
            [VM] * 8, scratch,
        )(main, halo, par_main, par_halo, below, above, below_first, above_first)
        below, above = neighbours(send_up, send_down, "region")
    v, packet = call(
        last_velocity_kernel, (struct(3, PLANES, ZROWS, 128), struct(8, 128)),
        [SM, SM] + [VM] * 11, scratch + [pltpu.VMEM((16, 128), jnp.float32)],
    )(place, station_count, main, halo, par_main, par_halo, below, above, below_first, above_first,
      observed, station_weight.reshape(1, S), station_cell.reshape(1, S))
    here = lax.all_gather(packet, "region")
    before, after = neighbours(here, here, "tile")
    out = call(
        last_kernel, struct(9 * NZ * CX, CY), [SM] * 4 + [VM] * 7,
        [pltpu.VMEM((3, NZ, 128), jnp.float32)],
    )(place, influence, influence_count, depth_profile, main, par_main, v, before, here, after,
      par_halo)
    return out.reshape(9, NZ, CX, CY)


def solution(mesh):
    in_specs = (
        P(None, None, "region", "tile"),
        P(None, "region", "tile"),
        P(None, "region", "tile"),
        P(None, "region", "tile"),
        P(None, ("region", "tile")),
        P(("region", "tile")),
        P(),
        P(("region", "tile")),
        P(("region", "tile")),
        P(("region", "tile"), None),
        P(("region", "tile")),
    )
    out_specs = P(None, None, "region", "tile")
    return jax.shard_map(
        per_device, mesh=mesh, in_specs=in_specs, out_specs=out_specs, check_vma=False
    )
```

time: 668 us -> 148 us (0.22)
  the two profiles are of different devices: /device:TPU:8 before, /device:TPU:22 now
where the time goes in v1:
time: 148 us; the launch traced here: 146 us
  Pallas kernels  47 us (32%)
  waiting for transfers between devices  43.6 us (29%)
  starting transfers between devices  35.8 us (24%)
  local copies, waits for them, and re-layouts  11.7 us (8%)
  blocking collectives  6.68 us (5%)
  between operations  1.51 us (1%)
    ppermute x12, waiting for transfers between devices, neighbours(): return (lax.ppermute(up, axis, forward), lax.ppermute(down, axis, backward))  43.6 us
    ppermute x12, starting transfers between devices, neighbours(): return (lax.ppermute(up, axis, forward), lax.ppermute(down, axis, backward))  35.8 us
    pallas_call x3, Pallas kernels, per_device(): call(step_kernel, (struct(9, CX, NZ, 128), struct(9, CX, PACK, 128), stru...  29.5 us
    unnamed x36, local copies, waits for them, and re-layouts  11.7 us
    pallas_call x1, Pallas kernels, per_device(): call(last_velocity_kernel, (struct(3, PLANES, ZROWS, 128), struct(8, 128)...  8.17 us
    all_gather x1, blocking collectives, per_device(): here = lax.all_gather(packet, 'region')  6.68 us
    pallas_call x1, Pallas kernels, per_device(): call(last_kernel, struct(9 * NZ * CX, CY), [SM] * 4 + [VM] * 7, [pltpu.VM...  6.1 us
  transfers between devices with their start and end apart: 12, of which 7 were waited for; matrix products, arithmetic and copies ran while one was open for 0% of the time, Pallas kernels for 0%

profile of v1, /device:TPU:22, one launch (start us, length us, event | category | flops | bytes accessed | tf_op | source)
XLA Modules:
  0.0 146.4 jit_solution(17869166651710917465)
XLA Ops:
  0.0 0.0 copy-start.7
  0.0 1.7 %copy-done.7 = f32[9,32,16,128]{3,2,1,0:T(8,128)S(1)} copy-done((f32[9,32,16,128]{3,2,1,0:T(8,128)S(1)}, f32[9,32,16,128]{3,2,1,0:T(8,128)}, u32[]{:S(2)}) %copy-start.7) | copy-done | bytes 2359320
  1.7 0.0 copy-start.10
  1.7 0.9 copy-done.10
  2.6 0.0 copy-start.11
  2.6 0.9 copy-done.11
  3.6 0.0 copy-start.12
  3.6 0.9 copy-done.12
  4.5 2.5 %shard_map.109 = (f32[12,16,32,128]{3,2,1,0:T(8,128)S(1)}, f32[12,8,8,128]{3,2,1,0:T(8,128)S(1)}, f32[12,8,8,128]{3,2,1,0:T(8,128)S(1)}) custom-call(f32[4608,128]{1,0:T(8,128)S(1)} %bitcast.10, f32[512,128]{1,0:T(8,128)S(1)} %bitcast.11, f32[512,128]{1,0:T(8,128)S(1)} %bitcast.12, f32[512,128]{1,0:T(8,128)S(1)} %bitcast.13), custom_call_target="tpu_custom_call" | custom-call | tf_op jit(solution)/shard_map/pallas_call | solution.py:362
  7.0 3.2 %collective-permute-start = (f32[12,8,8,128]{3,2,1,0:T(8,128)S(1)}, f32[12,8,8,128]{3,2,1,0:T(8,128)S(1)}, u32[]{:S(2)}, u32[]{:S(2)}) collective-permute-start(f32[12,8,8,128]{3,2,1,0:T(8,128)S(1)} %get-tuple-element.26), channel_id=1, source_target_pairs={{0,1},{1,2},{2,3},{3,4},{4,5},{5,6},{6,7},{7,8},{8,9},{9,10},{10,1... | collective-permute-start | bytes 1179656 | tf_op jit(solution)/shard_map/ppermute | solution.py:356
  10.2 5.7 %collective-permute-start.1 = (f32[12,8,8,128]{3,2,1,0:T(8,128)S(1)}, f32[12,8,8,128]{3,2,1,0:T(8,128)S(1)}, u32[]{:S(2)}, u32[]{:S(2)}) collective-permute-start(f32[12,8,8,128]{3,2,1,0:T(8,128)S(1)} %get-tuple-element.27), channel_id=1, source_target_pairs={{1,0},{2,1},{3,2},{4,3},{5,4},{6,5},{7,6},{8,7},{9,8},{10,9},{11,1... | collective-permute-start | bytes 1179656 | tf_op jit(solution)/shard_map/ppermute | solution.py:356
  15.9 7.3 %collective-permute-done.from_left = f32[12,8,8,128]{3,2,1,0:T(8,128)S(1)} collective-permute-done((f32[12,8,8,128]{3,2,1,0:T(8,128)S(1)}, f32[12,8,8,128]{3,2,1,0:T(8,128)S(1)}, u32[]{:S(2)}, u32[]{:S(2)}) %collective-permute-start) | collective-permute-done | bytes 393248 | tf_op jit(solution)/shard_map/ppermute | solution.py:356
  23.2 6.4 %collective-permute-done.1.from_right = f32[12,8,8,128]{3,2,1,0:T(8,128)S(1)} collective-permute-done((f32[12,8,8,128]{3,2,1,0:T(8,128)S(1)}, f32[12,8,8,128]{3,2,1,0:T(8,128)S(1)}, u32[]{:S(2)}, u32[]{:S(2)}) %collective-permute-start.1) | collective-permute-done | bytes 393248 | tf_op jit(solution)/shard_map/ppermute | solution.py:356
  29.6 0.8 shard_map.110
  30.3 0.0 copy-start
  30.3 1.9 %collective-permute-start.3 = (f32[22,40,128]{2,1,0:T(8,128)S(1)}, f32[22,40,128]{2,1,0:T(8,128)S(1)}, u32[]{:S(2)}, u32[]{:S(2)}) collective-permute-start(f32[22,40,128]{2,1,0:T(8,128)S(1)} %get-tuple-element.30), channel_id=1, source_target_pairs={{32,0},{64,32},{96,64},{33,1},{65,33},{97,65},{34,2},{66,34},{98,6... | collective-permute-start | bytes 1351688 | tf_op jit(solution)/shard_map/ppermute | solution.py:356
  32.3 2.4 %collective-permute-start.2 = (f32[18,40,128]{2,1,0:T(8,128)S(1)}, f32[18,40,128]{2,1,0:T(8,128)S(1)}, u32[]{:S(2)}, u32[]{:S(2)}) collective-permute-start(f32[18,40,128]{2,1,0:T(8,128)S(1)} %get-tuple-element.29), channel_id=1, source_target_pairs={{0,32},{32,64},{64,96},{1,33},{33,65},{65,97},{2,34},{34,66},{66,9... | collective-permute-start | bytes 1105928 | tf_op jit(solution)/shard_map/ppermute | solution.py:356
  34.7 7.9 %collective-permute-done.2.below_ref.below_first = f32[18,40,128]{2,1,0:T(8,128)S(1)} collective-permute-done((f32[18,40,128]{2,1,0:T(8,128)S(1)}, f32[18,40,128]{2,1,0:T(8,128)S(1)}, u32[]{:S(2)}, u32[]{:S(2)}) %collective-permute-start.2) | collective-permute-done | bytes 368672 | tf_op jit(solution)/shard_map/ppermute | solution.py:356
  42.6 0.0 collective-permute-done.3.above_ref.above_first
  42.6 0.0 copy-start.2
  42.6 9.5 %shard_map.111 = (f32[9,16,32,128]{3,2,1,0:T(8,128)S(1)}, f32[9,16,8,128]{3,2,1,0:T(8,128)S(1)}, f32[20,40,128]{2,1,0:T(8,128)S(1)}, f32[16,40,128]{2,1,0:T(8,128)S(1)}) custom-call(f32[12,16,32,128]{3,2,1,0:T(8,128)S(1)} %get-tuple-element.25.main_ref.par_main, f32[12,16,8,128]{3,2,1,0:T(8,128)S(1)} %get-tuple-element.28.halo_ref.par_halo, ...), custom_call_target="tpu_custom_call" | custom-call | tf_op jit(solution)/shard_map/pallas_call | solution.py:382
  52.2 1.9 %collective-permute-start.5 = (f32[20,40,128]{2,1,0:T(8,128)S(1)}, f32[20,40,128]{2,1,0:T(8,128)S(1)}, u32[]{:S(2)}, u32[]{:S(2)}) collective-permute-start(f32[20,40,128]{2,1,0:T(8,128)S(1)} %get-tuple-element.34), channel_id=1, source_target_pairs={{32,0},{64,32},{96,64},{33,1},{65,33},{97,65},{34,2},{66,34},{98,6... | collective-permute-start | bytes 1228808 | tf_op jit(solution)/shard_map/ppermute | solution.py:356
  54.1 2.4 %collective-permute-start.4 = (f32[16,40,128]{2,1,0:T(8,128)S(1)}, f32[16,40,128]{2,1,0:T(8,128)S(1)}, u32[]{:S(2)}, u32[]{:S(2)}) collective-permute-start(f32[16,40,128]{2,1,0:T(8,128)S(1)} %get-tuple-element.33), channel_id=1, source_target_pairs={{0,32},{32,64},{64,96},{1,33},{33,65},{65,97},{2,34},{34,66},{66,9... | collective-permute-start | bytes 983048 | tf_op jit(solution)/shard_map/ppermute | solution.py:356
  56.5 7.5 %collective-permute-done.4.below_ref = f32[16,40,128]{2,1,0:T(8,128)S(1)} collective-permute-done((f32[16,40,128]{2,1,0:T(8,128)S(1)}, f32[16,40,128]{2,1,0:T(8,128)S(1)}, u32[]{:S(2)}, u32[]{:S(2)}) %collective-permute-start.4) | collective-permute-done | bytes 327712 | tf_op jit(solution)/shard_map/ppermute | solution.py:356
  64.0 0.0 collective-permute-done.5.above_ref
  64.0 9.5 %shard_map.112 = (f32[9,16,32,128]{3,2,1,0:T(8,128)S(1)}, f32[9,16,8,128]{3,2,1,0:T(8,128)S(1)}, f32[20,40,128]{2,1,0:T(8,128)S(1)}, f32[16,40,128]{2,1,0:T(8,128)S(1)}) custom-call(f32[9,16,32,128]{3,2,1,0:T(8,128)S(1)} %get-tuple-element.31.main_ref, f32[9,16,8,128]{3,2,1,0:T(8,128)S(1)} %get-tuple-element.32.halo_ref, ...), custom_call_target="tpu_custom_call" | custom-call | tf_op jit(solution)/shard_map/pallas_call | solution.py:382
  73.5 1.9 %collective-permute-start.7 = (f32[20,40,128]{2,1,0:T(8,128)S(1)}, f32[20,40,128]{2,1,0:T(8,128)S(1)}, u32[]{:S(2)}, u32[]{:S(2)}) collective-permute-start(f32[20,40,128]{2,1,0:T(8,128)S(1)} %get-tuple-element.38), channel_id=1, source_target_pairs={{32,0},{64,32},{96,64},{33,1},{65,33},{97,65},{34,2},{66,34},{98,6... | collective-permute-start | bytes 1228808 | tf_op jit(solution)/shard_map/ppermute | solution.py:356
  75.5 2.4 %collective-permute-start.6 = (f32[16,40,128]{2,1,0:T(8,128)S(1)}, f32[16,40,128]{2,1,0:T(8,128)S(1)}, u32[]{:S(2)}, u32[]{:S(2)}) collective-permute-start(f32[16,40,128]{2,1,0:T(8,128)S(1)} %get-tuple-element.37), channel_id=1, source_target_pairs={{0,32},{32,64},{64,96},{1,33},{33,65},{65,97},{2,34},{34,66},{66,9... | collective-permute-start | bytes 983048 | tf_op jit(solution)/shard_map/ppermute | solution.py:356
  77.9 7.5 %collective-permute-done.6.below_ref = f32[16,40,128]{2,1,0:T(8,128)S(1)} collective-permute-done((f32[16,40,128]{2,1,0:T(8,128)S(1)}, f32[16,40,128]{2,1,0:T(8,128)S(1)}, u32[]{:S(2)}, u32[]{:S(2)}) %collective-permute-start.6) | collective-permute-done | bytes 327712 | tf_op jit(solution)/shard_map/ppermute | solution.py:356
  85.4 0.0 collective-permute-done.7.above_ref
  85.4 0.0 copy-done
  85.4 0.0 copy-done.2
  85.4 0.0 copy-start.14
  85.4 0.0 copy-start.16
  85.4 0.0 copy-start.17
  85.4 10.4 %shard_map.113 = (f32[9,16,32,128]{3,2,1,0:T(8,128)S(1)}, f32[9,16,8,128]{3,2,1,0:T(8,128)S(1)}, f32[20,40,128]{2,1,0:T(8,128)}, f32[16,40,128]{2,1,0:T(8,128)}) custom-call(f32[9,16,32,128]{3,2,1,0:T(8,128)S(1)} %get-tuple-element.35.main_ref, f32[9,16,8,128]{3,2,1,0:T(8,128)S(1)} %get-tuple-element.36.halo_ref, ...), custom_call_target="tpu_custom_call" | custom-call | tf_op jit(solution)/shard_map/pallas_call | solution.py:382
  95.8 0.0 copy-start.4
  95.8 1.4 copy-done.4
  97.2 0.0 copy-start.8
  97.3 0.8 copy-done.8
  98.1 1.9 %collective-permute-start.9 = (f32[20,40,128]{2,1,0:T(8,128)}, f32[20,40,128]{2,1,0:T(8,128)}, u32[]{:S(2)}, u32[]{:S(2)}) collective-permute-start(f32[20,40,128]{2,1,0:T(8,128)} %get-tuple-element.42), channel_id=1, source_target_pairs={{32,0},{64,32},{96,64},{33,1},{65,33},{97,65},{34,2},{66,34},{98,6... | collective-permute-start | bytes 1228808 | tf_op jit(solution)/shard_map/ppermute | solution.py:356
  100.0 3.2 %collective-permute-start.8 = (f32[16,40,128]{2,1,0:T(8,128)}, f32[16,40,128]{2,1,0:T(8,128)}, u32[]{:S(2)}, u32[]{:S(2)}) collective-permute-start(f32[16,40,128]{2,1,0:T(8,128)} %get-tuple-element.41), channel_id=1, source_target_pairs={{0,32},{32,64},{64,96},{1,33},{33,65},{65,97},{2,34},{34,66},{66,9... | collective-permute-start | bytes 983048 | tf_op jit(solution)/shard_map/ppermute | solution.py:356
  103.8 0.1 pad_add_fusion.place_ref
  103.9 6.3 %collective-permute-done.8.below_ref = f32[16,40,128]{2,1,0:T(8,128)} collective-permute-done((f32[16,40,128]{2,1,0:T(8,128)}, f32[16,40,128]{2,1,0:T(8,128)}, u32[]{:S(2)}, u32[]{:S(2)}) %collective-permute-start.8) | collective-permute-done | bytes 327712 | tf_op jit(solution)/shard_map/ppermute | solution.py:356
  110.2 0.0 collective-permute-done.9.above_ref
  110.2 0.0 copy-done.14
  110.2 0.0 copy-done.16
  110.2 0.0 copy-done.17
  110.2 0.0 copy-start.1
  110.3 1.1 copy-done.1
  111.4 0.0 copy-start.3
  111.4 1.0 copy-done.3
  112.4 1.7 %copy-done.5 = f32[9,16,32,128]{3,2,1,0:T(8,128)S(1)} copy-done((f32[9,16,32,128]{3,2,1,0:T(8,128)S(1)}, f32[9,16,32,128]{3,2,1,0:T(8,128)}, u32[]{:S(2)}) %copy-start.5) | copy-done | bytes 2359320
  114.1 1.1 copy-done.9
  115.1 8.2 %shard_map.114 = (f32[3,24,72,128]{3,2,1,0:T(8,128)S(1)}, f32[8,128]{1,0:T(8,128)S(1)}) custom-call(s32[2]{0:T(128)S(1)} %pad_add_fusion.place_ref, s32[1]{0:T(128)S(6)} %copy.12.count_ref, f32[9,16,32,128]{3,2,1,0:T(8,128)S(1)} %copy-done.5, f32[9,16,8,128]{3,2,1,0:T(8,128)S(1)} %copy-done.9, f32[12,16,32,128]{3,2,1,0:T(8,128)S(1)} %get-tuple-element.25.main_ref.par_main, ...), custom_call_target="tpu_custom_call" | custom-call | tf_op jit(solution)/shard_map/pallas_call | solution.py:389
  123.3 6.7 %all-gather = f32[32,128]{1,0:T(8,128)S(1)} all-gather(f32[8,128]{1,0:T(8,128)S(1)} %get-tuple-element.44), channel_id=2, replica_groups=mesh['region'=4,'tile'=32] {'region'}, dimensions={0}, use_global_device_ids=true | all-gather | bytes 20480 | tf_op jit(solution)/shard_map/all_gather | solution.py:394
  130.0 3.2 %collective-permute-start.10 = (f32[4,8,128]{2,1,0:T(8,128)S(1)}, f32[4,8,128]{2,1,0:T(8,128)S(1)}, u32[]{:S(2)}, u32[]{:S(2)}) collective-permute-start(f32[4,8,128]{2,1,0:T(8,128)S(1)} %bitcast.14), channel_id=1, source_target_pairs={{0,1},{1,2},{2,3},{3,4},{4,5},{5,6},{6,7},{7,8},{8,9},{9,10},{10,1... | collective-permute-start | bytes 49160 | tf_op jit(solution)/shard_map/ppermute | solution.py:356
  133.2 5.7 %collective-permute-start.11 = (f32[4,8,128]{2,1,0:T(8,128)S(1)}, f32[4,8,128]{2,1,0:T(8,128)S(1)}, u32[]{:S(2)}, u32[]{:S(2)}) collective-permute-start(f32[4,8,128]{2,1,0:T(8,128)S(1)} %bitcast.15), channel_id=1, source_target_pairs={{1,0},{2,1},{3,2},{4,3},{5,4},{6,5},{7,6},{8,7},{9,8},{10,9},{11,1... | collective-permute-start | bytes 49160 | tf_op jit(solution)/shard_map/ppermute | solution.py:356
  139.5 0.0 collective-permute-done.10.before_ref
  139.5 0.8 collective-permute-done.11.after_ref
  140.3 0.0 copy-done.6
  140.3 0.0 copy-done.13
  140.3 0.0 copy-done.15
  140.3 6.1 %shard_map.115 = f32[4608,128]{1,0:T(8,128)} custom-call(s32[2]{0:T(128)S(1)} %pad_add_fusion.place_ref, s32[1,64]{1,0:T(1,128)S(1)} %copy-done.15, s32[1]{0:T(128)S(6)} %copy.13.count_ref, f32[3,32]{1,0:T(4,128)S(1)} %copy-done.13, f32[9,16,32,128]{3,2,1,0:T(8,128)S(1)} %copy-done.6, f32[12,16,32,128]{3,2,1,0:T(8,128)S(1)} %get-tuple-element.25.main_ref.par_main, ...), custom_call_target="tpu_custom_call" | custom-call | tf_op jit(solution)/shard_map/pallas_call | solution.py:396
  (5 shorter events, 0.0 us)
Async XLA Ops:
  0.0 1.7 %copy-start.7 = (f32[9,32,16,128]{3,2,1,0:T(8,128)S(1)}, f32[9,32,16,128]{3,2,1,0:T(8,128)}, u32[]{:S(2)}) copy-start(f32[9,32,16,128]{3,2,1,0:T(8,128)} %param.11) | copy-start | bytes 7077892
  1.7 0.9 copy-start.10
  2.6 0.9 copy-start.11
  3.6 0.9 copy-start.12
  7.0 16.1 %collective-permute-start = (f32[12,8,8,128]{3,2,1,0:T(8,128)S(1)}, f32[12,8,8,128]{3,2,1,0:T(8,128)S(1)}, u32[]{:S(2)}, u32[]{:S(2)}) collective-permute-start(f32[12,8,8,128]{3,2,1,0:T(8,128)S(1)} %get-tuple-element.26), channel_id=1, source_target_pairs={{0,1},{1,2},{2,3},{3,4},{4,5},{5,6},{6,7},{7,8},{8,9},{9,10},{10,1... | collective-permute-start | bytes 1179656 | tf_op jit(solution)/shard_map/ppermute | solution.py:356
  10.2 19.3 %collective-permute-start.1 = (f32[12,8,8,128]{3,2,1,0:T(8,128)S(1)}, f32[12,8,8,128]{3,2,1,0:T(8,128)S(1)}, u32[]{:S(2)}, u32[]{:S(2)}) collective-permute-start(f32[12,8,8,128]{3,2,1,0:T(8,128)S(1)} %get-tuple-element.27), channel_id=1, source_target_pairs={{1,0},{2,1},{3,2},{4,3},{5,4},{6,5},{7,6},{8,7},{9,8},{10,9},{11,1... | collective-permute-start | bytes 1179656 | tf_op jit(solution)/shard_map/ppermute | solution.py:356
  30.3 55.0 %copy-start = (f32[12,16,8,128]{3,2,1,0:T(8,128)}, f32[12,16,8,128]{3,2,1,0:T(8,128)S(1)}, u32[]{:S(2)}) copy-start(f32[12,16,8,128]{3,2,1,0:T(8,128)S(1)} %get-tuple-element.28.halo_ref.par_halo) | copy-start | bytes 2359300
  30.3 12.3 %collective-permute-start.3 = (f32[22,40,128]{2,1,0:T(8,128)S(1)}, f32[22,40,128]{2,1,0:T(8,128)S(1)}, u32[]{:S(2)}, u32[]{:S(2)}) collective-permute-start(f32[22,40,128]{2,1,0:T(8,128)S(1)} %get-tuple-element.30), channel_id=1, source_target_pairs={{32,0},{64,32},{96,64},{33,1},{65,33},{97,65},{34,2},{66,34},{98,6... | collective-permute-start | bytes 1351688 | tf_op jit(solution)/shard_map/ppermute | solution.py:356
  32.3 10.3 %collective-permute-start.2 = (f32[18,40,128]{2,1,0:T(8,128)S(1)}, f32[18,40,128]{2,1,0:T(8,128)S(1)}, u32[]{:S(2)}, u32[]{:S(2)}) collective-permute-start(f32[18,40,128]{2,1,0:T(8,128)S(1)} %get-tuple-element.29), channel_id=1, source_target_pairs={{0,32},{32,64},{64,96},{1,33},{33,65},{65,97},{2,34},{34,66},{66,9... | collective-permute-start | bytes 1105928 | tf_op jit(solution)/shard_map/ppermute | solution.py:356
  42.6 42.7 %copy-start.2 = (f32[22,40,128]{2,1,0:T(8,128)}, f32[22,40,128]{2,1,0:T(8,128)S(1)}, u32[]{:S(2)}) copy-start(f32[22,40,128]{2,1,0:T(8,128)S(1)} %collective-permute-done.3.above_ref.above_first) | copy-start | bytes 1351684
  52.2 11.8 %collective-permute-start.5 = (f32[20,40,128]{2,1,0:T(8,128)S(1)}, f32[20,40,128]{2,1,0:T(8,128)S(1)}, u32[]{:S(2)}, u32[]{:S(2)}) collective-permute-start(f32[20,40,128]{2,1,0:T(8,128)S(1)} %get-tuple-element.34), channel_id=1, source_target_pairs={{32,0},{64,32},{96,64},{33,1},{65,33},{97,65},{34,2},{66,34},{98,6... | collective-permute-start | bytes 1228808 | tf_op jit(solution)/shard_map/ppermute | solution.py:356
  54.1 9.9 %collective-permute-start.4 = (f32[16,40,128]{2,1,0:T(8,128)S(1)}, f32[16,40,128]{2,1,0:T(8,128)S(1)}, u32[]{:S(2)}, u32[]{:S(2)}) collective-permute-start(f32[16,40,128]{2,1,0:T(8,128)S(1)} %get-tuple-element.33), channel_id=1, source_target_pairs={{0,32},{32,64},{64,96},{1,33},{33,65},{65,97},{2,34},{34,66},{66,9... | collective-permute-start | bytes 983048 | tf_op jit(solution)/shard_map/ppermute | solution.py:356
  73.5 11.8 %collective-permute-start.7 = (f32[20,40,128]{2,1,0:T(8,128)S(1)}, f32[20,40,128]{2,1,0:T(8,128)S(1)}, u32[]{:S(2)}, u32[]{:S(2)}) collective-permute-start(f32[20,40,128]{2,1,0:T(8,128)S(1)} %get-tuple-element.38), channel_id=1, source_target_pairs={{32,0},{64,32},{96,64},{33,1},{65,33},{97,65},{34,2},{66,34},{98,6... | collective-permute-start | bytes 1228808 | tf_op jit(solution)/shard_map/ppermute | solution.py:356
  75.5 9.9 %collective-permute-start.6 = (f32[16,40,128]{2,1,0:T(8,128)S(1)}, f32[16,40,128]{2,1,0:T(8,128)S(1)}, u32[]{:S(2)}, u32[]{:S(2)}) collective-permute-start(f32[16,40,128]{2,1,0:T(8,128)S(1)} %get-tuple-element.37), channel_id=1, source_target_pairs={{0,32},{32,64},{64,96},{1,33},{33,65},{65,97},{2,34},{34,66},{66,9... | collective-permute-start | bytes 983048 | tf_op jit(solution)/shard_map/ppermute | solution.py:356
  85.4 24.9 %copy-start.14 = (f32[3,32]{1,0:T(4,128)S(1)}, f32[3,32]{1,0:T(4,128)}, u32[]{:S(2)}) copy-start(f32[3,32]{1,0:T(4,128)} %observed_ref.1) | copy-start | bytes 1156
  85.4 24.8 %copy-start.16 = (f32[32]{0:T(128)S(1)}, f32[32]{0:T(128)}, u32[]{:S(2)}) copy-start(f32[32]{0:T(128)} %param.16) | copy-start | bytes 388
  85.4 24.8 %copy-start.17 = (s32[32]{0:T(128)S(1)}, s32[32]{0:T(128)}, u32[]{:S(2)}) copy-start(s32[32]{0:T(128)} %param.18) | copy-start | bytes 388
  95.8 1.4 copy-start.4
  97.2 0.8 copy-start.8
  98.1 12.1 %collective-permute-start.9 = (f32[20,40,128]{2,1,0:T(8,128)}, f32[20,40,128]{2,1,0:T(8,128)}, u32[]{:S(2)}, u32[]{:S(2)}) collective-permute-start(f32[20,40,128]{2,1,0:T(8,128)} %get-tuple-element.42), channel_id=1, source_target_pairs={{32,0},{64,32},{96,64},{33,1},{65,33},{97,65},{34,2},{66,34},{98,6... | collective-permute-start | bytes 1228808 | tf_op jit(solution)/shard_map/ppermute | solution.py:356
  100.0 10.2 %collective-permute-start.8 = (f32[16,40,128]{2,1,0:T(8,128)}, f32[16,40,128]{2,1,0:T(8,128)}, u32[]{:S(2)}, u32[]{:S(2)}) collective-permute-start(f32[16,40,128]{2,1,0:T(8,128)} %get-tuple-element.41), channel_id=1, source_target_pairs={{0,32},{32,64},{64,96},{1,33},{33,65},{65,97},{2,34},{34,66},{66,9... | collective-permute-start | bytes 983048 | tf_op jit(solution)/shard_map/ppermute | solution.py:356
  110.2 1.1 copy-start.1
  111.4 1.0 copy-start.3
  112.4 1.7 %copy-start.5 = (f32[9,16,32,128]{3,2,1,0:T(8,128)S(1)}, f32[9,16,32,128]{3,2,1,0:T(8,128)}, u32[]{:S(2)}) copy-start(f32[9,16,32,128]{3,2,1,0:T(8,128)} %copy-done.4) | copy-start | bytes 7077892
  114.1 1.1 copy-start.9
  115.1 25.1 %copy-start.6 = (f32[9,16,32,128]{3,2,1,0:T(8,128)S(1)}, f32[9,16,32,128]{3,2,1,0:T(8,128)}, u32[]{:S(2)}) copy-start(f32[9,16,32,128]{3,2,1,0:T(8,128)} %copy-done.4) | copy-start | bytes 7077892
  115.1 25.1 %copy-start.13 = (f32[3,32]{1,0:T(4,128)S(1)}, f32[3,32]{1,0:T(4,128)}, u32[]{:S(2)}) copy-start(f32[3,32]{1,0:T(4,128)} %profile_ref.1) | copy-start | bytes 1156
  115.1 25.1 %copy-start.15 = (s32[1,64]{1,0:T(1,128)S(1)}, s32[1,64]{1,0:T(1,128)}, u32[]{:S(2)}) copy-start(s32[1,64]{1,0:T(1,128)} %influence_ref.1) | copy-start | bytes 772
  130.0 9.5 %collective-permute-start.10 = (f32[4,8,128]{2,1,0:T(8,128)S(1)}, f32[4,8,128]{2,1,0:T(8,128)S(1)}, u32[]{:S(2)}, u32[]{:S(2)}) collective-permute-start(f32[4,8,128]{2,1,0:T(8,128)S(1)} %bitcast.14), channel_id=1, source_target_pairs={{0,1},{1,2},{2,3},{3,4},{4,5},{5,6},{6,7},{7,8},{8,9},{9,10},{10,1... | collective-permute-start | bytes 49160 | tf_op jit(solution)/shard_map/ppermute | solution.py:356
  133.2 7.1 %collective-permute-start.11 = (f32[4,8,128]{2,1,0:T(8,128)S(1)}, f32[4,8,128]{2,1,0:T(8,128)S(1)}, u32[]{:S(2)}, u32[]{:S(2)}) collective-permute-start(f32[4,8,128]{2,1,0:T(8,128)S(1)} %bitcast.15), channel_id=1, source_target_pairs={{1,0},{2,1},{3,2},{4,3},{5,4},{6,5},{7,6},{8,7},{9,8},{10,9},{11,1... | collective-permute-start | bytes 49160 | tf_op jit(solution)/shard_map/ppermute | solution.py:356

commit v2 on v0

v2 whole, which is shorter than its diff:
```python
import jax
import jax.numpy as jnp
import numpy as np
from jax import lax
from jax.experimental import pallas as pl
from jax.experimental.pallas import tpu as pltpu
from jax.sharding import PartitionSpec as P

NEAR = 1.125
FAR = -1.0 / 24.0
DT = 0.15

CX, CY, NZ = 16, 128, 32
S, LIST = 32, 64
GROUPS = 4
HALF = 16
WIDE = 12
PACK = NZ // GROUPS
DEPTH = NZ + PACK
LOW = 6
PLANES = CX + 2 * LOW
ZROWS = 72

VX, VY, VZ = range(3)
SXX, SYY, SZZ, SXY, SXZ, SYZ = range(6)
Z_STRESS = (SZZ, SXZ, SYZ)

OUTER = [("t", f, 6) for f in (SXX, SXY, SXZ)] + [("t", f, 5) for f in (SYY, SYZ, SZZ)] + [
    ("v", f, 5) for f in range(3)]
OUTER_FIRST = OUTER + [("p", 0, 5), ("p", 1, 3), ("p", 2, 3)]
INNER = [("t", f, 3) for f in (SXX, SXY, SXZ)] + [("t", f, 2) for f in (SYY, SYZ, SZZ)] + [
    ("v", f, 2) for f in range(3)]
INNER_FIRST = INNER + [("p", 0, 2)]

VMEM_BYTES = 8 * 2 ** 20


def is_odd():
    return lax.rem(lax.axis_index("region"), 2) > 0


def plane_count(items):
    return sum(d for _, _, d in items)


def lanes(rows):
    return lax.broadcasted_iota(jnp.int32, (rows, 128), 1)


def band_matrices():
    taps = {0: ((-1, 1), (0, -27), (1, 27), (2, -1)), 1: ((-2, 1), (-1, -27), (0, 27), (1, -1))}
    own = np.zeros((2, GROUPS, 256, 128), np.float32)
    halo = np.zeros((2, 640, 128), np.float32)
    for k in range(2):
        for offset, coef in taps[k]:
            for g in range(GROUPS):
                for lane in range(128):
                    y = lane + offset
                    if 0 <= y < CY:
                        own[k, g, y, lane] += coef
                    else:
                        own[k, g, 128 + 32 * g + HALF + (y if y < 0 else y - CY), lane] += coef
                for spot in range(32):
                    to = spot + offset
                    out = 32 * g + spot
                    if not 0 <= to < 32:
                        continue
                    if (spot < HALF) == (to < HALF):
                        halo[k, 512 + 32 * g + to, out] += coef
                    elif spot < HALF:
                        halo[k, 128 * g + to - HALF, out] += coef
                    else:
                        halo[k, 128 * g + CY + to - HALF, out] += coef
    return own, halo


def two_terms(value):
    high = value.astype(jnp.bfloat16)
    return high, (value - high.astype(jnp.float32)).astype(jnp.bfloat16)


def y_differences(items, count, forward, own_ref, halo_ref, out_ref):
    k = 0 if forward else 1
    even = count + count % 2

    def rows(at):
        return jnp.concatenate(
            [ref[f, x + j, at:at + 8, :] for ref, f, x, _ in items for j in range(even)], axis=0)

    parts = [two_terms(rows(8 + 8 * g)) for g in range(GROUPS)] + [two_terms(rows(56))]

    def product(lhs, rhs):
        return jnp.dot(lhs, rhs, preferred_element_type=jnp.float32)

    for g in range(GROUPS + 1):
        total = 0.0
        for term in range(2):
            if g < GROUPS:
                lhs = jnp.concatenate([parts[g][term], parts[GROUPS][term]], axis=1)
                total += product(lhs, own_ref[k, g])
            else:
                lhs = jnp.concatenate([parts[n][term] for n in range(GROUPS + 1)], axis=1)
                total += product(lhs, halo_ref[k])
        total = total * (1.0 / 24.0)
        for n, (_, _, _, slot) in enumerate(items):
            for j in range(count):
                r = 8 * (n * even + j)
                out_ref[slot, j, 8 * g:8 * g + 8, :] = total[r:r + 8]


def load(ref, f, x, dz=0):
    return jnp.concatenate(
        [ref[f, x, 8 + dz:8 + NZ + dz, :], ref[f, x, 56 + dz:64 + dz, :]], axis=0)


def store(ref, f, x, value):
    ref[f, x, 8:8 + NZ, :] = value[:NZ]
    ref[f, x, 56:64, :] = value[NZ:]


def pad_halo(ref, f, x):
    lane = lanes(PACK)
    halo = ref[f, x, 56:64, :]
    ref[f, x, 48:56, :] = jnp.where(lane < 32, 0.0, pltpu.roll(halo, 32, 1))
    ref[f, x, 64:72, :] = jnp.where(lane >= 96, 0.0, pltpu.roll(halo, 96, 1))


def combine(m1, c0, p1, p2):
    return NEAR * (p1 - c0) + FAR * (p2 - m1)


def diff_x(ref, f, x, forward):
    first = -1 if forward else -2
    return combine(*[load(ref, f, x + first + k) for k in range(4)])


def diff_z(ref, f, x, forward):
    first = -1 if forward else -2
    return combine(*[load(ref, f, x, first + k) for k in range(4)])


def velocity_pass(v_ref, t_ref, p_ref, own_ref, halo_ref, d_ref, x_first, y_first, count):
    xa, ya = x_first + LOW, y_first + LOW
    y_differences([(t_ref, SXY, xa, 0), (t_ref, SYZ, ya, 2)], count, False, own_ref, halo_ref, d_ref)
    y_differences([(t_ref, SYY, ya, 1)], count, True, own_ref, halo_ref, d_ref)

    def body(j, _):
        x = xa + j
        force = diff_x(t_ref, SXX, x, True) + d_ref[0, j] + diff_z(t_ref, SXZ, x, False)
        store(v_ref, VX, x, load(v_ref, VX, x) + p_ref[0, x] * force)
        x = ya + j
        b = p_ref[0, x]
        force = diff_x(t_ref, SXY, x, False) + d_ref[1, j] + diff_z(t_ref, SYZ, x, False)
        store(v_ref, VY, x, load(v_ref, VY, x) + b * force)
        force = diff_x(t_ref, SXZ, x, False) + d_ref[2, j] + diff_z(t_ref, SZZ, x, True)
        store(v_ref, VZ, x, load(v_ref, VZ, x) + b * force)
        return 0

    lax.fori_loop(0, count, body, 0)
    for j in range(count):
        pad_halo(v_ref, VX, xa + j)
        pad_halo(v_ref, VY, ya + j)
        pad_halo(v_ref, VZ, ya + j)


def stress_pass(v_ref, t_ref, p_ref, own_ref, halo_ref, d_ref, first, count, pads=True):
    a = first + LOW
    y_differences([(v_ref, VX, a, 0), (v_ref, VZ, a, 2)], count, True, own_ref, halo_ref, d_ref)
    y_differences([(v_ref, VY, a, 1)], count, False, own_ref, halo_ref, d_ref)

    def body(j, _):
        x = a + j
        lame, mu = p_ref[1, x], p_ref[2, x]
        grad_x = diff_x(v_ref, VX, x, False)
        grad_y = d_ref[1, j]
        grad_z = diff_z(v_ref, VZ, x, False)
        modulus = lame + 2.0 * mu
        rates = (
            (SXX, modulus * grad_x + lame * (grad_y + grad_z)),
            (SYY, modulus * grad_y + lame * (grad_x + grad_z)),
            (SZZ, modulus * grad_z + lame * (grad_x + grad_y)),
            (SXY, mu * (d_ref[0, j] + diff_x(v_ref, VY, x, True))),
            (SXZ, mu * (diff_z(v_ref, VX, x, True) + diff_x(v_ref, VZ, x, True))),
            (SYZ, mu * (diff_z(v_ref, VY, x, True) + d_ref[2, j])),
        )
        for f, rate in rates:
            store(t_ref, f, x, load(t_ref, f, x) + rate)
        return 0

    lax.fori_loop(0, count, body, 0)
    if pads:
        for j in range(count):
            for f in Z_STRESS:
                pad_halo(t_ref, f, a + j)


def take_halo(items, odd, inner, got_ref, v_ref, t_ref, p_ref):
    n = 0
    padded = []
    for kind, f, depth in items:
        above, below = CX, -depth
        row = jnp.where(odd, below, above) if inner else jnp.where(odd, above, below)
        for k in range(depth):
            x = row + LOW + k
            if kind == "p":
                p_ref[f, x] = got_ref[n]
            else:
                store(v_ref if kind == "v" else t_ref, f, x, got_ref[n])
                if kind == "v" or f in Z_STRESS:
                    padded.append((v_ref if kind == "v" else t_ref, f, x))
            n += 1
    for ref, f, x in padded:
        pad_halo(ref, f, x)


def give_halo(items, odd, inner, send_ref, v_ref, t_ref, p_ref):
    n = 0
    for kind, f, depth in items:
        top, bottom = CX - depth, 0
        row = jnp.where(odd, bottom, top) if inner else jnp.where(odd, top, bottom)
        for k in range(depth):
            x = row + LOW + k
            if kind == "p":
                send_ref[n] = p_ref[f, x]
            else:
                send_ref[n] = load(v_ref if kind == "v" else t_ref, f, x)
            n += 1


def pieces():
    out = []
    for u in range(8):
        for v in range(3):
            start = WIDE * u - 32 * v
            a, b = max(0, start), min(32, start + WIDE)
            if a < b:
                out.append((u, v, start, a, b))
    return out


PIECES = pieces()


def edge_pack(main):
    lane = lanes(PACK)
    out = pltpu.roll(main[0:8], HALF, 1)
    for g in range(1, GROUPS):
        rolled = pltpu.roll(main[8 * g:8 * g + 8], (HALF + 32 * g) % 128, 1)
        out = jnp.where(lane >= 32 * g, rolled, out)
    return out


def fetch(refs, buf_ref, sems):
    size = NZ * CX
    waits = []
    for a in range(12):
        src = refs[0].at[pl.ds(a * size, size)] if a < 9 else refs[a - 8]
        waits.append(pltpu.make_async_copy(src, buf_ref.at[pl.ds(a * size, size)], sems.at[a]))
    for copy in waits:
        copy.start()
    return waits


def edge_kernel(fields_ref, buoy_ref, lame_ref, mu_ref, right_ref, left_ref, buf_ref, sems):
    size = NZ * CX
    spot = lanes(PACK) % 32
    for a, copy in enumerate(fetch((fields_ref, buoy_ref, lame_ref, mu_ref), buf_ref, sems)):
        copy.wait()
        for block in range(2):
            rights, lefts = [None] * 3, [None] * 3
            edges = [edge_pack(buf_ref[pl.ds(a * size + 8 * block + u, NZ, stride=CX), :])
                     for u in range(8)]
            for u, v, start, lo, hi in PIECES:
                keep = (spot >= lo) & (spot < hi)
                for parts, at in ((rights, HALF - WIDE), (lefts, HALF)):
                    moved = pltpu.roll(edges[u], (start - at) % 128, 1)
                    parts[v] = moved if parts[v] is None else jnp.where(keep, moved, parts[v])
            for v in range(3):
                right_ref[a, 3 * block + v] = rights[v]
                left_ref[a, 3 * block + v] = lefts[v]


def build_kernel(fields_ref, buoy_ref, lame_ref, mu_ref, v_ref, t_ref, p_ref):
    size = NZ * CX
    zero = jnp.zeros((8, 128), jnp.float32)

    def clear(x, _):
        for ref, f in [(v_ref, f) for f in range(3)] + [(t_ref, f) for f in Z_STRESS]:
            ref[f, x, 0:8, :] = zero
            ref[f, x, 40:48, :] = zero
        return 0

    lax.fori_loop(0, PLANES, clear, 0)
    for a in range(12):
        for x in range(CX):
            if a < 3:
                v_ref[a, x + LOW, 8:8 + NZ, :] = fields_ref[pl.ds(a * size + x, NZ, stride=CX), :]
            elif a < 9:
                t_ref[a - 3, x + LOW, 8:8 + NZ, :] = fields_ref[pl.ds(a * size + x, NZ, stride=CX), :]
            else:
                ref = (buoy_ref, lame_ref, mu_ref)[a - 9]
                p_ref[a - 9, x + LOW, 0:NZ, :] = DT * ref[pl.ds(x, NZ, stride=CX), :]


def halo_kernel(from_left, from_right, v_in, t_in, p_in, v_ref, t_ref, p_ref, outer_ref,
                inner_ref):
    odd = is_odd()
    spot = lanes(PACK) % 32

    def one(a, put):
        for block in range(2):
            for u in range(8):
                value = jnp.zeros((PACK, 128), jnp.float32)
                for w, v, start, lo, hi in PIECES:
                    if w != u:
                        continue
                    for ref, at in ((from_left, HALF - WIDE), (from_right, HALF)):
                        keep = (spot >= lo - start + at) & (spot < hi - start + at)
                        moved = pltpu.roll(ref[a, 3 * block + v], (at - start) % 128, 1)
                        value = jnp.where(keep, moved, value)
                put(8 * block + u + LOW, value)

    def to_v(f, _):
        def put(x, value):
            v_ref[f, x, 56:64, :] = value
        one(f, put)
        return 0

    def to_t(f, _):
        def put(x, value):
            t_ref[f, x, 56:64, :] = value
        one(f + 3, put)
        return 0

    def to_p(f, _):
        def put(x, value):
            p_ref[f, x, NZ:DEPTH, :] = DT * value
        one(f + 9, put)
        return 0

    lax.fori_loop(0, 3, to_v, 0)
    lax.fori_loop(0, 6, to_t, 0)
    lax.fori_loop(0, 3, to_p, 0)

    give_halo(OUTER_FIRST, odd, False, outer_ref, v_ref, t_ref, p_ref)
    give_halo(INNER_FIRST, odd, True, inner_ref, v_ref, t_ref, p_ref)


def pad_own(v_ref, t_ref):
    def pads(x, _):
        for f in range(3):
            pad_halo(v_ref, f, x)
        for f in Z_STRESS:
            pad_halo(t_ref, f, x)
        return 0

    lax.fori_loop(LOW, LOW + CX, pads, 0)


def near_kernel(items, back, sends, own_ref, halo_ref, got_ref, v_in, t_in, p_in, *refs):
    if sends:
        v_ref, t_ref, p_ref, inner_ref, d_ref = refs
    else:
        v_ref, t_ref, p_ref, d_ref = refs
    odd = is_odd()
    if items is INNER_FIRST:
        pad_own(v_ref, t_ref)
    take_halo(items, odd, True, got_ref, v_ref, t_ref, p_ref)
    mats = (v_ref, t_ref, p_ref, own_ref, halo_ref, d_ref)
    velocity_pass(*mats, jnp.where(odd, -2, back + 1), jnp.where(odd, -1, back + 2), CX - back)
    stress_pass(*mats, jnp.where(odd, 0, back + 3), CX - 3 - back)
    if sends:
        give_halo(INNER, odd, True, inner_ref, v_ref, t_ref, p_ref)


def far_steps(items, last, odd, got_ref, v_ref, t_ref, p_ref, own_ref, halo_ref, d_ref):
    take_halo(items, odd, False, got_ref, v_ref, t_ref, p_ref)
    mats = (v_ref, t_ref, p_ref, own_ref, halo_ref, d_ref)
    velocity_pass(*mats, jnp.where(odd, 14, -5), jnp.where(odd, 15, -4), 6)
    stress_pass(*mats, jnp.where(odd, 13, -3), 6)
    velocity_pass(*mats, jnp.where(odd, 11, -2), jnp.where(odd, 12, -1), 6)
    if not last:
        stress_pass(*mats, jnp.where(odd, 10, 0), 6)


def far_kernel(items, own_ref, halo_ref, got_ref, v_in, t_in, p_in, v_ref, t_ref, p_ref,
               outer_ref, d_ref):
    odd = is_odd()
    far_steps(items, False, odd, got_ref, v_ref, t_ref, p_ref, own_ref, halo_ref, d_ref)
    give_halo(OUTER, odd, False, outer_ref, v_ref, t_ref, p_ref)


def station_kernel(items, count_ref, observed_ref, gain_ref, cell_ref, own_ref, halo_ref,
                   got_ref, v_in, t_in, p_in, v_ref, t_ref, p_ref, packet_ref, d_ref, slot_ref):
    odd = is_odd()
    far_steps(items, True, odd, got_ref, v_ref, t_ref, p_ref, own_ref, halo_ref, d_ref)
    slot_ref[...] = jnp.zeros((16, 128), jnp.float32)
    slot_ref[0:3, 0:S] = observed_ref[...]
    slot_ref[3:4, 0:S] = gain_ref[...]
    slot_ref[4:5, 0:S] = cell_ref[...].astype(jnp.float32)
    cell = slot_ref[4:5, :].astype(jnp.int32)
    cell_x, cell_y = cell // CY, cell % CY
    pick_y = (lax.broadcasted_iota(jnp.int32, (CY, 128), 0) == cell_y).astype(jnp.float32)
    pick_x = lax.broadcasted_iota(jnp.int32, (CX, 128), 0) == cell_x
    live = lanes(1) < count_ref[0]
    gain = slot_ref[3:4, :]
    region, tile = lax.axis_index("region"), lax.axis_index("tile")
    surface = jnp.concatenate(
        [v_ref[c, r + LOW, 8:9, :] for c in range(3) for r in range(CX)], axis=0)
    rows = jnp.dot(surface, pick_y, precision=lax.Precision.HIGHEST,
                   preferred_element_type=jnp.float32)
    for c in range(3):
        picked = jnp.where(pick_x, rows[c * CX:(c + 1) * CX], 0.0)
        sample = jnp.sum(picked, axis=0, keepdims=True)
        slot_ref[8 + c:9 + c, :] = jnp.where(live, gain * (slot_ref[c:c + 1, :] - sample), 0.0)
    slot_ref[11:12, :] = (region * CX + cell_x).astype(jnp.float32)
    slot_ref[12:13, :] = (tile * CY + cell_y).astype(jnp.float32)
    own = jnp.where(lanes(8) < S, slot_ref[8:16, :], 0.0)
    packet_ref[...] = pltpu.roll(own, region * S, 1)


def stress_out_kernel(own_ref, halo_ref, v_ref, t_in, p_ref, t_ref, out_ref, d_ref,
                      rows_ref, sem):
    odd = is_odd()
    stress_pass(v_ref, t_ref, p_ref, own_ref, halo_ref, d_ref, jnp.where(odd, 10, 0), 6, pads=False)
    size = NZ * CX

    def body(r, _):
        for f in range(6):
            rows_ref[pl.ds(f * size + r, NZ, stride=CX), :] = t_ref[f, r + LOW, 8:8 + NZ, :]
        return 0

    lax.fori_loop(0, CX, body, 0)
    copy = pltpu.make_async_copy(rows_ref, out_ref.at[pl.ds(3 * size, 6 * size)], sem)
    copy.start()
    copy.wait()


def increment_kernel(influence_ref, count_ref, profile_ref, v_ref, before_ref, here_ref,
                     after_ref, out_in, out_ref, profile_rows, rows_ref, sem):
    region, tile = lax.axis_index("region"), lax.axis_index("tile")
    lane = lanes(8)
    column = lax.broadcasted_iota(jnp.int32, (8, 128), 0) + tile - 1
    slot_id = (lane // S * 32 + column) * S + lane % S
    slot_id = jnp.where((column >= 0) & (column < 32), slot_id, -1)
    used = jnp.zeros((8, 128), jnp.int32)
    for k in range(LIST):
        hit = (slot_id == influence_ref[0, k]) & (k < count_ref[0])
        used = jnp.where(hit, 1, used)
    cell_x = (lax.broadcasted_iota(jnp.int32, (CX, 128), 0) + region * CX).astype(jnp.float32)
    cell_y = (lax.broadcasted_iota(jnp.int32, (CY, 128), 0) + tile * CY).astype(jnp.float32)
    increment = jnp.zeros((3 * CX, CY), jnp.float32)
    for d, ref in enumerate((before_ref, here_ref, after_ref)):
        packet = ref[0] + ref[1] + ref[2] + ref[3]
        dist_x = cell_x - packet[3:4]
        dist_y = cell_y - packet[4:5]
        along_x = jnp.exp(-(dist_x * dist_x) / (2.0 * (0.5 * CX) ** 2))
        along_y = jnp.exp(-(dist_y * dist_y) / (2.0 * (0.25 * CY) ** 2))
        keep = used[d:d + 1] > 0
        scaled = jnp.concatenate(
            [jnp.where(keep, packet[c:c + 1] * along_x, 0.0) for c in range(3)], axis=0)
        increment += lax.dot_general(
            scaled, along_y, (((1,), (1,)), ((), ())), precision=lax.Precision.HIGHEST,
            preferred_element_type=jnp.float32)
    for c in range(3):
        for z in range(NZ):
            profile_rows[c, z:z + 1, :] = jnp.full((1, 128), profile_ref[c, z], jnp.float32)
    for c in range(3):
        for r in range(CX):
            value = v_ref[c, r + LOW, 8:8 + NZ, :]
            value = value + profile_rows[c] * increment[c * CX + r:c * CX + r + 1, :]
            rows_ref[pl.ds(c * NZ * CX + r, NZ, stride=CX), :] = value
    copy = pltpu.make_async_copy(rows_ref, out_ref.at[pl.ds(0, 3 * NZ * CX)], sem)
    copy.start()
    copy.wait()


def struct(*shape):
    return jax.ShapeDtypeStruct(shape, jnp.float32)


VM = pl.BlockSpec(memory_space=pltpu.VMEM)
SM = pl.BlockSpec(memory_space=pltpu.SMEM)
HB = pl.BlockSpec(memory_space=pltpu.HBM)


def call(kernel, outs, specs, scratch, out_specs=None, aliases=None, vmem=VMEM_BYTES):
    return pl.pallas_call(
        kernel, out_shape=outs, in_specs=specs, out_specs=out_specs or [VM] * len(outs),
        scratch_shapes=list(scratch), input_output_aliases=aliases or {},
        compiler_params=pltpu.CompilerParams(vmem_limit_bytes=vmem))


INNER_SWAP = [(0, 1), (1, 0), (2, 3), (3, 2)]
OUTER_SWAP = [(1, 2), (2, 1)]


def bind(kernel, *first):
    def bound(*refs):
        return kernel(*first, *refs)
    return bound


def per_device(fields, buoyancy, lame_first, shear_modulus, observed, station_weight, depth_profile,
               station_cell, station_count, influence, influence_count):
    own, edge = band_matrices()
    own, edge = jnp.asarray(own, jnp.bfloat16), jnp.asarray(edge, jnp.bfloat16)
    size = NZ * CX
    state = (struct(3, PLANES, ZROWS, 128), struct(6, PLANES, ZROWS, 128),
             struct(3, PLANES, DEPTH, 128))
    given = (fields.reshape(9 * size, CY), buoyancy.reshape(size, CY),
             lame_first.reshape(size, CY), shear_modulus.reshape(size, CY))
    fetched = [pltpu.VMEM((12 * size, 128), jnp.float32), pltpu.SemaphoreType.DMA((12,))]
    right, left = call(edge_kernel, (struct(12, 6, PACK, 128),) * 2, [HB] * 4, fetched,
                       vmem=60 * 2 ** 20)(*given)
    count = lax.axis_size("tile")
    forward = [(i, i + 1) for i in range(count - 1)]
    backward = [(b, a) for a, b in forward]
    from_left = lax.ppermute(right, "tile", forward)
    from_right = lax.ppermute(left, "tile", backward)
    v, t, p = call(build_kernel, state, [VM] * 4, [])(*given)
    v, t, p, outer, inner = call(
        halo_kernel, state + (struct(plane_count(OUTER_FIRST), DEPTH, 128),
                              struct(plane_count(INNER_FIRST), DEPTH, 128)),
        [VM] * 5, [], aliases={2: 0, 3: 1, 4: 2},
    )(from_left, from_right, v, t, p)
    inner_struct = struct(plane_count(INNER), DEPTH, 128)
    d_scratch = pltpu.VMEM((3, CX, DEPTH, 128), jnp.float32)
    alias = {3: 0, 4: 1, 5: 2}
    for block in range(2):
        got = lax.ppermute(inner, "region", INNER_SWAP)
        got_outer = lax.ppermute(outer, "region", OUTER_SWAP)
        v, t, p, inner = call(
            bind(near_kernel, INNER_FIRST if block == 0 else INNER, 0, True),
            state + (inner_struct,), [VM] * 6, [d_scratch], aliases=alias,
        )(own, edge, got, v, t, p)
        got = lax.ppermute(inner, "region", INNER_SWAP)
        if block == 0:
            v, t, p, inner = call(
                bind(near_kernel, INNER, 3, True), state + (inner_struct,), [VM] * 6,
                [d_scratch], aliases=alias,
            )(own, edge, got, v, t, p)
            v, t, p, outer = call(
                bind(far_kernel, OUTER_FIRST), state + (struct(plane_count(OUTER), DEPTH, 128),),
                [VM] * 6, [d_scratch], aliases=alias,
            )(own, edge, got_outer, v, t, p)
        else:
            v, t, p = call(
                bind(near_kernel, INNER, 3, False), state, [VM] * 6, [d_scratch],
                aliases=alias,
            )(own, edge, got, v, t, p)
    v, t, p, packet = call(
        bind(station_kernel, OUTER), state + (struct(8, 128),), [SM] + [VM] * 9,
        [d_scratch, pltpu.VMEM((16, 128), jnp.float32)], aliases={7: 0, 8: 1, 9: 2},
    )(station_count, observed, station_weight.reshape(1, S), station_cell.reshape(1, S),
      own, edge, got_outer, v, t, p)
    here = lax.all_gather(packet, "region")
    before = lax.ppermute(here, "tile", forward)
    after = lax.ppermute(here, "tile", backward)
    _, out = call(
        stress_out_kernel, (state[1], struct(9 * size, 128)), [VM] * 5,
        [d_scratch, pltpu.VMEM((6 * size, 128), jnp.float32), pltpu.SemaphoreType.DMA],
        out_specs=[VM, HB], aliases={3: 0},
    )(own, edge, v, t, p)
    out, = call(
        increment_kernel, (struct(9 * size, 128),), [SM] * 3 + [VM] * 4 + [HB],
        [pltpu.VMEM((3, NZ, 128), jnp.float32), pltpu.VMEM((3 * size, 128), jnp.float32),
         pltpu.SemaphoreType.DMA], out_specs=[HB], aliases={7: 0},
    )(influence, influence_count, depth_profile, v, before, here, after, out)
    return out.reshape(9, NZ, CX, CY)


def solution(mesh):
    in_specs = (
        P(None, None, "region", "tile"),
        P(None, "region", "tile"),
        P(None, "region", "tile"),
        P(None, "region", "tile"),
        P(None, ("region", "tile")),
        P(("region", "tile")),
        P(),
        P(("region", "tile")),
        P(("region", "tile")),
        P(("region", "tile"), None),
        P(("region", "tile")),
    )
    out_specs = P(None, None, "region", "tile")
    return jax.shard_map(
        per_device, mesh=mesh, in_specs=in_specs, out_specs=out_specs, check_vma=False
    )
```

time: 668 us -> 88.6 us (0.13)
  the two profiles are of different devices: /device:TPU:8 before, /device:TPU:22 now
where the time goes in v2:
time: 88.6 us; the launch traced here: 88.3 us
  Pallas kernels  31.3 us (35%)
  waiting for transfers between devices  26.3 us (30%)
  starting transfers between devices  22.3 us (25%)
  blocking collectives  6.68 us (8%)
  between operations  1.69 us (2%)
    ppermute x2, waiting for transfers between devices, per_device(): got_outer = lax.ppermute(outer, 'region', OUTER_SWAP)  11.6 us
    pallas_call x2, Pallas kernels, per_device(): call(bind(near_kernel, INNER_FIRST if block == 0 else INNER, 0, True), st...  7.81 us
    all_gather x1, blocking collectives, per_device(): here = lax.all_gather(packet, 'region')  6.68 us
    ppermute x4, waiting for transfers between devices, per_device(): got = lax.ppermute(inner, 'region', INNER_SWAP)  6.24 us
    ppermute x1, starting transfers between devices, per_device(): after = lax.ppermute(here, 'tile', backward)  5.66 us
    ppermute x1, starting transfers between devices, per_device(): from_right = lax.ppermute(left, 'tile', backward)  5.66 us
    pallas_call x1, Pallas kernels, per_device(): call(edge_kernel, (struct(12, 6, PACK, 128),) * 2, [HB] * 4, fetched, vme...  4.77 us
    ppermute x1, waiting for transfers between devices, per_device(): from_right = lax.ppermute(left, 'tile', backward)  4.28 us
  transfers between devices with their start and end apart: 10, of which 8 were waited for; matrix products, arithmetic and copies ran while one was open for 0% of the time, Pallas kernels for 19%

profile of v2, /device:TPU:22, one launch (start us, length us, event | category | flops | bytes accessed | tf_op | source)
XLA Modules:
  0.0 88.3 jit_solution(11537042059870174077)
XLA Ops:
  0.0 0.0 copy-start.2
  0.0 0.0 copy-start.3
  0.0 0.0 copy-start.4
  0.0 0.0 copy-start.5
  0.0 4.8 %shard_map.127 = (f32[12,6,8,128]{3,2,1,0:T(8,128)}, f32[12,6,8,128]{3,2,1,0:T(8,128)}) custom-call(f32[4608,128]{1,0:T(8,128)} %bitcast.8, f32[512,128]{1,0:T(8,128)} %bitcast.10, f32[512,128]{1,0:T(8,128)} %bitcast.12, f32[512,128]{1,0:T(8,128)} %bitcast.14), custom_call_target="tpu_custom_call" | custom-call | tf_op jit(solution)/shard_map/pallas_call | solution.py:514
  4.8 3.2 %collective-permute-start = (f32[12,6,8,128]{3,2,1,0:T(8,128)}, f32[12,6,8,128]{3,2,1,0:T(8,128)S(1)}, u32[]{:S(2)}, u32[]{:S(2)}) collective-permute-start(f32[12,6,8,128]{3,2,1,0:T(8,128)} %get-tuple-element.39), channel_id=1, source_target_pairs={{0,1},{1,2},{2,3},{3,4},{4,5},{5,6},{6,7},{7,8},{8,9},{9,10},{10,1... | collective-permute-start | bytes 884744 | tf_op jit(solution)/shard_map/ppermute | solution.py:519
  8.0 5.7 %collective-permute-start.1 = (f32[12,6,8,128]{3,2,1,0:T(8,128)}, f32[12,6,8,128]{3,2,1,0:T(8,128)S(1)}, u32[]{:S(2)}, u32[]{:S(2)}) collective-permute-start(f32[12,6,8,128]{3,2,1,0:T(8,128)} %get-tuple-element.40), channel_id=1, source_target_pairs={{1,0},{2,1},{3,2},{4,3},{5,4},{6,5},{7,6},{8,7},{9,8},{10,9},{11,1... | collective-permute-start | bytes 884744 | tf_op jit(solution)/shard_map/ppermute | solution.py:520
  13.7 0.0 copy-done.2
  13.7 0.0 copy-done.3
  13.7 0.0 copy-done.4
  13.7 0.0 copy-done.5
  13.7 1.2 %shard_map.128 = (f32[3,28,72,128]{3,2,1,0:T(8,128)S(1)}, f32[6,28,72,128]{3,2,1,0:T(8,128)S(1)}, f32[3,28,40,128]{3,2,1,0:T(8,128)S(1)}) custom-call(f32[4608,128]{1,0:T(8,128)S(1)} %bitcast.9, f32[512,128]{1,0:T(8,128)S(1)} %bitcast.11, f32[512,128]{1,0:T(8,128)S(1)} %bitcast.13, f32[512,128]{1,0:T(8,128)S(1)} %bitcast.15), custom_call_target="tpu_custom_call" | custom-call | tf_op jit(solution)/shard_map/pallas_call | solution.py:521
  14.9 4.2 %collective-permute-done.from_left = f32[12,6,8,128]{3,2,1,0:T(8,128)S(1)} collective-permute-done((f32[12,6,8,128]{3,2,1,0:T(8,128)}, f32[12,6,8,128]{3,2,1,0:T(8,128)S(1)}, u32[]{:S(2)}, u32[]{:S(2)}) %collective-permute-start) | collective-permute-done | bytes 294944 | tf_op jit(solution)/shard_map/ppermute | solution.py:519
  19.0 4.3 %collective-permute-done.1.from_right = f32[12,6,8,128]{3,2,1,0:T(8,128)S(1)} collective-permute-done((f32[12,6,8,128]{3,2,1,0:T(8,128)}, f32[12,6,8,128]{3,2,1,0:T(8,128)S(1)}, u32[]{:S(2)}, u32[]{:S(2)}) %collective-permute-start.1) | collective-permute-done | bytes 294944 | tf_op jit(solution)/shard_map/ppermute | solution.py:520
  23.3 0.0 copy-start
  23.3 0.0 copy-start.1
  23.3 1.4 %shard_map.129 = (f32[3,28,72,128]{3,2,1,0:T(8,128)S(1)}, f32[6,28,72,128]{3,2,1,0:T(8,128)S(1)}, f32[3,28,40,128]{3,2,1,0:T(8,128)S(1)}, f32[59,40,128]{2,1,0:T(8,128)S(1)}, f32[23,40,128]{2,1,0:T(8,128)S(1)}) custom-call(f32[12,6,8,128]{3,2,1,0:T(8,128)S(1)} %collective-permute-done.from_left, ...), custom_call_target="tpu_custom_call", output_to_operand_aliasing={{0}: (2, {}), {1}: (3, {}), {2}: (4, {})} | custom-call | tf_op jit(solution)/shard_map/pallas_call | solution.py:522
  24.7 1.9 %collective-permute-start.2 = (f32[59,40,128]{2,1,0:T(8,128)S(1)}, f32[59,40,128]{2,1,0:T(8,128)S(1)}, u32[]{:S(2)}, u32[]{:S(2)}) collective-permute-start(f32[59,40,128]{2,1,0:T(8,128)S(1)} %get-tuple-element.44), channel_id=1, source_target_pairs={{32,64},{64,32},{33,65},{65,33},{34,66},{66,34},{35,67},{67,35},{3... | collective-permute-start | bytes 3624968 | tf_op jit(solution)/shard_map/ppermute | solution.py:532
  26.6 0.1 collective-permute-start.3
  26.7 1.8 %collective-permute-done.3.refs_2_ = f32[23,40,128]{2,1,0:T(8,128)S(1)} collective-permute-done((f32[23,40,128]{2,1,0:T(8,128)S(1)}, f32[23,40,128]{2,1,0:T(8,128)S(1)}, u32[]{:S(2)}, u32[]{:S(2)}) %collective-permute-start.3) | collective-permute-done | bytes 471072 | tf_op jit(solution)/shard_map/ppermute | solution.py:531
  28.5 0.0 copy-done
  28.6 0.0 copy-done.1
  28.6 4.6 %shard_map.130 = (f32[3,28,72,128]{3,2,1,0:T(8,128)S(1)}, f32[6,28,72,128]{3,2,1,0:T(8,128)S(1)}, f32[3,28,40,128]{3,2,1,0:T(8,128)S(1)}, f32[21,40,128]{2,1,0:T(8,128)S(1)}) custom-call(bf16[2,4,256,128]{3,2,1,0:T(8,128)(2,1)S(1)} %copy-done, bf16[2,640,128]{2,1,0:T(8,128)(2,1)S(1)} %copy-done.1, ...), custom_call_target="tpu_custom_call", output_to_operand_aliasing={{0}: (3, {}), {1}: (4, {}), {2}: (5, {})} | custom-call | tf_op jit(solution)/shard_map/pallas_call | solution.py:533
  33.1 0.2 collective-permute-start.4
  33.3 1.7 %collective-permute-done.4.refs_2_ = f32[21,40,128]{2,1,0:T(8,128)S(1)} collective-permute-done((f32[21,40,128]{2,1,0:T(8,128)S(1)}, f32[21,40,128]{2,1,0:T(8,128)S(1)}, u32[]{:S(2)}, u32[]{:S(2)}) %collective-permute-start.4) | collective-permute-done | bytes 430112 | tf_op jit(solution)/shard_map/ppermute | solution.py:537
  35.0 2.7 %shard_map.131 = (f32[3,28,72,128]{3,2,1,0:T(8,128)S(1)}, f32[6,28,72,128]{3,2,1,0:T(8,128)S(1)}, f32[3,28,40,128]{3,2,1,0:T(8,128)S(1)}, f32[21,40,128]{2,1,0:T(8,128)S(1)}) custom-call(bf16[2,4,256,128]{3,2,1,0:T(8,128)(2,1)S(1)} %copy-done, bf16[2,640,128]{2,1,0:T(8,128)(2,1)S(1)} %copy-done.1, ...), custom_call_target="tpu_custom_call", output_to_operand_aliasing={{0}: (3, {}), {1}: (4, {}), {2}: (5, {})} | custom-call | tf_op jit(solution)/shard_map/pallas_call | solution.py:539
  37.7 6.4 %collective-permute-done.2.refs_2_ = f32[59,40,128]{2,1,0:T(8,128)S(1)} collective-permute-done((f32[59,40,128]{2,1,0:T(8,128)S(1)}, f32[59,40,128]{2,1,0:T(8,128)S(1)}, u32[]{:S(2)}, u32[]{:S(2)}) %collective-permute-start.2) | collective-permute-done | bytes 1208352 | tf_op jit(solution)/shard_map/ppermute | solution.py:532
  44.0 3.2 %shard_map.132 = (f32[3,28,72,128]{3,2,1,0:T(8,128)S(1)}, f32[6,28,72,128]{3,2,1,0:T(8,128)S(1)}, f32[3,28,40,128]{3,2,1,0:T(8,128)S(1)}, f32[48,40,128]{2,1,0:T(8,128)S(1)}) custom-call(bf16[2,4,256,128]{3,2,1,0:T(8,128)(2,1)S(1)} %copy-done, bf16[2,640,128]{2,1,0:T(8,128)(2,1)S(1)} %copy-done.1, ...), custom_call_target="tpu_custom_call", output_to_operand_aliasing={{0}: (3, {}), {1}: (4, {}), {2}: (5, {})} | custom-call | tf_op jit(solution)/shard_map/pallas_call | solution.py:543
  47.3 1.9 %collective-permute-start.5 = (f32[48,40,128]{2,1,0:T(8,128)S(1)}, f32[48,40,128]{2,1,0:T(8,128)S(1)}, u32[]{:S(2)}, u32[]{:S(2)}) collective-permute-start(f32[48,40,128]{2,1,0:T(8,128)S(1)} %get-tuple-element.56), channel_id=1, source_target_pairs={{32,64},{64,32},{33,65},{65,33},{34,66},{66,34},{35,67},{67,35},{3... | collective-permute-start | bytes 2949128 | tf_op jit(solution)/shard_map/ppermute | solution.py:532
  49.2 0.1 collective-permute-start.6
  49.3 1.8 %collective-permute-done.6.refs_2_ = f32[21,40,128]{2,1,0:T(8,128)S(1)} collective-permute-done((f32[21,40,128]{2,1,0:T(8,128)S(1)}, f32[21,40,128]{2,1,0:T(8,128)S(1)}, u32[]{:S(2)}, u32[]{:S(2)}) %collective-permute-start.6) | collective-permute-done | bytes 430112 | tf_op jit(solution)/shard_map/ppermute | solution.py:531
  51.1 3.2 %shard_map.133 = (f32[3,28,72,128]{3,2,1,0:T(8,128)S(1)}, f32[6,28,72,128]{3,2,1,0:T(8,128)S(1)}, f32[3,28,40,128]{3,2,1,0:T(8,128)S(1)}, f32[21,40,128]{2,1,0:T(8,128)S(1)}) custom-call(bf16[2,4,256,128]{3,2,1,0:T(8,128)(2,1)S(1)} %copy-done, bf16[2,640,128]{2,1,0:T(8,128)(2,1)S(1)} %copy-done.1, ...), custom_call_target="tpu_custom_call", output_to_operand_aliasing={{0}: (3, {}), {1}: (4, {}), {2}: (5, {})} | custom-call | tf_op jit(solution)/shard_map/pallas_call | solution.py:533
  54.3 0.4 collective-permute-start.7
  55.3 1.0 %collective-permute-done.7.refs_2_ = f32[21,40,128]{2,1,0:T(8,128)S(1)} collective-permute-done((f32[21,40,128]{2,1,0:T(8,128)S(1)}, f32[21,40,128]{2,1,0:T(8,128)S(1)}, u32[]{:S(2)}, u32[]{:S(2)}) %collective-permute-start.7) | collective-permute-done | bytes 430112 | tf_op jit(solution)/shard_map/ppermute | solution.py:537
  56.3 0.0 copy-start.6
  56.3 0.0 copy-start.8
  56.3 0.0 copy-start.9
  56.3 2.6 %shard_map.134 = (f32[3,28,72,128]{3,2,1,0:T(8,128)S(1)}, f32[6,28,72,128]{3,2,1,0:T(8,128)S(1)}, f32[3,28,40,128]{3,2,1,0:T(8,128)S(1)}) custom-call(bf16[2,4,256,128]{3,2,1,0:T(8,128)(2,1)S(1)} %copy-done, bf16[2,640,128]{2,1,0:T(8,128)(2,1)S(1)} %copy-done.1, ...), custom_call_target="tpu_custom_call", output_to_operand_aliasing={{0}: (3, {}), {1}: (4, {}), {2}: (5, {})} | custom-call | tf_op jit(solution)/shard_map/pallas_call | solution.py:548
  59.0 5.2 %collective-permute-done.5.refs_6_ = f32[48,40,128]{2,1,0:T(8,128)S(1)} collective-permute-done((f32[48,40,128]{2,1,0:T(8,128)S(1)}, f32[48,40,128]{2,1,0:T(8,128)S(1)}, u32[]{:S(2)}, u32[]{:S(2)}) %collective-permute-start.5) | collective-permute-done | bytes 983072 | tf_op jit(solution)/shard_map/ppermute | solution.py:532
  64.2 0.0 copy-done.6
  64.2 0.0 copy-done.8
  64.2 0.0 copy-done.9
  64.2 2.6 %shard_map.135 = (f32[3,28,72,128]{3,2,1,0:T(8,128)S(1)}, f32[6,28,72,128]{3,2,1,0:T(8,128)S(1)}, f32[3,28,40,128]{3,2,1,0:T(8,128)S(1)}, f32[8,128]{1,0:T(8,128)S(1)}) custom-call(s32[1]{0:T(128)S(6)} %copy.60.refs_0_, f32[3,32]{1,0:T(4,128)S(1)} %copy-done.6, f32[1,32]{1,0:T(1,128)S(1)} %bitcast.19, ...), custom_call_target="tpu_custom_call", output_to_operand_aliasing={{0}: (7, {}), {1}: (8, {}), {2}: (9, {})} | custom-call | tf_op jit(solution)/shard_map/pallas_call | solution.py:552
  66.8 6.7 %all-gather = f32[32,128]{1,0:T(8,128)S(1)} all-gather(f32[8,128]{1,0:T(8,128)S(1)} %get-tuple-element.69), channel_id=2, replica_groups=mesh['region'=4,'tile'=32] {'region'}, dimensions={0}, use_global_device_ids=true | all-gather | bytes 20480 | tf_op jit(solution)/shard_map/all_gather | solution.py:557
  73.5 3.2 %collective-permute-start.8 = (f32[4,8,128]{2,1,0:T(8,128)S(1)}, f32[4,8,128]{2,1,0:T(8,128)S(1)}, u32[]{:S(2)}, u32[]{:S(2)}) collective-permute-start(f32[4,8,128]{2,1,0:T(8,128)S(1)} %bitcast.16), channel_id=1, source_target_pairs={{0,1},{1,2},{2,3},{3,4},{4,5},{5,6},{6,7},{7,8},{8,9},{9,10},{10,1... | collective-permute-start | bytes 49160 | tf_op jit(solution)/shard_map/ppermute | solution.py:558
  76.7 5.7 %collective-permute-start.9 = (f32[4,8,128]{2,1,0:T(8,128)S(1)}, f32[4,8,128]{2,1,0:T(8,128)S(1)}, u32[]{:S(2)}, u32[]{:S(2)}) collective-permute-start(f32[4,8,128]{2,1,0:T(8,128)S(1)} %bitcast.17), channel_id=1, source_target_pairs={{1,0},{2,1},{3,2},{4,3},{5,4},{6,5},{7,6},{8,7},{9,8},{10,9},{11,1... | collective-permute-start | bytes 49160 | tf_op jit(solution)/shard_map/ppermute | solution.py:559
  83.0 0.0 copy-start.7
  83.0 0.0 copy-start.10
  83.0 2.8 %shard_map.136 = (f32[6,28,72,128]{3,2,1,0:T(8,128)S(1)}, f32[4608,128]{1,0:T(8,128)}) custom-call(bf16[2,4,256,128]{3,2,1,0:T(8,128)(2,1)S(1)} %copy-done, bf16[2,640,128]{2,1,0:T(8,128)(2,1)S(1)} %copy-done.1, f32[3,28,72,128]{3,2,1,0:T(8,128)S(1)} %get-tuple-element.68.v_ref, ...), custom_call_target="tpu_custom_call", output_to_operand_aliasing={{0}: (3, {})} | custom-call | tf_op jit(solution)/shard_map/pallas_call | solution.py:560
  85.8 0.0 collective-permute-done.8.before_ref
  85.8 0.0 collective-permute-done.9.after_ref
  85.8 0.0 copy-done.7
  85.8 0.0 copy-done.10
  85.9 2.3 %shard_map.137 = f32[4608,128]{1,0:T(8,128)} custom-call(s32[1,64]{1,0:T(1,128)S(1)} %copy-done.10, s32[1]{0:T(128)S(6)} %copy.61.count_ref, f32[3,32]{1,0:T(4,128)S(1)} %copy-done.7, f32[3,28,72,128]{3,2,1,0:T(8,128)S(1)} %get-tuple-element.68.v_ref, f32[4,8,128]{2,1,0:T(8,128)S(1)} %collective-permute-done.8.before_ref, ...), custom_call_target="tpu_custom_call", output_to_operand_aliasing={{}: (7, {})} | custom-call | tf_op jit(solution)/shard_map/pallas_call | solution.py:565
Async XLA Ops:
  0.0 13.7 %copy-start.2 = (f32[9,32,16,128]{3,2,1,0:T(8,128)S(1)}, f32[9,32,16,128]{3,2,1,0:T(8,128)}, u32[]{:S(2)}) copy-start(f32[9,32,16,128]{3,2,1,0:T(8,128)} %param.13) | copy-start | bytes 7077892
  0.0 13.7 %copy-start.3 = (f32[32,16,128]{2,1,0:T(8,128)S(1)}, f32[32,16,128]{2,1,0:T(8,128)}, u32[]{:S(2)}) copy-start(f32[32,16,128]{2,1,0:T(8,128)} %param.14) | copy-start | bytes 786436
  0.0 13.7 %copy-start.4 = (f32[32,16,128]{2,1,0:T(8,128)S(1)}, f32[32,16,128]{2,1,0:T(8,128)}, u32[]{:S(2)}) copy-start(f32[32,16,128]{2,1,0:T(8,128)} %param.15) | copy-start | bytes 786436
  0.0 13.7 %copy-start.5 = (f32[32,16,128]{2,1,0:T(8,128)S(1)}, f32[32,16,128]{2,1,0:T(8,128)}, u32[]{:S(2)}) copy-start(f32[32,16,128]{2,1,0:T(8,128)} %param.16) | copy-start | bytes 786436
  4.8 14.2 %collective-permute-start = (f32[12,6,8,128]{3,2,1,0:T(8,128)}, f32[12,6,8,128]{3,2,1,0:T(8,128)S(1)}, u32[]{:S(2)}, u32[]{:S(2)}) collective-permute-start(f32[12,6,8,128]{3,2,1,0:T(8,128)} %get-tuple-element.39), channel_id=1, source_target_pairs={{0,1},{1,2},{2,3},{3,4},{4,5},{5,6},{6,7},{7,8},{8,9},{9,10},{10,1... | collective-permute-start | bytes 884744 | tf_op jit(solution)/shard_map/ppermute | solution.py:519
  8.0 15.3 %collective-permute-start.1 = (f32[12,6,8,128]{3,2,1,0:T(8,128)}, f32[12,6,8,128]{3,2,1,0:T(8,128)S(1)}, u32[]{:S(2)}, u32[]{:S(2)}) collective-permute-start(f32[12,6,8,128]{3,2,1,0:T(8,128)} %get-tuple-element.40), channel_id=1, source_target_pairs={{1,0},{2,1},{3,2},{4,3},{5,4},{6,5},{7,6},{8,7},{9,8},{10,9},{11,1... | collective-permute-start | bytes 884744 | tf_op jit(solution)/shard_map/ppermute | solution.py:520
  23.3 5.2 %copy-start = (bf16[2,4,256,128]{3,2,1,0:T(8,128)(2,1)S(1)}, bf16[2,4,256,128]{3,2,1,0:T(8,128)(2,1)}, u32[]{:S(2)}) copy-start(bf16[2,4,256,128]{3,2,1,0:T(8,128)(2,1)} %constant.4.clone.refs_0_.refs_4_.own_ref) | copy-start | bytes 1572868
  23.3 5.2 %copy-start.1 = (bf16[2,640,128]{2,1,0:T(8,128)(2,1)S(1)}, bf16[2,640,128]{2,1,0:T(8,128)(2,1)}, u32[]{:S(2)}) copy-start(bf16[2,640,128]{2,1,0:T(8,128)(2,1)} %constant.5.clone.refs_1_.refs_5_.halo_ref) | copy-start | bytes 983044
  24.7 19.3 %collective-permute-start.2 = (f32[59,40,128]{2,1,0:T(8,128)S(1)}, f32[59,40,128]{2,1,0:T(8,128)S(1)}, u32[]{:S(2)}, u32[]{:S(2)}) collective-permute-start(f32[59,40,128]{2,1,0:T(8,128)S(1)} %get-tuple-element.44), channel_id=1, source_target_pairs={{32,64},{64,32},{33,65},{65,33},{34,66},{66,34},{35,67},{67,35},{3... | collective-permute-start | bytes 3624968 | tf_op jit(solution)/shard_map/ppermute | solution.py:532
  26.6 1.9 %collective-permute-start.3 = (f32[23,40,128]{2,1,0:T(8,128)S(1)}, f32[23,40,128]{2,1,0:T(8,128)S(1)}, u32[]{:S(2)}, u32[]{:S(2)}) collective-permute-start(f32[23,40,128]{2,1,0:T(8,128)S(1)} %get-tuple-element.45), channel_id=1, source_target_pairs={{0,32},{32,0},{64,96},{96,64},{1,33},{33,1},{65,97},{97,65},{2,34}... | collective-permute-start | bytes 1413128 | tf_op jit(solution)/shard_map/ppermute | solution.py:531
  33.1 1.9 %collective-permute-start.4 = (f32[21,40,128]{2,1,0:T(8,128)S(1)}, f32[21,40,128]{2,1,0:T(8,128)S(1)}, u32[]{:S(2)}, u32[]{:S(2)}) collective-permute-start(f32[21,40,128]{2,1,0:T(8,128)S(1)} %get-tuple-element.49), channel_id=1, source_target_pairs={{0,32},{32,0},{64,96},{96,64},{1,33},{33,1},{65,97},{97,65},{2,34}... | collective-permute-start | bytes 1290248 | tf_op jit(solution)/shard_map/ppermute | solution.py:537
  47.3 16.9 %collective-permute-start.5 = (f32[48,40,128]{2,1,0:T(8,128)S(1)}, f32[48,40,128]{2,1,0:T(8,128)S(1)}, u32[]{:S(2)}, u32[]{:S(2)}) collective-permute-start(f32[48,40,128]{2,1,0:T(8,128)S(1)} %get-tuple-element.56), channel_id=1, source_target_pairs={{32,64},{64,32},{33,65},{65,33},{34,66},{66,34},{35,67},{67,35},{3... | collective-permute-start | bytes 2949128 | tf_op jit(solution)/shard_map/ppermute | solution.py:532
  49.2 1.9 %collective-permute-start.6 = (f32[21,40,128]{2,1,0:T(8,128)S(1)}, f32[21,40,128]{2,1,0:T(8,128)S(1)}, u32[]{:S(2)}, u32[]{:S(2)}) collective-permute-start(f32[21,40,128]{2,1,0:T(8,128)S(1)} %get-tuple-element.57), channel_id=1, source_target_pairs={{0,32},{32,0},{64,96},{96,64},{1,33},{33,1},{65,97},{97,65},{2,34}... | collective-permute-start | bytes 1290248 | tf_op jit(solution)/shard_map/ppermute | solution.py:531
  54.3 2.0 %collective-permute-start.7 = (f32[21,40,128]{2,1,0:T(8,128)S(1)}, f32[21,40,128]{2,1,0:T(8,128)S(1)}, u32[]{:S(2)}, u32[]{:S(2)}) collective-permute-start(f32[21,40,128]{2,1,0:T(8,128)S(1)} %get-tuple-element.61), channel_id=1, source_target_pairs={{0,32},{32,0},{64,96},{96,64},{1,33},{33,1},{65,97},{97,65},{2,34}... | collective-permute-start | bytes 1290248 | tf_op jit(solution)/shard_map/ppermute | solution.py:537
  56.3 7.9 %copy-start.6 = (f32[3,32]{1,0:T(4,128)S(1)}, f32[3,32]{1,0:T(4,128)}, u32[]{:S(2)}) copy-start(f32[3,32]{1,0:T(4,128)} %refs_1_.6) | copy-start | bytes 1156
  56.3 7.9 %copy-start.8 = (f32[32]{0:T(128)S(1)}, f32[32]{0:T(128)}, u32[]{:S(2)}) copy-start(f32[32]{0:T(128)} %param.18) | copy-start | bytes 388
  56.3 7.9 %copy-start.9 = (s32[32]{0:T(128)S(1)}, s32[32]{0:T(128)}, u32[]{:S(2)}) copy-start(s32[32]{0:T(128)} %param.20) | copy-start | bytes 388
  73.5 12.3 %collective-permute-start.8 = (f32[4,8,128]{2,1,0:T(8,128)S(1)}, f32[4,8,128]{2,1,0:T(8,128)S(1)}, u32[]{:S(2)}, u32[]{:S(2)}) collective-permute-start(f32[4,8,128]{2,1,0:T(8,128)S(1)} %bitcast.16), channel_id=1, source_target_pairs={{0,1},{1,2},{2,3},{3,4},{4,5},{5,6},{6,7},{7,8},{8,9},{9,10},{10,1... | collective-permute-start | bytes 49160 | tf_op jit(solution)/shard_map/ppermute | solution.py:558
  76.7 9.1 %collective-permute-start.9 = (f32[4,8,128]{2,1,0:T(8,128)S(1)}, f32[4,8,128]{2,1,0:T(8,128)S(1)}, u32[]{:S(2)}, u32[]{:S(2)}) collective-permute-start(f32[4,8,128]{2,1,0:T(8,128)S(1)} %bitcast.17), channel_id=1, source_target_pairs={{1,0},{2,1},{3,2},{4,3},{5,4},{6,5},{7,6},{8,7},{9,8},{10,9},{11,1... | collective-permute-start | bytes 49160 | tf_op jit(solution)/shard_map/ppermute | solution.py:559
  83.0 2.8 %copy-start.7 = (f32[3,32]{1,0:T(4,128)S(1)}, f32[3,32]{1,0:T(4,128)}, u32[]{:S(2)}) copy-start(f32[3,32]{1,0:T(4,128)} %profile_ref.1) | copy-start | bytes 1156
  83.0 2.8 %copy-start.10 = (s32[1,64]{1,0:T(1,128)S(1)}, s32[1,64]{1,0:T(1,128)}, u32[]{:S(2)}) copy-start(s32[1,64]{1,0:T(1,128)} %influence_ref.1) | copy-start | bytes 772

commit v3 on v2

--- a/solution.py
+++ b/solution.py
@@ -241,15 +241,6 @@
 PIECES = pieces()
 
 
-def edge_pack(main):
-    lane = lanes(PACK)
-    out = pltpu.roll(main[0:8], HALF, 1)
-    for g in range(1, GROUPS):
-        rolled = pltpu.roll(main[8 * g:8 * g + 8], (HALF + 32 * g) % 128, 1)
-        out = jnp.where(lane >= 32 * g, rolled, out)
-    return out
-
-
 def fetch(refs, buf_ref, sems):
     size = NZ * CX
     waits = []
@@ -261,23 +252,65 @@
     return waits
 
 
-def edge_kernel(fields_ref, buoy_ref, lame_ref, mu_ref, right_ref, left_ref, buf_ref, sems):
+def low_side(first):
+    odd = lax.rem(lax.axis_index("tile"), 2) > 0
+    return jnp.where(odd, HALF - WIDE, HALF) if first else jnp.where(odd, HALF, HALF - WIDE)
+
+
+def pack_units(units, at, put):
+    spot = lanes(PACK) % 32
+    parts = [None] * 3
+    for u, v, start, lo, hi in PIECES:
+        keep = (spot >= lo) & (spot < hi)
+        moved = pltpu.roll(units[u], lax.rem(start - at + 256, 128), 1)
+        parts[v] = moved if parts[v] is None else jnp.where(keep, moved, parts[v])
+    for v in range(3):
+        put(v, parts[v])
+
+
+def edge_kernel(fields_ref, buoy_ref, lame_ref, mu_ref, first_ref, second_ref, buf_ref, sems):
     size = NZ * CX
-    spot = lanes(PACK) % 32
+    lane = lanes(PACK)
     for a, copy in enumerate(fetch((fields_ref, buoy_ref, lame_ref, mu_ref), buf_ref, sems)):
         copy.wait()
         for block in range(2):
-            rights, lefts = [None] * 3, [None] * 3
-            edges = [edge_pack(buf_ref[pl.ds(a * size + 8 * block + u, NZ, stride=CX), :])
-                     for u in range(8)]
-            for u, v, start, lo, hi in PIECES:
-                keep = (spot >= lo) & (spot < hi)
-                for parts, at in ((rights, HALF - WIDE), (lefts, HALF)):
-                    moved = pltpu.roll(edges[u], (start - at) % 128, 1)
-                    parts[v] = moved if parts[v] is None else jnp.where(keep, moved, parts[v])
-            for v in range(3):
-                right_ref[a, 3 * block + v] = rights[v]
-                left_ref[a, 3 * block + v] = lefts[v]
+            units = []
+            for u in range(8):
+                out = None
+                for g in range(GROUPS):
+                    row = a * size + (8 * g + u) * CX + 8 * block
+                    moved = pltpu.roll(buf_ref[row:row + 8, :], (HALF + 32 * g) % 128, 1)
+                    out = moved if g == 0 else jnp.where(lane >= 32 * g, moved, out)
+                units.append(out)
+            for ref, is_first in ((first_ref, True), (second_ref, False)):
+                def put(v, value):
+                    ref[a, 3 * block + v] = value
+                pack_units(units, 2 * HALF - WIDE - low_side(is_first), put)
+
+
+def unpack_units(got_ref, a, block, at, under, put):
+    spot = lanes(PACK) % 32
+    for u in range(8):
+        value = under(u)
+        for w, v, start, lo, hi in PIECES:
+            if w == u:
+                keep = (spot >= lo - start + at) & (spot < hi - start + at)
+                moved = pltpu.roll(got_ref[a, 3 * block + v], lax.rem(at - start + 256, 128), 1)
+                value = jnp.where(keep, moved, value)
+        put(u, value)
+
+
+def first_halo_kernel(got_ref, half_ref):
+    at = low_side(True)
+
+    def body(a, _):
+        for block in range(2):
+            def put(u, value):
+                half_ref[a, block, u] = value
+            unpack_units(got_ref, a, block, at, lambda u: jnp.zeros((PACK, 128), jnp.float32), put)
+        return 0
+
+    lax.fori_loop(0, 12, body, 0)
 
 
 def build_kernel(fields_ref, buoy_ref, lame_ref, mu_ref, v_ref, t_ref, p_ref):
@@ -292,56 +325,38 @@
 
     lax.fori_loop(0, PLANES, clear, 0)
     for a in range(12):
+        ref, first = (fields_ref, a * size) if a < 9 else ((buoy_ref, lame_ref, mu_ref)[a - 9], 0)
         for x in range(CX):
+            value = ref[pl.ds(first + x, NZ, stride=CX), :]
             if a < 3:
-                v_ref[a, x + LOW, 8:8 + NZ, :] = fields_ref[pl.ds(a * size + x, NZ, stride=CX), :]
+                v_ref[a, x + LOW, 8:8 + NZ, :] = value
             elif a < 9:
-                t_ref[a - 3, x + LOW, 8:8 + NZ, :] = fields_ref[pl.ds(a * size + x, NZ, stride=CX), :]
+                t_ref[a - 3, x + LOW, 8:8 + NZ, :] = value
             else:
-                ref = (buoy_ref, lame_ref, mu_ref)[a - 9]
-                p_ref[a - 9, x + LOW, 0:NZ, :] = DT * ref[pl.ds(x, NZ, stride=CX), :]
-
-
-def halo_kernel(from_left, from_right, v_in, t_in, p_in, v_ref, t_ref, p_ref, outer_ref,
-                inner_ref):
+                p_ref[a - 9, x + LOW, 0:NZ, :] = DT * value
+
+
+def halo_kernel(got_ref, half_ref, v_in, t_in, p_in, v_ref, t_ref, p_ref, outer_ref, inner_ref):
     odd = is_odd()
-    spot = lanes(PACK) % 32
-
-    def one(a, put):
+    at = low_side(False)
+    v_rows = v_ref.reshape(3 * PLANES * ZROWS, 128)
+    t_rows = t_ref.reshape(6 * PLANES * ZROWS, 128)
+    p_rows = p_ref.reshape(3 * PLANES * DEPTH, 128)
+
+    def one(a, f, rows_ref, depth, begin, scale):
         for block in range(2):
-            for u in range(8):
-                value = jnp.zeros((PACK, 128), jnp.float32)
-                for w, v, start, lo, hi in PIECES:
-                    if w != u:
-                        continue
-                    for ref, at in ((from_left, HALF - WIDE), (from_right, HALF)):
-                        keep = (spot >= lo - start + at) & (spot < hi - start + at)
-                        moved = pltpu.roll(ref[a, 3 * block + v], (at - start) % 128, 1)
-                        value = jnp.where(keep, moved, value)
-                put(8 * block + u + LOW, value)
-
-    def to_v(f, _):
-        def put(x, value):
-            v_ref[f, x, 56:64, :] = value
-        one(f, put)
-        return 0
-
-    def to_t(f, _):
-        def put(x, value):
-            t_ref[f, x, 56:64, :] = value
-        one(f + 3, put)
-        return 0
-
-    def to_p(f, _):
-        def put(x, value):
-            p_ref[f, x, NZ:DEPTH, :] = DT * value
-        one(f + 9, put)
-        return 0
-
-    lax.fori_loop(0, 3, to_v, 0)
-    lax.fori_loop(0, 6, to_t, 0)
-    lax.fori_loop(0, 3, to_p, 0)
-
+            def put(u, value):
+                row = (f * PLANES + LOW + 8 * block) * depth + begin + u
+                rows_ref[pl.ds(row, 8, stride=depth), :] = scale * value if scale else value
+            unpack_units(got_ref, a, block, at, lambda u: half_ref[a, block, u], put)
+
+    for a in range(12):
+        if a < 3:
+            one(a, a, v_rows, ZROWS, 56, None)
+        elif a < 9:
+            one(a, a - 3, t_rows, ZROWS, 56, None)
+        else:
+            one(a, a - 9, p_rows, DEPTH, NZ, DT)
     give_halo(OUTER_FIRST, odd, False, outer_ref, v_ref, t_ref, p_ref)
     give_halo(INNER_FIRST, odd, True, inner_ref, v_ref, t_ref, p_ref)
 
@@ -419,8 +434,29 @@
     packet_ref[...] = pltpu.roll(own, region * S, 1)
 
 
-def stress_out_kernel(own_ref, halo_ref, v_ref, t_in, p_ref, t_ref, out_ref, d_ref,
-                      rows_ref, sem):
+def tile_column(packet_refs, used, cell_x, cell_y):
+    packet = packet_refs[0] + packet_refs[1] + packet_refs[2] + packet_refs[3]
+    dist_x = cell_x - packet[3:4]
+    dist_y = cell_y - packet[4:5]
+    along_x = jnp.exp(-(dist_x * dist_x) / (2.0 * (0.5 * CX) ** 2))
+    along_y = jnp.exp(-(dist_y * dist_y) / (2.0 * (0.25 * CY) ** 2))
+    scaled = jnp.concatenate(
+        [jnp.where(used > 0, packet[c:c + 1] * along_x, 0.0) for c in range(3)], axis=0)
+    return lax.dot_general(
+        scaled, along_y, (((1,), (1,)), ((), ())), precision=lax.Precision.HIGHEST,
+        preferred_element_type=jnp.float32)
+
+
+def cell_places():
+    region, tile = lax.axis_index("region"), lax.axis_index("tile")
+    cell_x = (lax.broadcasted_iota(jnp.int32, (CX, 128), 0) + region * CX).astype(jnp.float32)
+    cell_y = (lax.broadcasted_iota(jnp.int32, (CY, 128), 0) + tile * CY).astype(jnp.float32)
+    return cell_x, cell_y
+
+
+def stress_out_kernel(influence_ref, count_ref, profile_ref, own_ref, halo_ref, here_ref, v_ref,
+                      t_in, p_ref, t_ref, out_ref, used_ref, profile_rows, own_part, d_ref, rows_ref,
+                      sem):
     odd = is_odd()
     stress_pass(v_ref, t_ref, p_ref, own_ref, halo_ref, d_ref, jnp.where(odd, 10, 0), 6, pads=False)
     size = NZ * CX
@@ -433,38 +469,30 @@
     lax.fori_loop(0, CX, body, 0)
     copy = pltpu.make_async_copy(rows_ref, out_ref.at[pl.ds(3 * size, 6 * size)], sem)
     copy.start()
-    copy.wait()
-
-
-def increment_kernel(influence_ref, count_ref, profile_ref, v_ref, before_ref, here_ref,
-                     after_ref, out_in, out_ref, profile_rows, rows_ref, sem):
-    region, tile = lax.axis_index("region"), lax.axis_index("tile")
     lane = lanes(8)
-    column = lax.broadcasted_iota(jnp.int32, (8, 128), 0) + tile - 1
+    column = lax.broadcasted_iota(jnp.int32, (8, 128), 0) + lax.axis_index("tile") - 1
     slot_id = (lane // S * 32 + column) * S + lane % S
     slot_id = jnp.where((column >= 0) & (column < 32), slot_id, -1)
     used = jnp.zeros((8, 128), jnp.int32)
     for k in range(LIST):
         hit = (slot_id == influence_ref[0, k]) & (k < count_ref[0])
         used = jnp.where(hit, 1, used)
-    cell_x = (lax.broadcasted_iota(jnp.int32, (CX, 128), 0) + region * CX).astype(jnp.float32)
-    cell_y = (lax.broadcasted_iota(jnp.int32, (CY, 128), 0) + tile * CY).astype(jnp.float32)
-    increment = jnp.zeros((3 * CX, CY), jnp.float32)
-    for d, ref in enumerate((before_ref, here_ref, after_ref)):
-        packet = ref[0] + ref[1] + ref[2] + ref[3]
-        dist_x = cell_x - packet[3:4]
-        dist_y = cell_y - packet[4:5]
-        along_x = jnp.exp(-(dist_x * dist_x) / (2.0 * (0.5 * CX) ** 2))
-        along_y = jnp.exp(-(dist_y * dist_y) / (2.0 * (0.25 * CY) ** 2))
-        keep = used[d:d + 1] > 0
-        scaled = jnp.concatenate(
-            [jnp.where(keep, packet[c:c + 1] * along_x, 0.0) for c in range(3)], axis=0)
-        increment += lax.dot_general(
-            scaled, along_y, (((1,), (1,)), ((), ())), precision=lax.Precision.HIGHEST,
-            preferred_element_type=jnp.float32)
+    used_ref[...] = used
     for c in range(3):
         for z in range(NZ):
             profile_rows[c, z:z + 1, :] = jnp.full((1, 128), profile_ref[c, z], jnp.float32)
+    own_part[...] = tile_column(here_ref, used[1:2], *cell_places())
+    copy.wait()
+
+
+def increment_kernel(v_ref, first_ref, second_ref, used_ref, profile_rows, own_part, out_in, out_ref,
+                     rows_ref, sem):
+    odd = lax.rem(lax.axis_index("tile"), 2) > 0
+    before = [jnp.where(odd, first_ref[r], second_ref[r]) for r in range(4)]
+    after = [jnp.where(odd, second_ref[r], first_ref[r]) for r in range(4)]
+    places = cell_places()
+    increment = (own_part[...] + tile_column(before, used_ref[0:1], *places)
+                 + tile_column(after, used_ref[2:3], *places))
     for c in range(3):
         for r in range(CX):
             value = v_ref[c, r + LOW, 8:8 + NZ, :]
@@ -489,6 +517,10 @@
         kernel, out_shape=outs, in_specs=specs, out_specs=out_specs or [VM] * len(outs),
         scratch_shapes=list(scratch), input_output_aliases=aliases or {},
         compiler_params=pltpu.CompilerParams(vmem_limit_bytes=vmem))
+
+
+def pairs(first):
+    return [p for i in range(first, 31, 2) for p in ((i, i + 1), (i + 1, i))]
 
 
 INNER_SWAP = [(0, 1), (1, 0), (2, 3), (3, 2)]
@@ -511,19 +543,18 @@
     given = (fields.reshape(9 * size, CY), buoyancy.reshape(size, CY),
              lame_first.reshape(size, CY), shear_modulus.reshape(size, CY))
     fetched = [pltpu.VMEM((12 * size, 128), jnp.float32), pltpu.SemaphoreType.DMA((12,))]
-    right, left = call(edge_kernel, (struct(12, 6, PACK, 128),) * 2, [HB] * 4, fetched,
-                       vmem=60 * 2 ** 20)(*given)
-    count = lax.axis_size("tile")
-    forward = [(i, i + 1) for i in range(count - 1)]
-    backward = [(b, a) for a, b in forward]
-    from_left = lax.ppermute(right, "tile", forward)
-    from_right = lax.ppermute(left, "tile", backward)
+    packed, edges = struct(12, 6, PACK, 128), struct(12, 2, 8, 8, 128)
+    first, second = call(edge_kernel, (packed, packed), [HB] * 4, fetched,
+                         vmem=62 * 2 ** 20)(*given)
+    got_first = lax.ppermute(first, "tile", pairs(0))
+    got_second = lax.ppermute(second, "tile", pairs(1))
     v, t, p = call(build_kernel, state, [VM] * 4, [])(*given)
+    half, = call(first_halo_kernel, (edges,), [VM], [])(got_first)
     v, t, p, outer, inner = call(
         halo_kernel, state + (struct(plane_count(OUTER_FIRST), DEPTH, 128),
                               struct(plane_count(INNER_FIRST), DEPTH, 128)),
         [VM] * 5, [], aliases={2: 0, 3: 1, 4: 2},
-    )(from_left, from_right, v, t, p)
+    )(got_second, half, v, t, p)
     inner_struct = struct(plane_count(INNER), DEPTH, 128)
     d_scratch = pltpu.VMEM((3, CX, DEPTH, 128), jnp.float32)
     alias = {3: 0, 4: 1, 5: 2}
@@ -555,18 +586,20 @@
     )(station_count, observed, station_weight.reshape(1, S), station_cell.reshape(1, S),
       own, edge, got_outer, v, t, p)
     here = lax.all_gather(packet, "region")
-    before = lax.ppermute(here, "tile", forward)
-    after = lax.ppermute(here, "tile", backward)
-    _, out = call(
-        stress_out_kernel, (state[1], struct(9 * size, 128)), [VM] * 5,
+    got_first = lax.ppermute(here, "tile", pairs(0))
+    got_second = lax.ppermute(here, "tile", pairs(1))
+    _, out, used, profile_rows, own_part = call(
+        stress_out_kernel,
+        (state[1], struct(9 * size, 128), jax.ShapeDtypeStruct((8, 128), jnp.int32),
+         struct(3, NZ, 128), struct(3 * CX, CY)), [SM] * 3 + [VM] * 6,
         [d_scratch, pltpu.VMEM((6 * size, 128), jnp.float32), pltpu.SemaphoreType.DMA],
-        out_specs=[VM, HB], aliases={3: 0},
-    )(own, edge, v, t, p)
+        out_specs=[VM, HB, VM, VM, VM], aliases={7: 0},
+    )(influence, influence_count, depth_profile, own, edge, here, v, t, p)
     out, = call(
-        increment_kernel, (struct(9 * size, 128),), [SM] * 3 + [VM] * 4 + [HB],
-        [pltpu.VMEM((3, NZ, 128), jnp.float32), pltpu.VMEM((3 * size, 128), jnp.float32),
-         pltpu.SemaphoreType.DMA], out_specs=[HB], aliases={7: 0},
-    )(influence, influence_count, depth_profile, v, before, here, after, out)
+        increment_kernel, (struct(9 * size, 128),), [VM] * 6 + [HB],
+        [pltpu.VMEM((3 * size, 128), jnp.float32), pltpu.SemaphoreType.DMA], out_specs=[HB],
+        aliases={6: 0},
+    )(v, got_first, got_second, used, profile_rows, own_part, out)
     return out.reshape(9, NZ, CX, CY)
 
 

time: 88.6 us -> 84.1 us (0.949)
  waiting for transfers between devices: 26.3 us -> 21.2 us
  local copies, waits for them, and re-layouts: 0.05 us -> 1.7 us
  starting transfers between devices: 22.3 us -> 21.4 us
    ppermute x4, waiting for transfers between devices: 8.46 us -> 3.34 us  [the longest x1 3.33 us: per_device(): got_second = lax.ppermute(second, 'tile', pairs(1))]
    unnamed x22, local copies, waits for them, and re-layouts: 0.05 us -> 1.7 us
    pallas_call x1, Pallas kernels: 1.37 us -> 0.37 us  [per_device(): call(halo_kernel, state + (struct(plane_count(OUTER_FIRST), DEPTH, 128),...]
    pallas_call x3 -> x4, Pallas kernels: 9.83 us -> 10.8 us  [the longest x1 4.6 us: per_device(): call(edge_kernel, (packed, packed), [HB] * 4, fetched, vmem=62 * 2 ** 20)]
  transfers between devices with their start and end apart: 10 -> 10, of which waited for: 8 -> 7; matrix products, arithmetic and copies ran while one was open for 0% -> 0% of each run, Pallas kernels for 19% -> 22%
where the time goes in v3:
time: 84.1 us; the launch traced here: 83.8 us
  Pallas kernels  31.2 us (37%)
  starting transfers between devices  21.4 us (25%)
  waiting for transfers between devices  21.2 us (25%)
  blocking collectives  6.68 us (8%)
  local copies, waits for them, and re-layouts  1.7 us (2%)
  between operations  1.68 us (2%)
    ppermute x2, waiting for transfers between devices, per_device(): got_outer = lax.ppermute(outer, 'region', OUTER_SWAP)  11.6 us
    pallas_call x2, Pallas kernels, per_device(): call(bind(near_kernel, INNER_FIRST if block == 0 else INNER, 0, True), st...  7.78 us
    all_gather x1, blocking collectives, per_device(): here = lax.all_gather(packet, 'region')  6.68 us
    ppermute x1, starting transfers between devices, per_device(): got_second = lax.ppermute(second, 'tile', pairs(1))  6.38 us
    ppermute x4, waiting for transfers between devices, per_device(): got = lax.ppermute(inner, 'region', INNER_SWAP)  6.31 us
    ppermute x1, starting transfers between devices, per_device(): got_second = lax.ppermute(here, 'tile', pairs(1))  6.15 us
    pallas_call x1, Pallas kernels, per_device(): call(edge_kernel, (packed, packed), [HB] * 4, fetched, vmem=62 * 2 ** 20)  4.6 us
    ppermute x2, starting transfers between devices, per_device(): got_outer = lax.ppermute(outer, 'region', OUTER_SWAP)  3.84 us
  transfers between devices with their start and end apart: 10, of which 7 were waited for; matrix products, arithmetic and copies ran while one was open for 0% of the time, Pallas kernels for 22%

profile of v3, /device:TPU:22, one launch (start us, length us, event | category | flops | bytes accessed | tf_op | source)
XLA Modules:
  0.0 83.8 jit_solution(4680221656263500101)
XLA Ops:
  0.0 0.0 copy-start.3
  0.0 0.0 copy-start.4
  0.0 0.0 copy-start.5
  0.0 4.6 %shard_map.127 = (f32[12,6,8,128]{3,2,1,0:T(8,128)}, f32[12,6,8,128]{3,2,1,0:T(8,128)}) custom-call(f32[4608,128]{1,0:T(8,128)} %bitcast.8, f32[512,128]{1,0:T(8,128)} %bitcast.10, f32[512,128]{1,0:T(8,128)} %bitcast.12, f32[512,128]{1,0:T(8,128)} %bitcast.14), custom_call_target="tpu_custom_call" | custom-call | tf_op jit(solution)/shard_map/pallas_call | solution.py:547
  4.6 1.4 %collective-permute-start.1 = (f32[12,6,8,128]{3,2,1,0:T(8,128)}, f32[12,6,8,128]{3,2,1,0:T(8,128)S(1)}, u32[]{:S(2)}, u32[]{:S(2)}) collective-permute-start(f32[12,6,8,128]{3,2,1,0:T(8,128)} %get-tuple-element.43), channel_id=1, source_target_pairs={{0,1},{1,0},{2,3},{3,2},{4,5},{5,4},{6,7},{7,6},{8,9},{9,8},{10,11... | collective-permute-start | bytes 884744 | tf_op jit(solution)/shard_map/ppermute | solution.py:549
  6.0 6.4 %collective-permute-start = (f32[12,6,8,128]{3,2,1,0:T(8,128)}, f32[12,6,8,128]{3,2,1,0:T(8,128)S(1)}, u32[]{:S(2)}, u32[]{:S(2)}) collective-permute-start(f32[12,6,8,128]{3,2,1,0:T(8,128)} %get-tuple-element.42), channel_id=1, source_target_pairs={{1,2},{2,1},{3,4},{4,3},{5,6},{6,5},{7,8},{8,7},{9,10},{10,9},{11,... | collective-permute-start | bytes 884744 | tf_op jit(solution)/shard_map/ppermute | solution.py:550
  12.4 0.0 copy-done.3
  12.4 0.0 copy-done.4
  12.4 0.0 copy-done.5
  12.4 0.0 copy-start.2
  12.4 1.7 %copy-done.2 = f32[9,32,16,128]{3,2,1,0:T(8,128)S(1)} copy-done((f32[9,32,16,128]{3,2,1,0:T(8,128)S(1)}, f32[9,32,16,128]{3,2,1,0:T(8,128)}, u32[]{:S(2)}) %copy-start.2) | copy-done | bytes 2359320
  14.1 1.1 %shard_map.129 = (f32[3,28,72,128]{3,2,1,0:T(8,128)S(1)}, f32[6,28,72,128]{3,2,1,0:T(8,128)S(1)}, f32[3,28,40,128]{3,2,1,0:T(8,128)S(1)}) custom-call(f32[4608,128]{1,0:T(8,128)S(1)} %bitcast.9, f32[512,128]{1,0:T(8,128)S(1)} %bitcast.11, f32[512,128]{1,0:T(8,128)S(1)} %bitcast.13, f32[512,128]{1,0:T(8,128)S(1)} %bitcast.15), custom_call_target="tpu_custom_call" | custom-call | tf_op jit(solution)/shard_map/pallas_call | solution.py:551
  15.2 0.0 collective-permute-done.1.got_ref
  15.2 1.1 %shard_map.128.half_ref = f32[12,2,8,8,128]{4,3,2,1,0:T(8,128)S(1)} custom-call(f32[12,6,8,128]{3,2,1,0:T(8,128)S(1)} %collective-permute-done.1.got_ref), custom_call_target="tpu_custom_call" | custom-call | tf_op jit(solution)/shard_map/pallas_call | solution.py:552
  16.3 3.3 %collective-permute-done.got_ref = f32[12,6,8,128]{3,2,1,0:T(8,128)S(1)} collective-permute-done((f32[12,6,8,128]{3,2,1,0:T(8,128)}, f32[12,6,8,128]{3,2,1,0:T(8,128)S(1)}, u32[]{:S(2)}, u32[]{:S(2)}) %collective-permute-start) | collective-permute-done | bytes 294944 | tf_op jit(solution)/shard_map/ppermute | solution.py:550
  19.7 0.0 copy-start
  19.7 0.0 copy-start.1
  19.7 0.4 shard_map.130
  20.0 1.9 %collective-permute-start.2 = (f32[59,40,128]{2,1,0:T(8,128)S(1)}, f32[59,40,128]{2,1,0:T(8,128)S(1)}, u32[]{:S(2)}, u32[]{:S(2)}) collective-permute-start(f32[59,40,128]{2,1,0:T(8,128)S(1)} %get-tuple-element.47), channel_id=1, source_target_pairs={{32,64},{64,32},{33,65},{65,33},{34,66},{66,34},{35,67},{67,35},{3... | collective-permute-start | bytes 3624968 | tf_op jit(solution)/shard_map/ppermute | solution.py:563
  22.0 0.1 collective-permute-start.3
  22.1 1.8 %collective-permute-done.3.refs_2_ = f32[23,40,128]{2,1,0:T(8,128)S(1)} collective-permute-done((f32[23,40,128]{2,1,0:T(8,128)S(1)}, f32[23,40,128]{2,1,0:T(8,128)S(1)}, u32[]{:S(2)}, u32[]{:S(2)}) %collective-permute-start.3) | collective-permute-done | bytes 471072 | tf_op jit(solution)/shard_map/ppermute | solution.py:562
  23.9 0.0 copy-done
  23.9 0.0 copy-done.1
  23.9 4.5 %shard_map.131 = (f32[3,28,72,128]{3,2,1,0:T(8,128)S(1)}, f32[6,28,72,128]{3,2,1,0:T(8,128)S(1)}, f32[3,28,40,128]{3,2,1,0:T(8,128)S(1)}, f32[21,40,128]{2,1,0:T(8,128)S(1)}) custom-call(bf16[2,4,256,128]{3,2,1,0:T(8,128)(2,1)S(1)} %copy-done, bf16[2,640,128]{2,1,0:T(8,128)(2,1)S(1)} %copy-done.1, ...), custom_call_target="tpu_custom_call", output_to_operand_aliasing={{0}: (3, {}), {1}: (4, {}), {2}: (5, {})} | custom-call | tf_op jit(solution)/shard_map/pallas_call | solution.py:564
  28.4 0.2 collective-permute-start.4
  28.6 1.7 %collective-permute-done.4.refs_2_ = f32[21,40,128]{2,1,0:T(8,128)S(1)} collective-permute-done((f32[21,40,128]{2,1,0:T(8,128)S(1)}, f32[21,40,128]{2,1,0:T(8,128)S(1)}, u32[]{:S(2)}, u32[]{:S(2)}) %collective-permute-start.4) | collective-permute-done | bytes 430112 | tf_op jit(solution)/shard_map/ppermute | solution.py:568
  30.3 2.7 %shard_map.132 = (f32[3,28,72,128]{3,2,1,0:T(8,128)S(1)}, f32[6,28,72,128]{3,2,1,0:T(8,128)S(1)}, f32[3,28,40,128]{3,2,1,0:T(8,128)S(1)}, f32[21,40,128]{2,1,0:T(8,128)S(1)}) custom-call(bf16[2,4,256,128]{3,2,1,0:T(8,128)(2,1)S(1)} %copy-done, bf16[2,640,128]{2,1,0:T(8,128)(2,1)S(1)} %copy-done.1, ...), custom_call_target="tpu_custom_call", output_to_operand_aliasing={{0}: (3, {}), {1}: (4, {}), {2}: (5, {})} | custom-call | tf_op jit(solution)/shard_map/pallas_call | solution.py:570
  33.0 6.4 %collective-permute-done.2.refs_2_ = f32[59,40,128]{2,1,0:T(8,128)S(1)} collective-permute-done((f32[59,40,128]{2,1,0:T(8,128)S(1)}, f32[59,40,128]{2,1,0:T(8,128)S(1)}, u32[]{:S(2)}, u32[]{:S(2)}) %collective-permute-start.2) | collective-permute-done | bytes 1208352 | tf_op jit(solution)/shard_map/ppermute | solution.py:563
  39.4 3.2 %shard_map.133 = (f32[3,28,72,128]{3,2,1,0:T(8,128)S(1)}, f32[6,28,72,128]{3,2,1,0:T(8,128)S(1)}, f32[3,28,40,128]{3,2,1,0:T(8,128)S(1)}, f32[48,40,128]{2,1,0:T(8,128)S(1)}) custom-call(bf16[2,4,256,128]{3,2,1,0:T(8,128)(2,1)S(1)} %copy-done, bf16[2,640,128]{2,1,0:T(8,128)(2,1)S(1)} %copy-done.1, ...), custom_call_target="tpu_custom_call", output_to_operand_aliasing={{0}: (3, {}), {1}: (4, {}), {2}: (5, {})} | custom-call | tf_op jit(solution)/shard_map/pallas_call | solution.py:574
  42.6 1.9 %collective-permute-start.5 = (f32[48,40,128]{2,1,0:T(8,128)S(1)}, f32[48,40,128]{2,1,0:T(8,128)S(1)}, u32[]{:S(2)}, u32[]{:S(2)}) collective-permute-start(f32[48,40,128]{2,1,0:T(8,128)S(1)} %get-tuple-element.59), channel_id=1, source_target_pairs={{32,64},{64,32},{33,65},{65,33},{34,66},{66,34},{35,67},{67,35},{3... | collective-permute-start | bytes 2949128 | tf_op jit(solution)/shard_map/ppermute | solution.py:563
  44.5 0.3 collective-permute-start.6
  44.8 1.8 %collective-permute-done.6.refs_2_ = f32[21,40,128]{2,1,0:T(8,128)S(1)} collective-permute-done((f32[21,40,128]{2,1,0:T(8,128)S(1)}, f32[21,40,128]{2,1,0:T(8,128)S(1)}, u32[]{:S(2)}, u32[]{:S(2)}) %collective-permute-start.6) | collective-permute-done | bytes 430112 | tf_op jit(solution)/shard_map/ppermute | solution.py:562
  46.5 3.2 %shard_map.134 = (f32[3,28,72,128]{3,2,1,0:T(8,128)S(1)}, f32[6,28,72,128]{3,2,1,0:T(8,128)S(1)}, f32[3,28,40,128]{3,2,1,0:T(8,128)S(1)}, f32[21,40,128]{2,1,0:T(8,128)S(1)}) custom-call(bf16[2,4,256,128]{3,2,1,0:T(8,128)(2,1)S(1)} %copy-done, bf16[2,640,128]{2,1,0:T(8,128)(2,1)S(1)} %copy-done.1, ...), custom_call_target="tpu_custom_call", output_to_operand_aliasing={{0}: (3, {}), {1}: (4, {}), {2}: (5, {})} | custom-call | tf_op jit(solution)/shard_map/pallas_call | solution.py:564
  49.8 0.2 collective-permute-start.7
  50.6 1.1 %collective-permute-done.7.refs_2_ = f32[21,40,128]{2,1,0:T(8,128)S(1)} collective-permute-done((f32[21,40,128]{2,1,0:T(8,128)S(1)}, f32[21,40,128]{2,1,0:T(8,128)S(1)}, u32[]{:S(2)}, u32[]{:S(2)}) %collective-permute-start.7) | collective-permute-done | bytes 430112 | tf_op jit(solution)/shard_map/ppermute | solution.py:568
  51.6 0.0 copy-start.6
  51.6 0.0 copy-start.8
  51.6 0.0 copy-start.9
  51.6 2.7 %shard_map.135 = (f32[3,28,72,128]{3,2,1,0:T(8,128)S(1)}, f32[6,28,72,128]{3,2,1,0:T(8,128)S(1)}, f32[3,28,40,128]{3,2,1,0:T(8,128)S(1)}) custom-call(bf16[2,4,256,128]{3,2,1,0:T(8,128)(2,1)S(1)} %copy-done, bf16[2,640,128]{2,1,0:T(8,128)(2,1)S(1)} %copy-done.1, ...), custom_call_target="tpu_custom_call", output_to_operand_aliasing={{0}: (3, {}), {1}: (4, {}), {2}: (5, {})} | custom-call | tf_op jit(solution)/shard_map/pallas_call | solution.py:579
  54.3 5.2 %collective-permute-done.5.refs_6_ = f32[48,40,128]{2,1,0:T(8,128)S(1)} collective-permute-done((f32[48,40,128]{2,1,0:T(8,128)S(1)}, f32[48,40,128]{2,1,0:T(8,128)S(1)}, u32[]{:S(2)}, u32[]{:S(2)}) %collective-permute-start.5) | collective-permute-done | bytes 983072 | tf_op jit(solution)/shard_map/ppermute | solution.py:563
  59.5 0.0 copy-done.6
  59.5 0.0 copy-done.8
  59.5 0.0 copy-done.9
  59.5 0.0 copy-start.7
  59.5 0.0 copy-start.10
  59.5 2.6 %shard_map.136 = (f32[3,28,72,128]{3,2,1,0:T(8,128)S(1)}, f32[6,28,72,128]{3,2,1,0:T(8,128)S(1)}, f32[3,28,40,128]{3,2,1,0:T(8,128)S(1)}, f32[8,128]{1,0:T(8,128)S(1)}) custom-call(s32[1]{0:T(128)S(6)} %copy.60.refs_0_, f32[3,32]{1,0:T(4,128)S(1)} %copy-done.6, f32[1,32]{1,0:T(1,128)S(1)} %bitcast.19, ...), custom_call_target="tpu_custom_call", output_to_operand_aliasing={{0}: (7, {}), {1}: (8, {}), {2}: (9, {})} | custom-call | tf_op jit(solution)/shard_map/pallas_call | solution.py:583
  62.1 6.7 %all-gather = f32[32,128]{1,0:T(8,128)S(1)} all-gather(f32[8,128]{1,0:T(8,128)S(1)} %get-tuple-element.72), channel_id=2, replica_groups=mesh['region'=4,'tile'=32] {'region'}, dimensions={0}, use_global_device_ids=true | all-gather | bytes 20480 | tf_op jit(solution)/shard_map/all_gather | solution.py:588
  68.8 3.0 %collective-permute-start.8 = (f32[4,8,128]{2,1,0:T(8,128)S(1)}, f32[4,8,128]{2,1,0:T(8,128)S(1)}, u32[]{:S(2)}, u32[]{:S(2)}) collective-permute-start(f32[4,8,128]{2,1,0:T(8,128)S(1)} %bitcast.16), channel_id=1, source_target_pairs={{0,1},{1,0},{2,3},{3,2},{4,5},{5,4},{6,7},{7,6},{8,9},{9,8},{10,11... | collective-permute-start | bytes 49160 | tf_op jit(solution)/shard_map/ppermute | solution.py:589
  71.8 6.2 %collective-permute-start.9 = (f32[4,8,128]{2,1,0:T(8,128)S(1)}, f32[4,8,128]{2,1,0:T(8,128)S(1)}, u32[]{:S(2)}, u32[]{:S(2)}) collective-permute-start(f32[4,8,128]{2,1,0:T(8,128)S(1)} %bitcast.17), channel_id=1, source_target_pairs={{1,2},{2,1},{3,4},{4,3},{5,6},{6,5},{7,8},{8,7},{9,10},{10,9},{11,... | collective-permute-start | bytes 49160 | tf_op jit(solution)/shard_map/ppermute | solution.py:590
  78.6 0.0 copy-done.7
  78.6 0.0 copy-done.10
  78.6 3.5 %shard_map.137 = (f32[6,28,72,128]{3,2,1,0:T(8,128)S(1)}, f32[4608,128]{1,0:T(8,128)}, s32[8,128]{1,0:T(8,128)S(1)}, f32[3,32,128]{2,1,0:T(8,128)S(1)}, f32[48,128]{1,0:T(8,128)S(1)}) custom-call(s32[1,64]{1,0:T(1,128)S(1)} %copy-done.10, s32[1]{0:T(128)S(6)} %copy.61.count_ref, f32[3,32]{1,0:T(4,128)S(1)} %copy-done.7, ...), custom_call_target="tpu_custom_call", output_to_operand_aliasing={{0}: (7, {})} | custom-call | tf_op jit(solution)/shard_map/pallas_call | solution.py:591
  82.1 0.0 collective-permute-done.8.first_ref
  82.1 0.0 collective-permute-done.9.second_ref
  82.1 1.6 %shard_map.138 = f32[4608,128]{1,0:T(8,128)} custom-call(f32[3,28,72,128]{3,2,1,0:T(8,128)S(1)} %get-tuple-element.71.v_ref, f32[4,8,128]{2,1,0:T(8,128)S(1)} %collective-permute-done.8.first_ref, f32[4,8,128]{2,1,0:T(8,128)S(1)} %collective-permute-done.9.second_ref, s32[8,128]{1,0:T(8,128)S(1)} %get-tuple-element.75.used_ref, ...), custom_call_target="tpu_custom_call", output_to_operand_aliasing={{}: (6, {})} | custom-call | tf_op jit(solution)/shard_map/pallas_call | solution.py:598
Async XLA Ops:
  0.0 12.4 %copy-start.3 = (f32[32,16,128]{2,1,0:T(8,128)S(1)}, f32[32,16,128]{2,1,0:T(8,128)}, u32[]{:S(2)}) copy-start(f32[32,16,128]{2,1,0:T(8,128)} %param.14) | copy-start | bytes 786436
  0.0 12.4 %copy-start.4 = (f32[32,16,128]{2,1,0:T(8,128)S(1)}, f32[32,16,128]{2,1,0:T(8,128)}, u32[]{:S(2)}) copy-start(f32[32,16,128]{2,1,0:T(8,128)} %param.15) | copy-start | bytes 786436
  0.0 12.4 %copy-start.5 = (f32[32,16,128]{2,1,0:T(8,128)S(1)}, f32[32,16,128]{2,1,0:T(8,128)}, u32[]{:S(2)}) copy-start(f32[32,16,128]{2,1,0:T(8,128)} %param.16) | copy-start | bytes 786436
  4.6 10.6 %collective-permute-start.1 = (f32[12,6,8,128]{3,2,1,0:T(8,128)}, f32[12,6,8,128]{3,2,1,0:T(8,128)S(1)}, u32[]{:S(2)}, u32[]{:S(2)}) collective-permute-start(f32[12,6,8,128]{3,2,1,0:T(8,128)} %get-tuple-element.43), channel_id=1, source_target_pairs={{0,1},{1,0},{2,3},{3,2},{4,5},{5,4},{6,7},{7,6},{8,9},{9,8},{10,11... | collective-permute-start | bytes 884744 | tf_op jit(solution)/shard_map/ppermute | solution.py:549
  6.0 13.7 %collective-permute-start = (f32[12,6,8,128]{3,2,1,0:T(8,128)}, f32[12,6,8,128]{3,2,1,0:T(8,128)S(1)}, u32[]{:S(2)}, u32[]{:S(2)}) collective-permute-start(f32[12,6,8,128]{3,2,1,0:T(8,128)} %get-tuple-element.42), channel_id=1, source_target_pairs={{1,2},{2,1},{3,4},{4,3},{5,6},{6,5},{7,8},{8,7},{9,10},{10,9},{11,... | collective-permute-start | bytes 884744 | tf_op jit(solution)/shard_map/ppermute | solution.py:550
  12.4 1.7 %copy-start.2 = (f32[9,32,16,128]{3,2,1,0:T(8,128)S(1)}, f32[9,32,16,128]{3,2,1,0:T(8,128)}, u32[]{:S(2)}) copy-start(f32[9,32,16,128]{3,2,1,0:T(8,128)} %param.13) | copy-start | bytes 7077892
  19.7 4.2 %copy-start = (bf16[2,4,256,128]{3,2,1,0:T(8,128)(2,1)S(1)}, bf16[2,4,256,128]{3,2,1,0:T(8,128)(2,1)}, u32[]{:S(2)}) copy-start(bf16[2,4,256,128]{3,2,1,0:T(8,128)(2,1)} %constant.4.clone.refs_0_.refs_4_.own_ref) | copy-start | bytes 1572868
  19.7 4.2 %copy-start.1 = (bf16[2,640,128]{2,1,0:T(8,128)(2,1)S(1)}, bf16[2,640,128]{2,1,0:T(8,128)(2,1)}, u32[]{:S(2)}) copy-start(bf16[2,640,128]{2,1,0:T(8,128)(2,1)} %constant.5.clone.refs_1_.refs_5_.halo_ref) | copy-start | bytes 983044
  20.0 19.3 %collective-permute-start.2 = (f32[59,40,128]{2,1,0:T(8,128)S(1)}, f32[59,40,128]{2,1,0:T(8,128)S(1)}, u32[]{:S(2)}, u32[]{:S(2)}) collective-permute-start(f32[59,40,128]{2,1,0:T(8,128)S(1)} %get-tuple-element.47), channel_id=1, source_target_pairs={{32,64},{64,32},{33,65},{65,33},{34,66},{66,34},{35,67},{67,35},{3... | collective-permute-start | bytes 3624968 | tf_op jit(solution)/shard_map/ppermute | solution.py:563
  22.0 1.9 %collective-permute-start.3 = (f32[23,40,128]{2,1,0:T(8,128)S(1)}, f32[23,40,128]{2,1,0:T(8,128)S(1)}, u32[]{:S(2)}, u32[]{:S(2)}) collective-permute-start(f32[23,40,128]{2,1,0:T(8,128)S(1)} %get-tuple-element.48), channel_id=1, source_target_pairs={{0,32},{32,0},{64,96},{96,64},{1,33},{33,1},{65,97},{97,65},{2,34}... | collective-permute-start | bytes 1413128 | tf_op jit(solution)/shard_map/ppermute | solution.py:562
  28.4 1.9 %collective-permute-start.4 = (f32[21,40,128]{2,1,0:T(8,128)S(1)}, f32[21,40,128]{2,1,0:T(8,128)S(1)}, u32[]{:S(2)}, u32[]{:S(2)}) collective-permute-start(f32[21,40,128]{2,1,0:T(8,128)S(1)} %get-tuple-element.52), channel_id=1, source_target_pairs={{0,32},{32,0},{64,96},{96,64},{1,33},{33,1},{65,97},{97,65},{2,34}... | collective-permute-start | bytes 1290248 | tf_op jit(solution)/shard_map/ppermute | solution.py:568
  42.6 16.9 %collective-permute-start.5 = (f32[48,40,128]{2,1,0:T(8,128)S(1)}, f32[48,40,128]{2,1,0:T(8,128)S(1)}, u32[]{:S(2)}, u32[]{:S(2)}) collective-permute-start(f32[48,40,128]{2,1,0:T(8,128)S(1)} %get-tuple-element.59), channel_id=1, source_target_pairs={{32,64},{64,32},{33,65},{65,33},{34,66},{66,34},{35,67},{67,35},{3... | collective-permute-start | bytes 2949128 | tf_op jit(solution)/shard_map/ppermute | solution.py:563
  44.5 2.0 %collective-permute-start.6 = (f32[21,40,128]{2,1,0:T(8,128)S(1)}, f32[21,40,128]{2,1,0:T(8,128)S(1)}, u32[]{:S(2)}, u32[]{:S(2)}) collective-permute-start(f32[21,40,128]{2,1,0:T(8,128)S(1)} %get-tuple-element.60), channel_id=1, source_target_pairs={{0,32},{32,0},{64,96},{96,64},{1,33},{33,1},{65,97},{97,65},{2,34}... | collective-permute-start | bytes 1290248 | tf_op jit(solution)/shard_map/ppermute | solution.py:562
  49.8 1.9 %collective-permute-start.7 = (f32[21,40,128]{2,1,0:T(8,128)S(1)}, f32[21,40,128]{2,1,0:T(8,128)S(1)}, u32[]{:S(2)}, u32[]{:S(2)}) collective-permute-start(f32[21,40,128]{2,1,0:T(8,128)S(1)} %get-tuple-element.64), channel_id=1, source_target_pairs={{0,32},{32,0},{64,96},{96,64},{1,33},{33,1},{65,97},{97,65},{2,34}... | collective-permute-start | bytes 1290248 | tf_op jit(solution)/shard_map/ppermute | solution.py:568
  51.6 7.9 %copy-start.6 = (f32[3,32]{1,0:T(4,128)S(1)}, f32[3,32]{1,0:T(4,128)}, u32[]{:S(2)}) copy-start(f32[3,32]{1,0:T(4,128)} %refs_1_.6) | copy-start | bytes 1156
  51.6 7.9 %copy-start.8 = (f32[32]{0:T(128)S(1)}, f32[32]{0:T(128)}, u32[]{:S(2)}) copy-start(f32[32]{0:T(128)} %param.18) | copy-start | bytes 388
  51.6 7.9 %copy-start.9 = (s32[32]{0:T(128)S(1)}, s32[32]{0:T(128)}, u32[]{:S(2)}) copy-start(s32[32]{0:T(128)} %param.20) | copy-start | bytes 388
  59.5 19.1 %copy-start.7 = (f32[3,32]{1,0:T(4,128)S(1)}, f32[3,32]{1,0:T(4,128)}, u32[]{:S(2)}) copy-start(f32[3,32]{1,0:T(4,128)} %profile_ref.1) | copy-start | bytes 1156
  59.5 19.1 %copy-start.10 = (s32[1,64]{1,0:T(1,128)S(1)}, s32[1,64]{1,0:T(1,128)}, u32[]{:S(2)}) copy-start(s32[1,64]{1,0:T(1,128)} %influence_ref.1) | copy-start | bytes 772
  68.8 13.3 %collective-permute-start.8 = (f32[4,8,128]{2,1,0:T(8,128)S(1)}, f32[4,8,128]{2,1,0:T(8,128)S(1)}, u32[]{:S(2)}, u32[]{:S(2)}) collective-permute-start(f32[4,8,128]{2,1,0:T(8,128)S(1)} %bitcast.16), channel_id=1, source_target_pairs={{0,1},{1,0},{2,3},{3,2},{4,5},{5,4},{6,7},{7,6},{8,9},{9,8},{10,11... | collective-permute-start | bytes 49160 | tf_op jit(solution)/shard_map/ppermute | solution.py:589
  71.8 10.3 %collective-permute-start.9 = (f32[4,8,128]{2,1,0:T(8,128)S(1)}, f32[4,8,128]{2,1,0:T(8,128)S(1)}, u32[]{:S(2)}, u32[]{:S(2)}) collective-permute-start(f32[4,8,128]{2,1,0:T(8,128)S(1)} %bitcast.17), channel_id=1, source_target_pairs={{1,2},{2,1},{3,4},{4,3},{5,6},{6,5},{7,8},{8,7},{9,10},{10,9},{11,... | collective-permute-start | bytes 49160 | tf_op jit(solution)/shard_map/ppermute | solution.py:590

commit v4 on v3

--- a/solution.py
+++ b/solution.py
@@ -6,9 +6,7 @@
 from jax.experimental.pallas import tpu as pltpu
 from jax.sharding import PartitionSpec as P
 
-NEAR = 1.125
-FAR = -1.0 / 24.0
-DT = 0.15
+DT = 0.15 / 24.0
 
 CX, CY, NZ = 16, 128, 32
 S, LIST = 32, 64
@@ -101,7 +99,6 @@
             else:
                 lhs = jnp.concatenate([parts[n][term] for n in range(GROUPS + 1)], axis=1)
                 total += product(lhs, halo_ref[k])
-        total = total * (1.0 / 24.0)
         for n, (_, _, _, slot) in enumerate(items):
             for j in range(count):
                 r = 8 * (n * even + j)
@@ -126,7 +123,7 @@
 
 
 def combine(m1, c0, p1, p2):
-    return NEAR * (p1 - c0) + FAR * (p2 - m1)
+    return 27.0 * (p1 - c0) - (p2 - m1)
 
 
 def diff_x(ref, f, x, forward):
@@ -174,11 +171,12 @@
         grad_x = diff_x(v_ref, VX, x, False)
         grad_y = d_ref[1, j]
         grad_z = diff_z(v_ref, VZ, x, False)
-        modulus = lame + 2.0 * mu
+        spread = lame * (grad_x + grad_y + grad_z)
+        double = mu + mu
         rates = (
-            (SXX, modulus * grad_x + lame * (grad_y + grad_z)),
-            (SYY, modulus * grad_y + lame * (grad_x + grad_z)),
-            (SZZ, modulus * grad_z + lame * (grad_x + grad_y)),
+            (SXX, double * grad_x + spread),
+            (SYY, double * grad_y + spread),
+            (SZZ, double * grad_z + spread),
             (SXY, mu * (d_ref[0, j] + diff_x(v_ref, VY, x, True))),
             (SXZ, mu * (diff_z(v_ref, VX, x, True) + diff_x(v_ref, VZ, x, True))),
             (SYZ, mu * (diff_z(v_ref, VY, x, True) + d_ref[2, j])),
@@ -194,37 +192,37 @@
                 pad_halo(t_ref, f, a + j)
 
 
-def take_halo(items, odd, inner, got_ref, v_ref, t_ref, p_ref):
-    n = 0
+def planes_of(items, odd, inner, out):
+    for kind, f, depth in items:
+        low, high = (0, CX - depth) if out else (-depth, CX)
+        row = jnp.where(odd, low, high) if inner else jnp.where(odd, high, low)
+        for k in range(depth):
+            yield kind, f, row + LOW + k
+
+
+def take_halo(items, odd, inner, read, v_ref, t_ref, p_ref):
     padded = []
-    for kind, f, depth in items:
-        above, below = CX, -depth
-        row = jnp.where(odd, below, above) if inner else jnp.where(odd, above, below)
-        for k in range(depth):
-            x = row + LOW + k
-            if kind == "p":
-                p_ref[f, x] = got_ref[n]
-            else:
-                store(v_ref if kind == "v" else t_ref, f, x, got_ref[n])
-                if kind == "v" or f in Z_STRESS:
-                    padded.append((v_ref if kind == "v" else t_ref, f, x))
-            n += 1
+    for n, (kind, f, x) in enumerate(planes_of(items, odd, inner, False)):
+        if kind == "p":
+            p_ref[f, x] = read(n)
+        else:
+            ref = v_ref if kind == "v" else t_ref
+            store(ref, f, x, read(n))
+            if kind == "v" or f in Z_STRESS:
+                padded.append((ref, f, x))
     for ref, f, x in padded:
         pad_halo(ref, f, x)
 
 
-def give_halo(items, odd, inner, send_ref, v_ref, t_ref, p_ref):
-    n = 0
-    for kind, f, depth in items:
-        top, bottom = CX - depth, 0
-        row = jnp.where(odd, bottom, top) if inner else jnp.where(odd, top, bottom)
-        for k in range(depth):
-            x = row + LOW + k
-            if kind == "p":
-                send_ref[n] = p_ref[f, x]
-            else:
-                send_ref[n] = load(v_ref if kind == "v" else t_ref, f, x)
-            n += 1
+def give_halo(items, odd, inner, send_ref, v_ref, t_ref, p_ref, own=True, halo=True):
+    for n, (kind, f, x) in enumerate(planes_of(items, odd, inner, True)):
+        ref = {"v": v_ref, "t": t_ref, "p": p_ref}[kind]
+        a, b = (0, NZ) if kind == "p" else (8, 56)
+        if own:
+            send_ref[n, 0:NZ] = ref[f, x, a:a + NZ, :]
+        if halo:
+            at = NZ if own else 0
+            send_ref[n, at:at + PACK] = ref[f, x, b:b + PACK, :]
 
 
 def pieces():
@@ -268,9 +266,11 @@
         put(v, parts[v])
 
 
-def edge_kernel(fields_ref, buoy_ref, lame_ref, mu_ref, first_ref, second_ref, buf_ref, sems):
+def edge_kernel(fields_ref, buoy_ref, lame_ref, mu_ref, first_ref, second_ref, token_ref, buf_ref,
+                sems):
     size = NZ * CX
     lane = lanes(PACK)
+    token_ref[...] = jnp.zeros((8, 128), jnp.float32)
     for a, copy in enumerate(fetch((fields_ref, buoy_ref, lame_ref, mu_ref), buf_ref, sems)):
         copy.wait()
         for block in range(2):
@@ -313,7 +313,7 @@
     lax.fori_loop(0, 12, body, 0)
 
 
-def build_kernel(fields_ref, buoy_ref, lame_ref, mu_ref, v_ref, t_ref, p_ref):
+def build_kernel(fields_ref, buoy_ref, lame_ref, mu_ref, after_ref, v_ref, t_ref, p_ref, outer_ref):
     size = NZ * CX
     zero = jnp.zeros((8, 128), jnp.float32)
 
@@ -334,6 +334,7 @@
                 t_ref[a - 3, x + LOW, 8:8 + NZ, :] = value
             else:
                 p_ref[a - 9, x + LOW, 0:NZ, :] = DT * value
+    give_halo(OUTER_FIRST, is_odd(), False, outer_ref, v_ref, t_ref, p_ref, halo=False)
 
 
 def halo_kernel(got_ref, half_ref, v_in, t_in, p_in, v_ref, t_ref, p_ref, outer_ref, inner_ref):
@@ -357,7 +358,7 @@
             one(a, a - 3, t_rows, ZROWS, 56, None)
         else:
             one(a, a - 9, p_rows, DEPTH, NZ, DT)
-    give_halo(OUTER_FIRST, odd, False, outer_ref, v_ref, t_ref, p_ref)
+    give_halo(OUTER_FIRST, odd, False, outer_ref, v_ref, t_ref, p_ref, own=False)
     give_halo(INNER_FIRST, odd, True, inner_ref, v_ref, t_ref, p_ref)
 
 
@@ -380,7 +381,7 @@
     odd = is_odd()
     if items is INNER_FIRST:
         pad_own(v_ref, t_ref)
-    take_halo(items, odd, True, got_ref, v_ref, t_ref, p_ref)
+    take_halo(items, odd, True, lambda n: got_ref[n], v_ref, t_ref, p_ref)
     mats = (v_ref, t_ref, p_ref, own_ref, halo_ref, d_ref)
     velocity_pass(*mats, jnp.where(odd, -2, back + 1), jnp.where(odd, -1, back + 2), CX - back)
     stress_pass(*mats, jnp.where(odd, 0, back + 3), CX - 3 - back)
@@ -388,8 +389,8 @@
         give_halo(INNER, odd, True, inner_ref, v_ref, t_ref, p_ref)
 
 
-def far_steps(items, last, odd, got_ref, v_ref, t_ref, p_ref, own_ref, halo_ref, d_ref):
-    take_halo(items, odd, False, got_ref, v_ref, t_ref, p_ref)
+def far_steps(items, last, odd, read, v_ref, t_ref, p_ref, own_ref, halo_ref, d_ref):
+    take_halo(items, odd, False, read, v_ref, t_ref, p_ref)
     mats = (v_ref, t_ref, p_ref, own_ref, halo_ref, d_ref)
     velocity_pass(*mats, jnp.where(odd, 14, -5), jnp.where(odd, 15, -4), 6)
     stress_pass(*mats, jnp.where(odd, 13, -3), 6)
@@ -398,17 +399,18 @@
         stress_pass(*mats, jnp.where(odd, 10, 0), 6)
 
 
-def far_kernel(items, own_ref, halo_ref, got_ref, v_in, t_in, p_in, v_ref, t_ref, p_ref,
+def far_kernel(own_ref, halo_ref, got_own, got_halo, v_in, t_in, p_in, v_ref, t_ref, p_ref,
                outer_ref, d_ref):
     odd = is_odd()
-    far_steps(items, False, odd, got_ref, v_ref, t_ref, p_ref, own_ref, halo_ref, d_ref)
+    far_steps(OUTER_FIRST, False, odd, lambda n: jnp.concatenate([got_own[n], got_halo[n]], axis=0),
+              v_ref, t_ref, p_ref, own_ref, halo_ref, d_ref)
     give_halo(OUTER, odd, False, outer_ref, v_ref, t_ref, p_ref)
 
 
-def station_kernel(items, count_ref, observed_ref, gain_ref, cell_ref, own_ref, halo_ref,
+def station_kernel(count_ref, observed_ref, gain_ref, cell_ref, own_ref, halo_ref,
                    got_ref, v_in, t_in, p_in, v_ref, t_ref, p_ref, packet_ref, d_ref, slot_ref):
     odd = is_odd()
-    far_steps(items, True, odd, got_ref, v_ref, t_ref, p_ref, own_ref, halo_ref, d_ref)
+    far_steps(OUTER, True, odd, lambda n: got_ref[n], v_ref, t_ref, p_ref, own_ref, halo_ref, d_ref)
     slot_ref[...] = jnp.zeros((16, 128), jnp.float32)
     slot_ref[0:3, 0:S] = observed_ref[...]
     slot_ref[3:4, 0:S] = gain_ref[...]
@@ -512,10 +514,11 @@
 HB = pl.BlockSpec(memory_space=pltpu.HBM)
 
 
-def call(kernel, outs, specs, scratch, out_specs=None, aliases=None, vmem=VMEM_BYTES):
+def call(kernel, outs, specs, scratch, out_specs=None, aliases=None, vmem=VMEM_BYTES,
+         cost=None):
     return pl.pallas_call(
         kernel, out_shape=outs, in_specs=specs, out_specs=out_specs or [VM] * len(outs),
-        scratch_shapes=list(scratch), input_output_aliases=aliases or {},
+        scratch_shapes=list(scratch), input_output_aliases=aliases or {}, cost_estimate=cost,
         compiler_params=pltpu.CompilerParams(vmem_limit_bytes=vmem))
 
 
@@ -544,14 +547,18 @@
              lame_first.reshape(size, CY), shear_modulus.reshape(size, CY))
     fetched = [pltpu.VMEM((12 * size, 128), jnp.float32), pltpu.SemaphoreType.DMA((12,))]
     packed, edges = struct(12, 6, PACK, 128), struct(12, 2, 8, 8, 128)
-    first, second = call(edge_kernel, (packed, packed), [HB] * 4, fetched,
+    first, second, token = call(edge_kernel, (packed, packed, struct(8, 128)), [HB] * 4, fetched,
                          vmem=62 * 2 ** 20)(*given)
     got_first = lax.ppermute(first, "tile", pairs(0))
     got_second = lax.ppermute(second, "tile", pairs(1))
-    v, t, p = call(build_kernel, state, [VM] * 4, [])(*given)
+    planes = plane_count(OUTER_FIRST)
+    v, t, p, outer = call(build_kernel, state + (struct(planes, NZ, 128),), [VM] * 5, [],
+                          cost=pl.CostEstimate(flops=0, bytes_accessed=10 ** 8, transcendentals=0))(
+        *given, token)
+    got_own = lax.ppermute(outer, "region", OUTER_SWAP)
     half, = call(first_halo_kernel, (edges,), [VM], [])(got_first)
     v, t, p, outer, inner = call(
-        halo_kernel, state + (struct(plane_count(OUTER_FIRST), DEPTH, 128),
+        halo_kernel, state + (struct(planes, PACK, 128),
                               struct(plane_count(INNER_FIRST), DEPTH, 128)),
         [VM] * 5, [], aliases={2: 0, 3: 1, 4: 2},
     )(got_second, half, v, t, p)
@@ -572,16 +579,16 @@
                 [d_scratch], aliases=alias,
             )(own, edge, got, v, t, p)
             v, t, p, outer = call(
-                bind(far_kernel, OUTER_FIRST), state + (struct(plane_count(OUTER), DEPTH, 128),),
-                [VM] * 6, [d_scratch], aliases=alias,
-            )(own, edge, got_outer, v, t, p)
+                far_kernel, state + (struct(plane_count(OUTER), DEPTH, 128),),
+                [VM] * 7, [d_scratch], aliases={4: 0, 5: 1, 6: 2},
+            )(own, edge, got_own, got_outer, v, t, p)
         else:
             v, t, p = call(
                 bind(near_kernel, INNER, 3, False), state, [VM] * 6, [d_scratch],
                 aliases=alias,
             )(own, edge, got, v, t, p)
     v, t, p, packet = call(
-        bind(station_kernel, OUTER), state + (struct(8, 128),), [SM] + [VM] * 9,
+        station_kernel, state + (struct(8, 128),), [SM] + [VM] * 9,
         [d_scratch, pltpu.VMEM((16, 128), jnp.float32)], aliases={7: 0, 8: 1, 9: 2},
     )(station_count, observed, station_weight.reshape(1, S), station_cell.reshape(1, S),
       own, edge, got_outer, v, t, p)

time: 84.1 us -> 78.6 us (0.935)
  waiting for transfers between devices: 21.2 us -> 9.66 us
  starting transfers between devices: 21.4 us -> 26.3 us
    ppermute x2, waiting for transfers between devices: 11.6 us -> 4.38 us  [per_device(): got_outer = lax.ppermute(outer, 'region', OUTER_SWAP)]
    ppermute x2, starting transfers between devices: 3.84 us -> 9.15 us  [per_device(): got_outer = lax.ppermute(outer, 'region', OUTER_SWAP)]
    ppermute x1, starting transfers between devices: 2.95 us -> 0.09 us  [per_device(): got_first = lax.ppermute(here, 'tile', pairs(0))]
    ppermute x1, waiting for transfers between devices: 3.33 us -> 0.66 us  [per_device(): got_second = lax.ppermute(second, 'tile', pairs(1))]
    ppermute x0 -> x1, starting transfers between devices: none -> 1.92 us  [per_device(): got_own = lax.ppermute(outer, 'region', OUTER_SWAP)]
    ppermute x4, waiting for transfers between devices: 6.31 us -> 4.61 us  [per_device(): got = lax.ppermute(inner, 'region', INNER_SWAP)]
    unnamed x22 -> x24, local copies, waits for them, and re-layouts: 1.7 us -> 2.38 us
  transfers between devices with their start and end apart: 10 -> 11, of which waited for: 7 -> 6; matrix products, arithmetic and copies ran while one was open for 0% -> 0% of each run, Pallas kernels for 22% -> 24%
where the time goes in v4:
time: 78.6 us; the launch traced here: 77.6 us
  Pallas kernels  30.9 us (39%)
  starting transfers between devices  26.3 us (33%)
  waiting for transfers between devices  9.66 us (12%)
  blocking collectives  6.68 us (8%)
  local copies, waits for them, and re-layouts  2.38 us (3%)
  between operations  1.71 us (2%)
    ppermute x2, starting transfers between devices, per_device(): got_outer = lax.ppermute(outer, 'region', OUTER_SWAP)  9.15 us
    pallas_call x2, Pallas kernels, per_device(): call(bind(near_kernel, INNER_FIRST if block == 0 else INNER, 0, True), st...  7.58 us
    ppermute x1, starting transfers between devices, per_device(): got_second = lax.ppermute(here, 'tile', pairs(1))  6.73 us
    all_gather x1, blocking collectives, per_device(): here = lax.all_gather(packet, 'region')  6.68 us
    ppermute x1, starting transfers between devices, per_device(): got_second = lax.ppermute(second, 'tile', pairs(1))  6.38 us
    pallas_call x1, Pallas kernels, per_device(): call(edge_kernel, (packed, packed, struct(8, 128)), [HB] * 4, fetched, vm...  4.61 us
    ppermute x4, waiting for transfers between devices, per_device(): got = lax.ppermute(inner, 'region', INNER_SWAP)  4.61 us
    ppermute x2, waiting for transfers between devices, per_device(): got_outer = lax.ppermute(outer, 'region', OUTER_SWAP)  4.38 us
  transfers between devices with their start and end apart: 11, of which 6 were waited for; matrix products, arithmetic and copies ran while one was open for 0% of the time, Pallas kernels for 24%

profile of v4, /device:TPU:22, one launch (start us, length us, event | category | flops | bytes accessed | tf_op | source)
XLA Modules:
  0.0 77.6 jit_solution(13671199747041440873)
XLA Ops:
  0.0 0.0 copy-start.3
  0.0 0.0 copy-start.4
  0.0 0.0 copy-start.5
  0.0 4.6 %shard_map.127 = (f32[12,6,8,128]{3,2,1,0:T(8,128)}, f32[12,6,8,128]{3,2,1,0:T(8,128)}, f32[8,128]{1,0:T(8,128)}) custom-call(f32[4608,128]{1,0:T(8,128)} %bitcast.8, f32[512,128]{1,0:T(8,128)} %bitcast.10, f32[512,128]{1,0:T(8,128)} %bitcast.12, f32[512,128]{1,0:T(8,128)} %bitcast.14), custom_call_target="tpu_custom_call" | custom-call | tf_op jit(solution)/shard_map/pallas_call | solution.py:550
  4.6 1.4 %collective-permute-start.2 = (f32[12,6,8,128]{3,2,1,0:T(8,128)}, f32[12,6,8,128]{3,2,1,0:T(8,128)S(1)}, u32[]{:S(2)}, u32[]{:S(2)}) collective-permute-start(f32[12,6,8,128]{3,2,1,0:T(8,128)} %get-tuple-element.47), channel_id=1, source_target_pairs={{0,1},{1,0},{2,3},{3,2},{4,5},{5,4},{6,7},{7,6},{8,9},{9,8},{10,11... | collective-permute-start | bytes 884744 | tf_op jit(solution)/shard_map/ppermute | solution.py:552
  6.0 6.4 %collective-permute-start.1 = (f32[12,6,8,128]{3,2,1,0:T(8,128)}, f32[12,6,8,128]{3,2,1,0:T(8,128)S(1)}, u32[]{:S(2)}, u32[]{:S(2)}) collective-permute-start(f32[12,6,8,128]{3,2,1,0:T(8,128)} %get-tuple-element.46), channel_id=1, source_target_pairs={{1,2},{2,1},{3,4},{4,3},{5,6},{6,5},{7,8},{8,7},{9,10},{10,9},{11,... | collective-permute-start | bytes 884744 | tf_op jit(solution)/shard_map/ppermute | solution.py:553
  12.4 0.0 copy-done.3
  12.4 0.0 copy-done.4
  12.4 0.0 copy-done.5
  12.4 0.0 copy-start.2
  12.4 1.7 %copy-done.2 = f32[9,32,16,128]{3,2,1,0:T(8,128)S(1)} copy-done((f32[9,32,16,128]{3,2,1,0:T(8,128)S(1)}, f32[9,32,16,128]{3,2,1,0:T(8,128)}, u32[]{:S(2)}) %copy-start.2) | copy-done | bytes 2359320
  14.1 0.0 copy-start.6
  14.1 0.7 copy-done.6
  14.8 1.2 %shard_map.128 = (f32[3,28,72,128]{3,2,1,0:T(8,128)S(1)}, f32[6,28,72,128]{3,2,1,0:T(8,128)S(1)}, f32[3,28,40,128]{3,2,1,0:T(8,128)S(1)}, f32[59,32,128]{2,1,0:T(8,128)S(1)}) custom-call(f32[4608,128]{1,0:T(8,128)S(1)} %bitcast.9, f32[512,128]{1,0:T(8,128)S(1)} %bitcast.11, f32[512,128]{1,0:T(8,128)S(1)} %bitcast.13, f32[512,128]{1,0:T(8,128)S(1)} %bitcast.15, ...), custom_call_target="tpu_custom_call" | custom-call | bytes 100000000 | tf_op jit(solution)/shard_map/pallas_call | solution.py:555
  16.0 1.9 %collective-permute-start = (f32[59,32,128]{2,1,0:T(8,128)S(1)}, f32[59,32,128]{2,1,0:T(8,128)S(1)}, u32[]{:S(2)}, u32[]{:S(2)}) collective-permute-start(f32[59,32,128]{2,1,0:T(8,128)S(1)} %get-tuple-element.45), channel_id=1, source_target_pairs={{32,64},{64,32},{33,65},{65,33},{34,66},{66,34},{35,67},{67,35},{3... | collective-permute-start | bytes 2899976 | tf_op jit(solution)/shard_map/ppermute | solution.py:558
  17.9 0.0 collective-permute-done.2.got_ref
  17.9 1.1 %shard_map.129.half_ref = f32[12,2,8,8,128]{4,3,2,1,0:T(8,128)S(1)} custom-call(f32[12,6,8,128]{3,2,1,0:T(8,128)S(1)} %collective-permute-done.2.got_ref), custom_call_target="tpu_custom_call" | custom-call | tf_op jit(solution)/shard_map/pallas_call | solution.py:559
  19.0 0.7 collective-permute-done.1.got_ref
  19.7 0.0 copy-start
  19.7 0.0 copy-start.1
  19.7 0.3 shard_map.130
  20.0 0.1 collective-permute-start.4
  20.1 1.8 %collective-permute-done.4.refs_2_ = f32[23,40,128]{2,1,0:T(8,128)S(1)} collective-permute-done((f32[23,40,128]{2,1,0:T(8,128)S(1)}, f32[23,40,128]{2,1,0:T(8,128)S(1)}, u32[]{:S(2)}, u32[]{:S(2)}) %collective-permute-start.4) | collective-permute-done | bytes 471072 | tf_op jit(solution)/shard_map/ppermute | solution.py:569
  21.9 0.0 copy-done
  21.9 0.0 copy-done.1
  21.9 4.5 %shard_map.131 = (f32[3,28,72,128]{3,2,1,0:T(8,128)S(1)}, f32[6,28,72,128]{3,2,1,0:T(8,128)S(1)}, f32[3,28,40,128]{3,2,1,0:T(8,128)S(1)}, f32[21,40,128]{2,1,0:T(8,128)S(1)}) custom-call(bf16[2,4,256,128]{3,2,1,0:T(8,128)(2,1)S(1)} %copy-done, bf16[2,640,128]{2,1,0:T(8,128)(2,1)S(1)} %copy-done.1, ...), custom_call_target="tpu_custom_call", output_to_operand_aliasing={{0}: (3, {}), {1}: (4, {}), {2}: (5, {})} | custom-call | tf_op jit(solution)/shard_map/pallas_call | solution.py:571
  26.4 0.2 collective-permute-start.5
  26.6 4.6 %collective-permute-start.3 = (f32[59,8,128]{2,1,0:T(8,128)S(1)}, f32[59,8,128]{2,1,0:T(8,128)S(1)}, u32[]{:S(2)}, u32[]{:S(2)}) collective-permute-start(f32[59,8,128]{2,1,0:T(8,128)S(1)} %get-tuple-element.51), channel_id=1, source_target_pairs={{32,64},{64,32},{33,65},{65,33},{34,66},{66,34},{35,67},{67,35},{3... | collective-permute-start | bytes 725000 | tf_op jit(solution)/shard_map/ppermute | solution.py:570
  31.1 0.0 collective-permute-done.5.refs_2_
  31.1 2.6 %shard_map.132 = (f32[3,28,72,128]{3,2,1,0:T(8,128)S(1)}, f32[6,28,72,128]{3,2,1,0:T(8,128)S(1)}, f32[3,28,40,128]{3,2,1,0:T(8,128)S(1)}, f32[21,40,128]{2,1,0:T(8,128)S(1)}) custom-call(bf16[2,4,256,128]{3,2,1,0:T(8,128)(2,1)S(1)} %copy-done, bf16[2,640,128]{2,1,0:T(8,128)(2,1)S(1)} %copy-done.1, ...), custom_call_target="tpu_custom_call", output_to_operand_aliasing={{0}: (3, {}), {1}: (4, {}), {2}: (5, {})} | custom-call | tf_op jit(solution)/shard_map/pallas_call | solution.py:577
  33.8 1.7 %collective-permute-done.3.got_halo = f32[59,8,128]{2,1,0:T(8,128)S(1)} collective-permute-done((f32[59,8,128]{2,1,0:T(8,128)S(1)}, f32[59,8,128]{2,1,0:T(8,128)S(1)}, u32[]{:S(2)}, u32[]{:S(2)}) %collective-permute-start.3) | collective-permute-done | bytes 241696 | tf_op jit(solution)/shard_map/ppermute | solution.py:570
  35.5 0.0 collective-permute-done.got_own
  35.5 3.1 %shard_map.133 = (f32[3,28,72,128]{3,2,1,0:T(8,128)S(1)}, f32[6,28,72,128]{3,2,1,0:T(8,128)S(1)}, f32[3,28,40,128]{3,2,1,0:T(8,128)S(1)}, f32[48,40,128]{2,1,0:T(8,128)S(1)}) custom-call(bf16[2,4,256,128]{3,2,1,0:T(8,128)(2,1)S(1)} %copy-done, bf16[2,640,128]{2,1,0:T(8,128)(2,1)S(1)} %copy-done.1, ...), custom_call_target="tpu_custom_call", output_to_operand_aliasing={{0}: (4, {}), {1}: (5, {}), {2}: (6, {})} | custom-call | tf_op jit(solution)/shard_map/pallas_call | solution.py:581
  38.7 4.6 %collective-permute-start.6 = (f32[48,40,128]{2,1,0:T(8,128)S(1)}, f32[48,40,128]{2,1,0:T(8,128)S(1)}, u32[]{:S(2)}, u32[]{:S(2)}) collective-permute-start(f32[48,40,128]{2,1,0:T(8,128)S(1)} %get-tuple-element.63), channel_id=1, source_target_pairs={{32,64},{64,32},{33,65},{65,33},{34,66},{66,34},{35,67},{67,35},{3... | collective-permute-start | bytes 2949128 | tf_op jit(solution)/shard_map/ppermute | solution.py:570
  43.2 0.3 collective-permute-start.7
  43.5 1.8 %collective-permute-done.7.refs_2_ = f32[21,40,128]{2,1,0:T(8,128)S(1)} collective-permute-done((f32[21,40,128]{2,1,0:T(8,128)S(1)}, f32[21,40,128]{2,1,0:T(8,128)S(1)}, u32[]{:S(2)}, u32[]{:S(2)}) %collective-permute-start.7) | collective-permute-done | bytes 430112 | tf_op jit(solution)/shard_map/ppermute | solution.py:569
  45.3 3.1 %shard_map.134 = (f32[3,28,72,128]{3,2,1,0:T(8,128)S(1)}, f32[6,28,72,128]{3,2,1,0:T(8,128)S(1)}, f32[3,28,40,128]{3,2,1,0:T(8,128)S(1)}, f32[21,40,128]{2,1,0:T(8,128)S(1)}) custom-call(bf16[2,4,256,128]{3,2,1,0:T(8,128)(2,1)S(1)} %copy-done, bf16[2,640,128]{2,1,0:T(8,128)(2,1)S(1)} %copy-done.1, ...), custom_call_target="tpu_custom_call", output_to_operand_aliasing={{0}: (3, {}), {1}: (4, {}), {2}: (5, {})} | custom-call | tf_op jit(solution)/shard_map/pallas_call | solution.py:571
  48.4 0.2 collective-permute-start.8
  49.3 1.0 %collective-permute-done.8.refs_2_ = f32[21,40,128]{2,1,0:T(8,128)S(1)} collective-permute-done((f32[21,40,128]{2,1,0:T(8,128)S(1)}, f32[21,40,128]{2,1,0:T(8,128)S(1)}, u32[]{:S(2)}, u32[]{:S(2)}) %collective-permute-start.8) | collective-permute-done | bytes 430112 | tf_op jit(solution)/shard_map/ppermute | solution.py:575
  50.3 0.0 copy-start.7
  50.3 0.0 copy-start.9
  50.3 0.0 copy-start.10
  50.3 2.6 %shard_map.135 = (f32[3,28,72,128]{3,2,1,0:T(8,128)S(1)}, f32[6,28,72,128]{3,2,1,0:T(8,128)S(1)}, f32[3,28,40,128]{3,2,1,0:T(8,128)S(1)}) custom-call(bf16[2,4,256,128]{3,2,1,0:T(8,128)(2,1)S(1)} %copy-done, bf16[2,640,128]{2,1,0:T(8,128)(2,1)S(1)} %copy-done.1, ...), custom_call_target="tpu_custom_call", output_to_operand_aliasing={{0}: (3, {}), {1}: (4, {}), {2}: (5, {})} | custom-call | tf_op jit(solution)/shard_map/pallas_call | solution.py:586
  52.9 2.6 %collective-permute-done.6.got_ref = f32[48,40,128]{2,1,0:T(8,128)S(1)} collective-permute-done((f32[48,40,128]{2,1,0:T(8,128)S(1)}, f32[48,40,128]{2,1,0:T(8,128)S(1)}, u32[]{:S(2)}, u32[]{:S(2)}) %collective-permute-start.6) | collective-permute-done | bytes 983072 | tf_op jit(solution)/shard_map/ppermute | solution.py:570
  55.6 0.0 copy-done.7
  55.6 0.0 copy-done.9
  55.6 0.0 copy-done.10
  55.6 0.0 copy-start.8
  55.6 0.0 copy-start.11
  55.6 2.5 %shard_map.136 = (f32[3,28,72,128]{3,2,1,0:T(8,128)S(1)}, f32[6,28,72,128]{3,2,1,0:T(8,128)S(1)}, f32[3,28,40,128]{3,2,1,0:T(8,128)S(1)}, f32[8,128]{1,0:T(8,128)S(1)}) custom-call(s32[1]{0:T(128)S(6)} %copy.60.count_ref, f32[3,32]{1,0:T(4,128)S(1)} %copy-done.7, f32[1,32]{1,0:T(1,128)S(1)} %bitcast.19, ...), custom_call_target="tpu_custom_call", output_to_operand_aliasing={{0}: (7, {}), {1}: (8, {}), {2}: (9, {})} | custom-call | tf_op jit(solution)/shard_map/pallas_call | solution.py:590
  58.2 6.7 %all-gather = f32[32,128]{1,0:T(8,128)S(1)} all-gather(f32[8,128]{1,0:T(8,128)S(1)} %get-tuple-element.76), channel_id=2, replica_groups=mesh['region'=4,'tile'=32] {'region'}, dimensions={0}, use_global_device_ids=true | all-gather | bytes 20480 | tf_op jit(solution)/shard_map/all_gather | solution.py:595
  64.8 6.7 %collective-permute-start.10 = (f32[4,8,128]{2,1,0:T(8,128)S(1)}, f32[4,8,128]{2,1,0:T(8,128)S(1)}, u32[]{:S(2)}, u32[]{:S(2)}) collective-permute-start(f32[4,8,128]{2,1,0:T(8,128)S(1)} %bitcast.16), channel_id=1, source_target_pairs={{1,2},{2,1},{3,4},{4,3},{5,6},{6,5},{7,8},{8,7},{9,10},{10,9},{11,... | collective-permute-start | bytes 49160 | tf_op jit(solution)/shard_map/ppermute | solution.py:597
  71.6 0.1 collective-permute-start.9
  72.3 0.0 copy-done.8
  72.3 0.0 copy-done.11
  72.3 3.5 %shard_map.137 = (f32[6,28,72,128]{3,2,1,0:T(8,128)S(1)}, f32[4608,128]{1,0:T(8,128)}, s32[8,128]{1,0:T(8,128)S(1)}, f32[3,32,128]{2,1,0:T(8,128)S(1)}, f32[48,128]{1,0:T(8,128)S(1)}) custom-call(s32[1,64]{1,0:T(1,128)S(1)} %copy-done.11, s32[1]{0:T(128)S(6)} %copy.61.count_ref, f32[3,32]{1,0:T(4,128)S(1)} %copy-done.8, ...), custom_call_target="tpu_custom_call", output_to_operand_aliasing={{0}: (7, {})} | custom-call | tf_op jit(solution)/shard_map/pallas_call | solution.py:598
  75.8 0.0 collective-permute-done.10.second_ref
  75.8 0.0 collective-permute-done.9.first_ref
  75.8 1.6 %shard_map.138 = f32[4608,128]{1,0:T(8,128)} custom-call(f32[3,28,72,128]{3,2,1,0:T(8,128)S(1)} %get-tuple-element.75.v_ref, f32[4,8,128]{2,1,0:T(8,128)S(1)} %collective-permute-done.9.first_ref, f32[4,8,128]{2,1,0:T(8,128)S(1)} %collective-permute-done.10.second_ref, s32[8,128]{1,0:T(8,128)S(1)} %get-tuple-element.79.used_ref, ...), custom_call_target="tpu_custom_call", output_to_operand_aliasing={{}: (6, {})} | custom-call | tf_op jit(solution)/shard_map/pallas_call | solution.py:605
Async XLA Ops:
  0.0 12.4 %copy-start.3 = (f32[32,16,128]{2,1,0:T(8,128)S(1)}, f32[32,16,128]{2,1,0:T(8,128)}, u32[]{:S(2)}) copy-start(f32[32,16,128]{2,1,0:T(8,128)} %param.14) | copy-start | bytes 786436
  0.0 12.4 %copy-start.4 = (f32[32,16,128]{2,1,0:T(8,128)S(1)}, f32[32,16,128]{2,1,0:T(8,128)}, u32[]{:S(2)}) copy-start(f32[32,16,128]{2,1,0:T(8,128)} %param.15) | copy-start | bytes 786436
  0.0 12.4 %copy-start.5 = (f32[32,16,128]{2,1,0:T(8,128)S(1)}, f32[32,16,128]{2,1,0:T(8,128)}, u32[]{:S(2)}) copy-start(f32[32,16,128]{2,1,0:T(8,128)} %param.16) | copy-start | bytes 786436
  4.6 13.3 %collective-permute-start.2 = (f32[12,6,8,128]{3,2,1,0:T(8,128)}, f32[12,6,8,128]{3,2,1,0:T(8,128)S(1)}, u32[]{:S(2)}, u32[]{:S(2)}) collective-permute-start(f32[12,6,8,128]{3,2,1,0:T(8,128)} %get-tuple-element.47), channel_id=1, source_target_pairs={{0,1},{1,0},{2,3},{3,2},{4,5},{5,4},{6,7},{7,6},{8,9},{9,8},{10,11... | collective-permute-start | bytes 884744 | tf_op jit(solution)/shard_map/ppermute | solution.py:552
  6.0 13.7 %collective-permute-start.1 = (f32[12,6,8,128]{3,2,1,0:T(8,128)}, f32[12,6,8,128]{3,2,1,0:T(8,128)S(1)}, u32[]{:S(2)}, u32[]{:S(2)}) collective-permute-start(f32[12,6,8,128]{3,2,1,0:T(8,128)} %get-tuple-element.46), channel_id=1, source_target_pairs={{1,2},{2,1},{3,4},{4,3},{5,6},{6,5},{7,8},{8,7},{9,10},{10,9},{11,... | collective-permute-start | bytes 884744 | tf_op jit(solution)/shard_map/ppermute | solution.py:553
  12.4 1.7 %copy-start.2 = (f32[9,32,16,128]{3,2,1,0:T(8,128)S(1)}, f32[9,32,16,128]{3,2,1,0:T(8,128)}, u32[]{:S(2)}) copy-start(f32[9,32,16,128]{3,2,1,0:T(8,128)} %param.13) | copy-start | bytes 7077892
  14.1 0.7 copy-start.6
  16.0 19.6 %collective-permute-start = (f32[59,32,128]{2,1,0:T(8,128)S(1)}, f32[59,32,128]{2,1,0:T(8,128)S(1)}, u32[]{:S(2)}, u32[]{:S(2)}) collective-permute-start(f32[59,32,128]{2,1,0:T(8,128)S(1)} %get-tuple-element.45), channel_id=1, source_target_pairs={{32,64},{64,32},{33,65},{65,33},{34,66},{66,34},{35,67},{67,35},{3... | collective-permute-start | bytes 2899976 | tf_op jit(solution)/shard_map/ppermute | solution.py:558
  19.7 2.3 %copy-start = (bf16[2,4,256,128]{3,2,1,0:T(8,128)(2,1)S(1)}, bf16[2,4,256,128]{3,2,1,0:T(8,128)(2,1)}, u32[]{:S(2)}) copy-start(bf16[2,4,256,128]{3,2,1,0:T(8,128)(2,1)} %constant.4.clone.refs_0_.own_ref) | copy-start | bytes 1572868
  19.7 2.3 %copy-start.1 = (bf16[2,640,128]{2,1,0:T(8,128)(2,1)S(1)}, bf16[2,640,128]{2,1,0:T(8,128)(2,1)}, u32[]{:S(2)}) copy-start(bf16[2,640,128]{2,1,0:T(8,128)(2,1)} %constant.5.clone.refs_1_.halo_ref) | copy-start | bytes 983044
  20.0 1.9 %collective-permute-start.4 = (f32[23,40,128]{2,1,0:T(8,128)S(1)}, f32[23,40,128]{2,1,0:T(8,128)S(1)}, u32[]{:S(2)}, u32[]{:S(2)}) collective-permute-start(f32[23,40,128]{2,1,0:T(8,128)S(1)} %get-tuple-element.52), channel_id=1, source_target_pairs={{0,32},{32,0},{64,96},{96,64},{1,33},{33,1},{65,97},{97,65},{2,34}... | collective-permute-start | bytes 1413128 | tf_op jit(solution)/shard_map/ppermute | solution.py:569
  26.4 4.7 %collective-permute-start.5 = (f32[21,40,128]{2,1,0:T(8,128)S(1)}, f32[21,40,128]{2,1,0:T(8,128)S(1)}, u32[]{:S(2)}, u32[]{:S(2)}) collective-permute-start(f32[21,40,128]{2,1,0:T(8,128)S(1)} %get-tuple-element.56), channel_id=1, source_target_pairs={{0,32},{32,0},{64,96},{96,64},{1,33},{33,1},{65,97},{97,65},{2,34}... | collective-permute-start | bytes 1290248 | tf_op jit(solution)/shard_map/ppermute | solution.py:575
  26.6 9.0 %collective-permute-start.3 = (f32[59,8,128]{2,1,0:T(8,128)S(1)}, f32[59,8,128]{2,1,0:T(8,128)S(1)}, u32[]{:S(2)}, u32[]{:S(2)}) collective-permute-start(f32[59,8,128]{2,1,0:T(8,128)S(1)} %get-tuple-element.51), channel_id=1, source_target_pairs={{32,64},{64,32},{33,65},{65,33},{34,66},{66,34},{35,67},{67,35},{3... | collective-permute-start | bytes 725000 | tf_op jit(solution)/shard_map/ppermute | solution.py:570
  38.7 16.9 %collective-permute-start.6 = (f32[48,40,128]{2,1,0:T(8,128)S(1)}, f32[48,40,128]{2,1,0:T(8,128)S(1)}, u32[]{:S(2)}, u32[]{:S(2)}) collective-permute-start(f32[48,40,128]{2,1,0:T(8,128)S(1)} %get-tuple-element.63), channel_id=1, source_target_pairs={{32,64},{64,32},{33,65},{65,33},{34,66},{66,34},{35,67},{67,35},{3... | collective-permute-start | bytes 2949128 | tf_op jit(solution)/shard_map/ppermute | solution.py:570
  43.2 2.0 %collective-permute-start.7 = (f32[21,40,128]{2,1,0:T(8,128)S(1)}, f32[21,40,128]{2,1,0:T(8,128)S(1)}, u32[]{:S(2)}, u32[]{:S(2)}) collective-permute-start(f32[21,40,128]{2,1,0:T(8,128)S(1)} %get-tuple-element.64), channel_id=1, source_target_pairs={{0,32},{32,0},{64,96},{96,64},{1,33},{33,1},{65,97},{97,65},{2,34}... | collective-permute-start | bytes 1290248 | tf_op jit(solution)/shard_map/ppermute | solution.py:569
  48.4 1.9 %collective-permute-start.8 = (f32[21,40,128]{2,1,0:T(8,128)S(1)}, f32[21,40,128]{2,1,0:T(8,128)S(1)}, u32[]{:S(2)}, u32[]{:S(2)}) collective-permute-start(f32[21,40,128]{2,1,0:T(8,128)S(1)} %get-tuple-element.68), channel_id=1, source_target_pairs={{0,32},{32,0},{64,96},{96,64},{1,33},{33,1},{65,97},{97,65},{2,34}... | collective-permute-start | bytes 1290248 | tf_op jit(solution)/shard_map/ppermute | solution.py:575
  50.3 5.3 %copy-start.7 = (f32[3,32]{1,0:T(4,128)S(1)}, f32[3,32]{1,0:T(4,128)}, u32[]{:S(2)}) copy-start(f32[3,32]{1,0:T(4,128)} %observed_ref.1) | copy-start | bytes 1156
  50.3 5.3 %copy-start.9 = (f32[32]{0:T(128)S(1)}, f32[32]{0:T(128)}, u32[]{:S(2)}) copy-start(f32[32]{0:T(128)} %param.18) | copy-start | bytes 388
  50.3 5.3 %copy-start.10 = (s32[32]{0:T(128)S(1)}, s32[32]{0:T(128)}, u32[]{:S(2)}) copy-start(s32[32]{0:T(128)} %param.20) | copy-start | bytes 388
  55.6 16.7 %copy-start.8 = (f32[3,32]{1,0:T(4,128)S(1)}, f32[3,32]{1,0:T(4,128)}, u32[]{:S(2)}) copy-start(f32[3,32]{1,0:T(4,128)} %profile_ref.1) | copy-start | bytes 1156
  55.6 16.7 %copy-start.11 = (s32[1,64]{1,0:T(1,128)S(1)}, s32[1,64]{1,0:T(1,128)}, u32[]{:S(2)}) copy-start(s32[1,64]{1,0:T(1,128)} %influence_ref.1) | copy-start | bytes 772
  64.8 11.0 %collective-permute-start.10 = (f32[4,8,128]{2,1,0:T(8,128)S(1)}, f32[4,8,128]{2,1,0:T(8,128)S(1)}, u32[]{:S(2)}, u32[]{:S(2)}) collective-permute-start(f32[4,8,128]{2,1,0:T(8,128)S(1)} %bitcast.16), channel_id=1, source_target_pairs={{1,2},{2,1},{3,4},{4,3},{5,6},{6,5},{7,8},{8,7},{9,10},{10,9},{11,... | collective-permute-start | bytes 49160 | tf_op jit(solution)/shard_map/ppermute | solution.py:597
  71.6 4.3 %collective-permute-start.9 = (f32[4,8,128]{2,1,0:T(8,128)S(1)}, f32[4,8,128]{2,1,0:T(8,128)S(1)}, u32[]{:S(2)}, u32[]{:S(2)}) collective-permute-start(f32[4,8,128]{2,1,0:T(8,128)S(1)} %bitcast.17), channel_id=1, source_target_pairs={{0,1},{1,0},{2,3},{3,2},{4,5},{5,4},{6,7},{7,6},{8,9},{9,8},{10,11... | collective-permute-start | bytes 49160 | tf_op jit(solution)/shard_map/ppermute | solution.py:596

commit v5 on v4

--- a/solution.py
+++ b/solution.py
@@ -29,6 +29,9 @@
 INNER = [("t", f, 3) for f in (SXX, SXY, SXZ)] + [("t", f, 2) for f in (SYY, SYZ, SZZ)] + [
     ("v", f, 2) for f in range(3)]
 INNER_FIRST = INNER + [("p", 0, 2)]
+
+EARLY_FIELDS = 12
+SECOND_WIDE = 6
 
 VMEM_BYTES = 8 * 2 ** 20
 
@@ -153,7 +156,7 @@
         store(v_ref, VZ, x, load(v_ref, VZ, x) + b * force)
         return 0
 
-    lax.fori_loop(0, count, body, 0)
+    lax.fori_loop(0, count, body, 0, unroll=2)
     for j in range(count):
         pad_halo(v_ref, VX, xa + j)
         pad_halo(v_ref, VY, ya + j)
@@ -185,7 +188,7 @@
             store(t_ref, f, x, load(t_ref, f, x) + rate)
         return 0
 
-    lax.fori_loop(0, count, body, 0)
+    lax.fori_loop(0, count, body, 0, unroll=2)
     if pads:
         for j in range(count):
             for f in Z_STRESS:
@@ -214,15 +217,77 @@
         pad_halo(ref, f, x)
 
 
-def give_halo(items, odd, inner, send_ref, v_ref, t_ref, p_ref, own=True, halo=True):
+def give_halo(items, odd, inner, send_ref, v_ref, t_ref, p_ref):
     for n, (kind, f, x) in enumerate(planes_of(items, odd, inner, True)):
         ref = {"v": v_ref, "t": t_ref, "p": p_ref}[kind]
-        a, b = (0, NZ) if kind == "p" else (8, 56)
-        if own:
-            send_ref[n, 0:NZ] = ref[f, x, a:a + NZ, :]
-        if halo:
-            at = NZ if own else 0
-            send_ref[n, at:at + PACK] = ref[f, x, b:b + PACK, :]
+        send_ref[n] = p_ref[f, x] if kind == "p" else load(ref, f, x)
+
+
+def own_rows(kind, f, x, v_ref, t_ref, p_ref):
+    return p_ref[f, x, 0:NZ, :] if kind == "p" else {"v": v_ref, "t": t_ref}[kind][f, x, 8:8 + NZ, :]
+
+
+def packed_rows(kind, f, x, v_ref, t_ref, p_ref):
+    if kind == "p":
+        return p_ref[f, x, NZ:DEPTH, :]
+    return {"v": v_ref, "t": t_ref}[kind][f, x, 56:64, :]
+
+
+def give_early(odd, send_ref, *state):
+    for n, plane in enumerate(planes_of(OUTER_FIRST[:EARLY_FIELDS], odd, False, True)):
+        send_ref[n] = own_rows(*plane, *state)
+
+
+def give_late(odd, send_ref, *state):
+    at = plane_count(OUTER_FIRST)
+    for n, plane in enumerate(planes_of(OUTER_FIRST, odd, False, True)):
+        send_ref[n] = packed_rows(*plane, *state)
+    for plane in planes_of(OUTER_FIRST[EARLY_FIELDS:], odd, False, True):
+        rows = own_rows(*plane, *state)
+        for k in range(4):
+            send_ref[at + k] = rows[8 * k:8 * k + 8]
+        at += 4
+
+
+def read_first(early_ref, late_ref):
+    early, planes = plane_count(OUTER_FIRST[:EARLY_FIELDS]), plane_count(OUTER_FIRST)
+
+    def read(n):
+        if n < early:
+            return jnp.concatenate([early_ref[n], late_ref[n]], axis=0)
+        at = planes + 4 * (n - early)
+        return jnp.concatenate([late_ref[at + k] for k in range(4)] + [late_ref[n]], axis=0)
+
+    return read
+
+
+def near_lanes():
+    spot = lanes(PACK) % 32
+    return (spot >= HALF - SECOND_WIDE) & (spot < HALF + SECOND_WIDE)
+
+
+def give_second(odd, send_ref, *state):
+    planes = list(planes_of(OUTER, odd, False, True))
+    for n, plane in enumerate(planes):
+        rows = own_rows(*plane, *state)
+        for k in range(4):
+            send_ref[4 * n + k] = rows[8 * k:8 * k + 8]
+    keep = near_lanes()
+    for n in range(0, len(planes), 2):
+        one, two = (packed_rows(*plane, *state) for plane in planes[n:n + 2])
+        send_ref[4 * len(planes) + n // 2] = jnp.where(keep, one, pltpu.roll(two, HALF, 1))
+
+
+def read_second(got_ref):
+    planes = plane_count(OUTER)
+
+    def read(n):
+        halo = got_ref[4 * planes + n // 2]
+        halo = pltpu.roll(halo, 128 - HALF, 1) if n % 2 else halo
+        halo = jnp.where(near_lanes(), halo, 0.0)
+        return jnp.concatenate([got_ref[4 * n + k] for k in range(4)] + [halo], axis=0)
+
+    return read
 
 
 def pieces():
@@ -334,7 +399,7 @@
                 t_ref[a - 3, x + LOW, 8:8 + NZ, :] = value
             else:
                 p_ref[a - 9, x + LOW, 0:NZ, :] = DT * value
-    give_halo(OUTER_FIRST, is_odd(), False, outer_ref, v_ref, t_ref, p_ref, halo=False)
+    give_early(is_odd(), outer_ref, v_ref, t_ref, p_ref)
 
 
 def halo_kernel(got_ref, half_ref, v_in, t_in, p_in, v_ref, t_ref, p_ref, outer_ref, inner_ref):
@@ -358,7 +423,7 @@
             one(a, a - 3, t_rows, ZROWS, 56, None)
         else:
             one(a, a - 9, p_rows, DEPTH, NZ, DT)
-    give_halo(OUTER_FIRST, odd, False, outer_ref, v_ref, t_ref, p_ref, own=False)
+    give_late(odd, outer_ref, v_ref, t_ref, p_ref)
     give_halo(INNER_FIRST, odd, True, inner_ref, v_ref, t_ref, p_ref)
 
 
@@ -373,20 +438,66 @@
     lax.fori_loop(LOW, LOW + CX, pads, 0)
 
 
-def near_kernel(items, back, sends, own_ref, halo_ref, got_ref, v_in, t_in, p_in, *refs):
-    if sends:
-        v_ref, t_ref, p_ref, inner_ref, d_ref = refs
-    else:
-        v_ref, t_ref, p_ref, d_ref = refs
+def near_step(items, back, odd, read, v_ref, t_ref, p_ref, own_ref, halo_ref, d_ref):
+    take_halo(items, odd, True, read, v_ref, t_ref, p_ref)
+    mats = (v_ref, t_ref, p_ref, own_ref, halo_ref, d_ref)
+    velocity_pass(*mats, jnp.where(odd, -2, back + 1), jnp.where(odd, -1, back + 2), CX - back)
+    stress_pass(*mats, jnp.where(odd, 0, back + 3), CX - 3 - back)
+
+
+def near_kernel(items, back, gots, gives, own_ref, halo_ref, *refs):
+    got_refs, refs = refs[:gots], refs[gots + 3:]
+    v_ref, t_ref, p_ref = refs[:3]
+    send_refs, d_ref = refs[3:3 + gives], refs[-1]
     odd = is_odd()
     if items is INNER_FIRST:
         pad_own(v_ref, t_ref)
-    take_halo(items, odd, True, lambda n: got_ref[n], v_ref, t_ref, p_ref)
-    mats = (v_ref, t_ref, p_ref, own_ref, halo_ref, d_ref)
-    velocity_pass(*mats, jnp.where(odd, -2, back + 1), jnp.where(odd, -1, back + 2), CX - back)
-    stress_pass(*mats, jnp.where(odd, 0, back + 3), CX - 3 - back)
-    if sends:
-        give_halo(INNER, odd, True, inner_ref, v_ref, t_ref, p_ref)
+
+    def read(n):
+        part = plane_count(INNER[:4])
+        return got_refs[0][n] if gots == 1 or n < part else got_refs[1][n - part]
+
+    near_step(items, back, odd, read, v_ref, t_ref, p_ref, own_ref, halo_ref, d_ref)
+    if gives == 1:
+        give_halo(INNER, odd, True, send_refs[0], v_ref, t_ref, p_ref)
+    else:
+        give_halo(INNER[:4], odd, True, send_refs[0], v_ref, t_ref, p_ref)
+        give_halo(INNER[4:], odd, True, send_refs[1], v_ref, t_ref, p_ref)
+
+
+def stress_half(first, t_ref, out_ref, rows_ref, sem):
+    flat = rows_ref.reshape(6 * NZ * 8, 128)
+
+    def body(r, _):
+        for f in range(6):
+            flat[pl.ds(f * NZ * 8 + r, NZ, stride=8), :] = t_ref[f, first + r + LOW, 8:8 + NZ, :]
+        return 0
+
+    lax.fori_loop(0, 8, body, 0, unroll=2)
+    copy = pltpu.make_async_copy(
+        rows_ref, out_ref.at[pl.ds(3 * NZ, 6 * NZ), pl.ds(pl.multiple_of(first, 8), 8)], sem)
+    copy.start()
+    return copy
+
+
+def last_near_kernel(influence_ref, count_ref, profile_ref, own_ref, halo_ref, got_ref, v_in, t_in,
+                     p_in, v_ref, t_ref, p_ref, out_ref, used_ref, profile_rows, d_ref, rows_ref, sem):
+    odd = is_odd()
+    near_step(INNER, 3, odd, lambda n: got_ref[n], v_ref, t_ref, p_ref, own_ref, halo_ref, d_ref)
+    copy = stress_half(jnp.where(odd, 0, 8), t_ref, out_ref, rows_ref, sem)
+    lane = lanes(8)
+    column = lax.broadcasted_iota(jnp.int32, (8, 128), 0) + lax.axis_index("tile") - 1
+    slot_id = (lane // S * 32 + column) * S + lane % S
+    slot_id = jnp.where((column >= 0) & (column < 32), slot_id, -1)
+    used = jnp.zeros((8, 128), jnp.int32)
+    for k in range(LIST):
+        hit = (slot_id == influence_ref[0, k]) & (k < count_ref[0])
+        used = jnp.where(hit, 1, used)
+    used_ref[...] = used
+    for c in range(3):
+        for z in range(NZ):
+            profile_rows[c, z:z + 1, :] = jnp.full((1, 128), profile_ref[c, z], jnp.float32)
+    copy.wait()
 
 
 def far_steps(items, last, odd, read, v_ref, t_ref, p_ref, own_ref, halo_ref, d_ref):
@@ -402,15 +513,14 @@
 def far_kernel(own_ref, halo_ref, got_own, got_halo, v_in, t_in, p_in, v_ref, t_ref, p_ref,
                outer_ref, d_ref):
     odd = is_odd()
-    far_steps(OUTER_FIRST, False, odd, lambda n: jnp.concatenate([got_own[n], got_halo[n]], axis=0),
-              v_ref, t_ref, p_ref, own_ref, halo_ref, d_ref)
-    give_halo(OUTER, odd, False, outer_ref, v_ref, t_ref, p_ref)
+    far_steps(OUTER_FIRST, False, odd, read_first(got_own, got_halo), v_ref, t_ref, p_ref, own_ref, halo_ref, d_ref)
+    give_second(odd, outer_ref, v_ref, t_ref, p_ref)
 
 
 def station_kernel(count_ref, observed_ref, gain_ref, cell_ref, own_ref, halo_ref,
                    got_ref, v_in, t_in, p_in, v_ref, t_ref, p_ref, packet_ref, d_ref, slot_ref):
     odd = is_odd()
-    far_steps(OUTER, True, odd, lambda n: got_ref[n], v_ref, t_ref, p_ref, own_ref, halo_ref, d_ref)
+    far_steps(OUTER, True, odd, read_second(got_ref), v_ref, t_ref, p_ref, own_ref, halo_ref, d_ref)
     slot_ref[...] = jnp.zeros((16, 128), jnp.float32)
     slot_ref[0:3, 0:S] = observed_ref[...]
     slot_ref[3:4, 0:S] = gain_ref[...]
@@ -456,53 +566,35 @@
     return cell_x, cell_y
 
 
-def stress_out_kernel(influence_ref, count_ref, profile_ref, own_ref, halo_ref, here_ref, v_ref,
-                      t_in, p_ref, t_ref, out_ref, used_ref, profile_rows, own_part, d_ref, rows_ref,
-                      sem):
+def stress_out_kernel(own_ref, halo_ref, here_ref, used_ref, v_ref, t_in, p_ref, out_in, t_ref,
+                      out_ref, own_part, d_ref, rows_ref, sem):
     odd = is_odd()
     stress_pass(v_ref, t_ref, p_ref, own_ref, halo_ref, d_ref, jnp.where(odd, 10, 0), 6, pads=False)
-    size = NZ * CX
-
-    def body(r, _):
-        for f in range(6):
-            rows_ref[pl.ds(f * size + r, NZ, stride=CX), :] = t_ref[f, r + LOW, 8:8 + NZ, :]
-        return 0
-
-    lax.fori_loop(0, CX, body, 0)
-    copy = pltpu.make_async_copy(rows_ref, out_ref.at[pl.ds(3 * size, 6 * size)], sem)
-    copy.start()
-    lane = lanes(8)
-    column = lax.broadcasted_iota(jnp.int32, (8, 128), 0) + lax.axis_index("tile") - 1
-    slot_id = (lane // S * 32 + column) * S + lane % S
-    slot_id = jnp.where((column >= 0) & (column < 32), slot_id, -1)
-    used = jnp.zeros((8, 128), jnp.int32)
-    for k in range(LIST):
-        hit = (slot_id == influence_ref[0, k]) & (k < count_ref[0])
-        used = jnp.where(hit, 1, used)
-    used_ref[...] = used
-    for c in range(3):
-        for z in range(NZ):
-            profile_rows[c, z:z + 1, :] = jnp.full((1, 128), profile_ref[c, z], jnp.float32)
-    own_part[...] = tile_column(here_ref, used[1:2], *cell_places())
+    copy = stress_half(jnp.where(odd, 8, 0), t_ref, out_ref, rows_ref, sem)
+    own_part[...] = tile_column(here_ref, used_ref[1:2], *cell_places())
     copy.wait()
 
 
 def increment_kernel(v_ref, first_ref, second_ref, used_ref, profile_rows, own_part, out_in, out_ref,
-                     rows_ref, sem):
+                     rows_ref, sems):
     odd = lax.rem(lax.axis_index("tile"), 2) > 0
     before = [jnp.where(odd, first_ref[r], second_ref[r]) for r in range(4)]
     after = [jnp.where(odd, second_ref[r], first_ref[r]) for r in range(4)]
     places = cell_places()
     increment = (own_part[...] + tile_column(before, used_ref[0:1], *places)
                  + tile_column(after, used_ref[2:3], *places))
+    flat = rows_ref.reshape(3 * NZ * CX, 128)
+    copies = []
     for c in range(3):
         for r in range(CX):
             value = v_ref[c, r + LOW, 8:8 + NZ, :]
             value = value + profile_rows[c] * increment[c * CX + r:c * CX + r + 1, :]
-            rows_ref[pl.ds(c * NZ * CX + r, NZ, stride=CX), :] = value
-    copy = pltpu.make_async_copy(rows_ref, out_ref.at[pl.ds(0, 3 * NZ * CX)], sem)
-    copy.start()
-    copy.wait()
+            flat[pl.ds(c * NZ * CX + r, NZ, stride=CX), :] = value
+        part = pl.ds(c * NZ, NZ)
+        copies.append(pltpu.make_async_copy(rows_ref.at[part], out_ref.at[part], sems.at[c]))
+        copies[c].start()
+    for copy in copies:
+        copy.wait()
 
 
 def struct(*shape):
@@ -528,6 +620,9 @@
 
 INNER_SWAP = [(0, 1), (1, 0), (2, 3), (3, 2)]
 OUTER_SWAP = [(1, 2), (2, 1)]
+
+
+FREE = pl.CostEstimate(flops=1024, bytes_accessed=1024, transcendentals=0)
 
 
 def bind(kernel, *first):
@@ -551,42 +646,49 @@
                          vmem=62 * 2 ** 20)(*given)
     got_first = lax.ppermute(first, "tile", pairs(0))
     got_second = lax.ppermute(second, "tile", pairs(1))
-    planes = plane_count(OUTER_FIRST)
-    v, t, p, outer = call(build_kernel, state + (struct(planes, NZ, 128),), [VM] * 5, [],
+    early, planes = plane_count(OUTER_FIRST[:EARLY_FIELDS]), plane_count(OUTER_FIRST)
+    v, t, p, outer = call(build_kernel, state + (struct(early, NZ, 128),), [VM] * 5, [],
                           cost=pl.CostEstimate(flops=0, bytes_accessed=10 ** 8, transcendentals=0))(
         *given, token)
     got_own = lax.ppermute(outer, "region", OUTER_SWAP)
     half, = call(first_halo_kernel, (edges,), [VM], [])(got_first)
     v, t, p, outer, inner = call(
-        halo_kernel, state + (struct(planes, PACK, 128),
+        halo_kernel, state + (struct(planes + 4 * (planes - early), PACK, 128),
                               struct(plane_count(INNER_FIRST), DEPTH, 128)),
         [VM] * 5, [], aliases={2: 0, 3: 1, 4: 2},
     )(got_second, half, v, t, p)
     inner_struct = struct(plane_count(INNER), DEPTH, 128)
     d_scratch = pltpu.VMEM((3, CX, DEPTH, 128), jnp.float32)
     alias = {3: 0, 4: 1, 5: 2}
+    result = struct(9 * NZ, CX, 128)
     for block in range(2):
         got = lax.ppermute(inner, "region", INNER_SWAP)
         got_outer = lax.ppermute(outer, "region", OUTER_SWAP)
-        v, t, p, inner = call(
-            bind(near_kernel, INNER_FIRST if block == 0 else INNER, 0, True),
-            state + (inner_struct,), [VM] * 6, [d_scratch], aliases=alias,
+        split = 2 if block == 0 else 1
+        parts = (INNER[:4], INNER[4:]) if block == 0 else (INNER,)
+        v, t, p, *inner = call(
+            bind(near_kernel, INNER_FIRST if block == 0 else INNER, 0, 1, split),
+            state + tuple(struct(plane_count(part), DEPTH, 128) for part in parts), [VM] * 6,
+            [d_scratch], aliases=alias, cost=FREE,
         )(own, edge, got, v, t, p)
-        got = lax.ppermute(inner, "region", INNER_SWAP)
+        got = [lax.ppermute(part, "region", INNER_SWAP) for part in inner]
         if block == 0:
             v, t, p, inner = call(
-                bind(near_kernel, INNER, 3, True), state + (inner_struct,), [VM] * 6,
-                [d_scratch], aliases=alias,
-            )(own, edge, got, v, t, p)
+                bind(near_kernel, INNER, 3, 2, 1), state + (inner_struct,), [VM] * 7,
+                [d_scratch], aliases={4: 0, 5: 1, 6: 2}, cost=FREE,
+            )(own, edge, *got, v, t, p)
             v, t, p, outer = call(
-                far_kernel, state + (struct(plane_count(OUTER), DEPTH, 128),),
+                far_kernel, state + (struct(4 * plane_count(OUTER) + plane_count(OUTER) // 2, 8, 128),),
                 [VM] * 7, [d_scratch], aliases={4: 0, 5: 1, 6: 2},
             )(own, edge, got_own, got_outer, v, t, p)
         else:
-            v, t, p = call(
-                bind(near_kernel, INNER, 3, False), state, [VM] * 6, [d_scratch],
-                aliases=alias,
-            )(own, edge, got, v, t, p)
+            v, t, p, out, used, profile_rows = call(
+                last_near_kernel,
+                state + (result, jax.ShapeDtypeStruct((8, 128), jnp.int32), struct(3, NZ, 128)),
+                [SM] * 3 + [VM] * 6,
+                [d_scratch, pltpu.VMEM((6 * NZ, 8, 128), jnp.float32), pltpu.SemaphoreType.DMA],
+                out_specs=[VM] * 3 + [HB] + [VM] * 2, aliases={6: 0, 7: 1, 8: 2},
+            )(influence, influence_count, depth_profile, own, edge, *got, v, t, p)
     v, t, p, packet = call(
         station_kernel, state + (struct(8, 128),), [SM] + [VM] * 9,
         [d_scratch, pltpu.VMEM((16, 128), jnp.float32)], aliases={7: 0, 8: 1, 9: 2},
@@ -595,17 +697,15 @@
     here = lax.all_gather(packet, "region")
     got_first = lax.ppermute(here, "tile", pairs(0))
     got_second = lax.ppermute(here, "tile", pairs(1))
-    _, out, used, profile_rows, own_part = call(
-        stress_out_kernel,
-        (state[1], struct(9 * size, 128), jax.ShapeDtypeStruct((8, 128), jnp.int32),
-         struct(3, NZ, 128), struct(3 * CX, CY)), [SM] * 3 + [VM] * 6,
-        [d_scratch, pltpu.VMEM((6 * size, 128), jnp.float32), pltpu.SemaphoreType.DMA],
-        out_specs=[VM, HB, VM, VM, VM], aliases={7: 0},
-    )(influence, influence_count, depth_profile, own, edge, here, v, t, p)
+    _, out, own_part = call(
+        stress_out_kernel, (state[1], result, struct(3 * CX, CY)), [VM] * 7 + [HB],
+        [d_scratch, pltpu.VMEM((6 * NZ, 8, 128), jnp.float32), pltpu.SemaphoreType.DMA],
+        out_specs=[VM, HB, VM], aliases={5: 0, 7: 1},
+    )(own, edge, here, used, v, t, p, out)
     out, = call(
-        increment_kernel, (struct(9 * size, 128),), [VM] * 6 + [HB],
-        [pltpu.VMEM((3 * size, 128), jnp.float32), pltpu.SemaphoreType.DMA], out_specs=[HB],
-        aliases={6: 0},
+        increment_kernel, (result,), [VM] * 6 + [HB],
+        [pltpu.VMEM((3 * NZ, CX, 128), jnp.float32), pltpu.SemaphoreType.DMA((3,))],
+        out_specs=[HB], aliases={6: 0},
     )(v, got_first, got_second, used, profile_rows, own_part, out)
     return out.reshape(9, NZ, CX, CY)
 

time: 78.6 us -> 74.9 us (0.953)
  starting transfers between devices: 26.3 us -> 23.5 us
    ppermute x4 -> x2, waiting for transfers between devices: 4.61 us -> 1.76 us  [per_device(): got = lax.ppermute(inner, 'region', INNER_SWAP)]
    ppermute x2, starting transfers between devices: 9.15 us -> 6.45 us  [per_device(): got_outer = lax.ppermute(outer, 'region', OUTER_SWAP)]
    ppermute x0 -> x3, waiting for transfers between devices: none -> 1.61 us  [per_device(): got = [lax.ppermute(part, 'region', INNER_SWAP) for part in inner]]
    ppermute x1, starting transfers between devices: 6.73 us -> 5.26 us  [per_device(): got_second = lax.ppermute(here, 'tile', pairs(1))]
    ppermute x1, waiting for transfers between devices: 0.01 us -> 1.43 us  [per_device(): got_second = lax.ppermute(here, 'tile', pairs(1))]
    ppermute x1, starting transfers between devices: 0.09 us -> 0.93 us  [per_device(): got_first = lax.ppermute(here, 'tile', pairs(0))]
    ppermute x0 -> x3, starting transfers between devices: none -> 0.8 us  [per_device(): got = [lax.ppermute(part, 'region', INNER_SWAP) for part in inner]]
  transfers between devices with their start and end apart: 11 -> 12, of which waited for: 6 -> 7; matrix products, arithmetic and copies ran while one was open for 0% -> 0% of each run, Pallas kernels for 24% -> 25%
where the time goes in v5:
time: 74.9 us; the launch traced here: 74.6 us
  Pallas kernels  30.2 us (40%)
  starting transfers between devices  23.5 us (31%)
  waiting for transfers between devices  10.2 us (14%)
  blocking collectives  6.68 us (9%)
  local copies, waits for them, and re-layouts  2.37 us (3%)
  between operations  1.7 us (2%)
    pallas_call x2, Pallas kernels, per_device(): call(bind(near_kernel, INNER_FIRST if block == 0 else INNER, 0, 1, split)...  7.33 us
    all_gather x1, blocking collectives, per_device(): here = lax.all_gather(packet, 'region')  6.68 us
    ppermute x2, starting transfers between devices, per_device(): got_outer = lax.ppermute(outer, 'region', OUTER_SWAP)  6.45 us
    ppermute x1, starting transfers between devices, per_device(): got_second = lax.ppermute(second, 'tile', pairs(1))  6.38 us
    ppermute x1, starting transfers between devices, per_device(): got_second = lax.ppermute(here, 'tile', pairs(1))  5.26 us
    ppermute x2, waiting for transfers between devices, per_device(): got_outer = lax.ppermute(outer, 'region', OUTER_SWAP)  4.68 us
    pallas_call x1, Pallas kernels, per_device(): call(edge_kernel, (packed, packed, struct(8, 128)), [HB] * 4, fetched, vm...  4.61 us
    pallas_call x1, Pallas kernels, per_device(): call(last_near_kernel, state + (result, jax.ShapeDtypeStruct((8, 128), jn...  4.2 us
  transfers between devices with their start and end apart: 12, of which 7 were waited for; matrix products, arithmetic and copies ran while one was open for 0% of the time, Pallas kernels for 25%

profile of v5, /device:TPU:22, one launch (start us, length us, event | category | flops | bytes accessed | tf_op | source)
XLA Modules:
  0.0 74.6 jit_solution(1595745533915415099)
XLA Ops:
  0.0 0.0 copy-start.3
  0.0 0.0 copy-start.4
  0.0 0.0 copy-start.5
  0.0 4.6 %shard_map.127 = (f32[12,6,8,128]{3,2,1,0:T(8,128)}, f32[12,6,8,128]{3,2,1,0:T(8,128)}, f32[8,128]{1,0:T(8,128)}) custom-call(f32[4608,128]{1,0:T(8,128)} %bitcast.8, f32[512,128]{1,0:T(8,128)} %bitcast.10, f32[512,128]{1,0:T(8,128)} %bitcast.12, f32[512,128]{1,0:T(8,128)} %bitcast.14), custom_call_target="tpu_custom_call" | custom-call | tf_op jit(solution)/shard_map/pallas_call | solution.py:645
  4.6 1.4 %collective-permute-start.2 = (f32[12,6,8,128]{3,2,1,0:T(8,128)}, f32[12,6,8,128]{3,2,1,0:T(8,128)S(1)}, u32[]{:S(2)}, u32[]{:S(2)}) collective-permute-start(f32[12,6,8,128]{3,2,1,0:T(8,128)} %get-tuple-element.49), channel_id=1, source_target_pairs={{0,1},{1,0},{2,3},{3,2},{4,5},{5,4},{6,7},{7,6},{8,9},{9,8},{10,11... | collective-permute-start | bytes 884744 | tf_op jit(solution)/shard_map/ppermute | solution.py:647
  6.0 6.4 %collective-permute-start.1 = (f32[12,6,8,128]{3,2,1,0:T(8,128)}, f32[12,6,8,128]{3,2,1,0:T(8,128)S(1)}, u32[]{:S(2)}, u32[]{:S(2)}) collective-permute-start(f32[12,6,8,128]{3,2,1,0:T(8,128)} %get-tuple-element.48), channel_id=1, source_target_pairs={{1,2},{2,1},{3,4},{4,3},{5,6},{6,5},{7,8},{8,7},{9,10},{10,9},{11,... | collective-permute-start | bytes 884744 | tf_op jit(solution)/shard_map/ppermute | solution.py:648
  12.4 0.0 copy-done.3
  12.4 0.0 copy-done.4
  12.4 0.0 copy-done.5
  12.4 0.0 copy-start.2
  12.4 1.7 %copy-done.2 = f32[9,32,16,128]{3,2,1,0:T(8,128)S(1)} copy-done((f32[9,32,16,128]{3,2,1,0:T(8,128)S(1)}, f32[9,32,16,128]{3,2,1,0:T(8,128)}, u32[]{:S(2)}) %copy-start.2) | copy-done | bytes 2359320
  14.1 0.0 copy-start.6
  14.1 0.7 copy-done.6
  14.8 1.2 %shard_map.128 = (f32[3,28,72,128]{3,2,1,0:T(8,128)S(1)}, f32[6,28,72,128]{3,2,1,0:T(8,128)S(1)}, f32[3,28,40,128]{3,2,1,0:T(8,128)S(1)}, f32[59,32,128]{2,1,0:T(8,128)S(1)}) custom-call(f32[4608,128]{1,0:T(8,128)S(1)} %bitcast.9, f32[512,128]{1,0:T(8,128)S(1)} %bitcast.11, f32[512,128]{1,0:T(8,128)S(1)} %bitcast.13, f32[512,128]{1,0:T(8,128)S(1)} %bitcast.15, ...), custom_call_target="tpu_custom_call" | custom-call | bytes 100000000 | tf_op jit(solution)/shard_map/pallas_call | solution.py:650
  16.0 1.9 %collective-permute-start = (f32[59,32,128]{2,1,0:T(8,128)S(1)}, f32[59,32,128]{2,1,0:T(8,128)S(1)}, u32[]{:S(2)}, u32[]{:S(2)}) collective-permute-start(f32[59,32,128]{2,1,0:T(8,128)S(1)} %get-tuple-element.47), channel_id=1, source_target_pairs={{32,64},{64,32},{33,65},{65,33},{34,66},{66,34},{35,67},{67,35},{3... | collective-permute-start | bytes 2899976 | tf_op jit(solution)/shard_map/ppermute | solution.py:653
  17.9 0.0 collective-permute-done.2.got_ref
  17.9 1.1 %shard_map.129.half_ref = f32[12,2,8,8,128]{4,3,2,1,0:T(8,128)S(1)} custom-call(f32[12,6,8,128]{3,2,1,0:T(8,128)S(1)} %collective-permute-done.2.got_ref), custom_call_target="tpu_custom_call" | custom-call | tf_op jit(solution)/shard_map/pallas_call | solution.py:654
  19.0 0.7 collective-permute-done.1.got_ref
  19.7 0.0 copy-start
  19.7 0.0 copy-start.1
  19.7 0.3 shard_map.130
  20.0 0.1 collective-permute-start.4
  20.1 4.5 %collective-permute-start.3 = (f32[59,8,128]{2,1,0:T(8,128)S(1)}, f32[59,8,128]{2,1,0:T(8,128)S(1)}, u32[]{:S(2)}, u32[]{:S(2)}) collective-permute-start(f32[59,8,128]{2,1,0:T(8,128)S(1)} %get-tuple-element.53), channel_id=1, source_target_pairs={{32,64},{64,32},{33,65},{65,33},{34,66},{66,34},{35,67},{67,35},{3... | collective-permute-start | bytes 725000 | tf_op jit(solution)/shard_map/ppermute | solution.py:666
  24.6 0.0 collective-permute-done.4.refs_2_
  24.7 0.0 copy-done
  24.7 0.0 copy-done.1
  24.7 4.3 %shard_map.131 = (f32[3,28,72,128]{3,2,1,0:T(8,128)S(1)}, f32[6,28,72,128]{3,2,1,0:T(8,128)S(1)}, f32[3,28,40,128]{3,2,1,0:T(8,128)S(1)}, f32[11,40,128]{2,1,0:T(8,128)S(1)}, f32[10,40,128]{2,1,0:T(8,128)S(1)}) custom-call(bf16[2,4,256,128]{3,2,1,0:T(8,128)(2,1)S(1)} %copy-done, ...), custom_call_target="tpu_custom_call", output_to_operand_aliasing={{0}: (3, {}), {1}: (4, {}), {2}: (5, {})} | custom-call | flops 1024 | bytes 1024 | tf_op jit(solution)/shard_map/pallas_call | solution.py:669
  29.0 0.1 collective-permute-start.5
  29.1 0.5 collective-permute-start.6
  29.6 1.3 %collective-permute-done.6.refs_3_ = f32[10,40,128]{2,1,0:T(8,128)S(1)} collective-permute-done((f32[10,40,128]{2,1,0:T(8,128)S(1)}, f32[10,40,128]{2,1,0:T(8,128)S(1)}, u32[]{:S(2)}, u32[]{:S(2)}) %collective-permute-start.6) | collective-permute-done | bytes 204832 | tf_op jit(solution)/shard_map/ppermute | solution.py:674
  30.9 0.0 collective-permute-done.5.refs_2_
  30.9 2.5 %shard_map.132 = (f32[3,28,72,128]{3,2,1,0:T(8,128)S(1)}, f32[6,28,72,128]{3,2,1,0:T(8,128)S(1)}, f32[3,28,40,128]{3,2,1,0:T(8,128)S(1)}, f32[21,40,128]{2,1,0:T(8,128)S(1)}) custom-call(bf16[2,4,256,128]{3,2,1,0:T(8,128)(2,1)S(1)} %copy-done, bf16[2,640,128]{2,1,0:T(8,128)(2,1)S(1)} %copy-done.1, ...), custom_call_target="tpu_custom_call", output_to_operand_aliasing={{0}: (4, {}), {1}: (5, {}), {2}: (6, {})} | custom-call | flops 1024 | bytes 1024 | tf_op jit(solution)/shard_map/pallas_call | solution.py:676
  33.4 1.9 %collective-permute-done.3.got_halo = f32[59,8,128]{2,1,0:T(8,128)S(1)} collective-permute-done((f32[59,8,128]{2,1,0:T(8,128)S(1)}, f32[59,8,128]{2,1,0:T(8,128)S(1)}, u32[]{:S(2)}, u32[]{:S(2)}) %collective-permute-start.3) | collective-permute-done | bytes 241696 | tf_op jit(solution)/shard_map/ppermute | solution.py:666
  35.3 0.0 collective-permute-done.got_own
  35.3 3.1 %shard_map.133 = (f32[3,28,72,128]{3,2,1,0:T(8,128)S(1)}, f32[6,28,72,128]{3,2,1,0:T(8,128)S(1)}, f32[3,28,40,128]{3,2,1,0:T(8,128)S(1)}, f32[216,8,128]{2,1,0:T(8,128)S(1)}) custom-call(bf16[2,4,256,128]{3,2,1,0:T(8,128)(2,1)S(1)} %copy-done, bf16[2,640,128]{2,1,0:T(8,128)(2,1)S(1)} %copy-done.1, ...), custom_call_target="tpu_custom_call", output_to_operand_aliasing={{0}: (4, {}), {1}: (5, {}), {2}: (6, {})} | custom-call | tf_op jit(solution)/shard_map/pallas_call | solution.py:680
  38.4 1.9 %collective-permute-start.7 = (f32[216,8,128]{2,1,0:T(8,128)S(1)}, f32[216,8,128]{2,1,0:T(8,128)S(1)}, u32[]{:S(2)}, u32[]{:S(2)}) collective-permute-start(f32[216,8,128]{2,1,0:T(8,128)S(1)} %get-tuple-element.66), channel_id=1, source_target_pairs={{32,64},{64,32},{33,65},{65,33},{34,66},{66,34},{35,67},{67,35},{3... | collective-permute-start | bytes 2654216 | tf_op jit(solution)/shard_map/ppermute | solution.py:666
  40.3 0.3 collective-permute-start.8
  40.6 1.8 %collective-permute-done.8.refs_2_ = f32[21,40,128]{2,1,0:T(8,128)S(1)} collective-permute-done((f32[21,40,128]{2,1,0:T(8,128)S(1)}, f32[21,40,128]{2,1,0:T(8,128)S(1)}, u32[]{:S(2)}, u32[]{:S(2)}) %collective-permute-start.8) | collective-permute-done | bytes 430112 | tf_op jit(solution)/shard_map/ppermute | solution.py:665
  42.4 0.0 copy-start.7
  42.4 0.0 copy-start.9
  42.4 3.0 %shard_map.134 = (f32[3,28,72,128]{3,2,1,0:T(8,128)S(1)}, f32[6,28,72,128]{3,2,1,0:T(8,128)S(1)}, f32[3,28,40,128]{3,2,1,0:T(8,128)S(1)}, f32[21,40,128]{2,1,0:T(8,128)S(1)}) custom-call(bf16[2,4,256,128]{3,2,1,0:T(8,128)(2,1)S(1)} %copy-done, bf16[2,640,128]{2,1,0:T(8,128)(2,1)S(1)} %copy-done.1, ...), custom_call_target="tpu_custom_call", output_to_operand_aliasing={{0}: (3, {}), {1}: (4, {}), {2}: (5, {})} | custom-call | flops 1024 | bytes 1024 | tf_op jit(solution)/shard_map/pallas_call | solution.py:669
  45.4 0.2 collective-permute-start.9
  46.9 0.3 collective-permute-done.9.got_ref
  47.2 0.0 copy-done.7
  47.2 0.0 copy-done.9
  47.2 0.0 copy-start.8
  47.2 0.0 copy-start.10
  47.2 0.0 copy-start.11
  47.3 4.2 %shard_map.135 = (f32[3,28,72,128]{3,2,1,0:T(8,128)S(1)}, f32[6,28,72,128]{3,2,1,0:T(8,128)S(1)}, f32[3,28,40,128]{3,2,1,0:T(8,128)S(1)}, f32[288,16,128]{2,1,0:...) custom-call(s32[1,64]{1,0:T(1,128)S(1)} %copy-done.9, ...), custom_call_target="tpu_custom_call", output_to_operand_aliasing={{0}: (6, {}), {1}: (7, {}), {2}: (8, {})} | custom-call | tf_op jit(solution)/shard_map/pallas_call | solution.py:685
  51.5 2.8 %collective-permute-done.7.got_ref = f32[216,8,128]{2,1,0:T(8,128)S(1)} collective-permute-done((f32[216,8,128]{2,1,0:T(8,128)S(1)}, f32[216,8,128]{2,1,0:T(8,128)S(1)}, u32[]{:S(2)}, u32[]{:S(2)}) %collective-permute-start.7) | collective-permute-done | bytes 884768 | tf_op jit(solution)/shard_map/ppermute | solution.py:666
  54.3 0.0 copy-done.8
  54.3 0.0 copy-done.10
  54.3 0.0 copy-done.11
  54.3 2.5 %shard_map.136 = (f32[3,28,72,128]{3,2,1,0:T(8,128)S(1)}, f32[6,28,72,128]{3,2,1,0:T(8,128)S(1)}, f32[3,28,40,128]{3,2,1,0:T(8,128)S(1)}, f32[8,128]{1,0:T(8,128)S(1)}) custom-call(s32[1]{0:T(128)S(6)} %copy.62.count_ref, f32[3,32]{1,0:T(4,128)S(1)} %copy-done.8, f32[1,32]{1,0:T(1,128)S(1)} %bitcast.19, ...), custom_call_target="tpu_custom_call", output_to_operand_aliasing={{0}: (7, {}), {1}: (8, {}), {2}: (9, {})} | custom-call | tf_op jit(solution)/shard_map/pallas_call | solution.py:692
  56.8 6.7 %all-gather = f32[32,128]{1,0:T(8,128)S(1)} all-gather(f32[8,128]{1,0:T(8,128)S(1)} %get-tuple-element.79), channel_id=2, replica_groups=mesh['region'=4,'tile'=32] {'region'}, dimensions={0}, use_global_device_ids=true | all-gather | bytes 20480 | tf_op jit(solution)/shard_map/all_gather | solution.py:697
  63.4 0.9 %collective-permute-start.10 = (f32[4,8,128]{2,1,0:T(8,128)S(1)}, f32[4,8,128]{2,1,0:T(8,128)S(1)}, u32[]{:S(2)}, u32[]{:S(2)}) collective-permute-start(f32[4,8,128]{2,1,0:T(8,128)S(1)} %bitcast.16), channel_id=1, source_target_pairs={{0,1},{1,0},{2,3},{3,2},{4,5},{5,4},{6,7},{7,6},{8,9},{9,8},{10,11... | collective-permute-start | bytes 49160 | tf_op jit(solution)/shard_map/ppermute | solution.py:698
  64.4 5.3 %collective-permute-start.11 = (f32[4,8,128]{2,1,0:T(8,128)S(1)}, f32[4,8,128]{2,1,0:T(8,128)S(1)}, u32[]{:S(2)}, u32[]{:S(2)}) collective-permute-start(f32[4,8,128]{2,1,0:T(8,128)S(1)} %bitcast.17), channel_id=1, source_target_pairs={{1,2},{2,1},{3,4},{4,3},{5,6},{6,5},{7,8},{8,7},{9,10},{10,9},{11,... | collective-permute-start | bytes 49160 | tf_op jit(solution)/shard_map/ppermute | solution.py:699
  69.6 1.9 %shard_map.137 = (f32[6,28,72,128]{3,2,1,0:T(8,128)S(1)}, f32[288,16,128]{2,1,0:T(8,128)}, f32[48,128]{1,0:T(8,128)S(1)}) custom-call(bf16[2,4,256,128]{3,2,1,0:T(8,128)(2,1)S(1)} %copy-done, bf16[2,640,128]{2,1,0:T(8,128)(2,1)S(1)} %copy-done.1, f32[4,8,128]{2,1,0:T(8,128)S(1)} %bitcast.18, ...), custom_call_target="tpu_custom_call", output_to_operand_aliasing={{0}: (5, {}), {1}: (7, {})} | custom-call | tf_op jit(solution)/shard_map/pallas_call | solution.py:700
  71.6 0.0 collective-permute-done.10.first_ref
  71.6 1.4 %collective-permute-done.11.second_ref = f32[4,8,128]{2,1,0:T(8,128)S(1)} collective-permute-done((f32[4,8,128]{2,1,0:T(8,128)S(1)}, f32[4,8,128]{2,1,0:T(8,128)S(1)}, u32[]{:S(2)}, u32[]{:S(2)}) %collective-permute-start.11) | collective-permute-done | bytes 16416 | tf_op jit(solution)/shard_map/ppermute | solution.py:699
  73.0 1.4 %shard_map.138 = f32[288,16,128]{2,1,0:T(8,128)} custom-call(f32[3,28,72,128]{3,2,1,0:T(8,128)S(1)} %get-tuple-element.78.v_ref, f32[4,8,128]{2,1,0:T(8,128)S(1)} %collective-permute-done.10.first_ref, f32[4,8,128]{2,1,0:T(8,128)S(1)} %collective-permute-done.11.second_ref, s32[8,128]{1,0:T(8,128)S(1)} %get-tuple-element.80.used_ref, ...), custom_call_target="tpu_custom_call", output_to_operand_aliasing={{}: (6, {})} | custom-call | tf_op jit(solution)/shard_map/pallas_call | solution.py:705
Async XLA Ops:
  0.0 12.4 %copy-start.3 = (f32[32,16,128]{2,1,0:T(8,128)S(1)}, f32[32,16,128]{2,1,0:T(8,128)}, u32[]{:S(2)}) copy-start(f32[32,16,128]{2,1,0:T(8,128)} %param.14) | copy-start | bytes 786436
  0.0 12.4 %copy-start.4 = (f32[32,16,128]{2,1,0:T(8,128)S(1)}, f32[32,16,128]{2,1,0:T(8,128)}, u32[]{:S(2)}) copy-start(f32[32,16,128]{2,1,0:T(8,128)} %param.15) | copy-start | bytes 786436
  0.0 12.4 %copy-start.5 = (f32[32,16,128]{2,1,0:T(8,128)S(1)}, f32[32,16,128]{2,1,0:T(8,128)}, u32[]{:S(2)}) copy-start(f32[32,16,128]{2,1,0:T(8,128)} %param.16) | copy-start | bytes 786436
  4.6 13.3 %collective-permute-start.2 = (f32[12,6,8,128]{3,2,1,0:T(8,128)}, f32[12,6,8,128]{3,2,1,0:T(8,128)S(1)}, u32[]{:S(2)}, u32[]{:S(2)}) collective-permute-start(f32[12,6,8,128]{3,2,1,0:T(8,128)} %get-tuple-element.49), channel_id=1, source_target_pairs={{0,1},{1,0},{2,3},{3,2},{4,5},{5,4},{6,7},{7,6},{8,9},{9,8},{10,11... | collective-permute-start | bytes 884744 | tf_op jit(solution)/shard_map/ppermute | solution.py:647
  6.0 13.7 %collective-permute-start.1 = (f32[12,6,8,128]{3,2,1,0:T(8,128)}, f32[12,6,8,128]{3,2,1,0:T(8,128)S(1)}, u32[]{:S(2)}, u32[]{:S(2)}) collective-permute-start(f32[12,6,8,128]{3,2,1,0:T(8,128)} %get-tuple-element.48), channel_id=1, source_target_pairs={{1,2},{2,1},{3,4},{4,3},{5,6},{6,5},{7,8},{8,7},{9,10},{10,9},{11,... | collective-permute-start | bytes 884744 | tf_op jit(solution)/shard_map/ppermute | solution.py:648
  12.4 1.7 %copy-start.2 = (f32[9,32,16,128]{3,2,1,0:T(8,128)S(1)}, f32[9,32,16,128]{3,2,1,0:T(8,128)}, u32[]{:S(2)}) copy-start(f32[9,32,16,128]{3,2,1,0:T(8,128)} %param.13) | copy-start | bytes 7077892
  14.1 0.7 copy-start.6
  16.0 19.3 %collective-permute-start = (f32[59,32,128]{2,1,0:T(8,128)S(1)}, f32[59,32,128]{2,1,0:T(8,128)S(1)}, u32[]{:S(2)}, u32[]{:S(2)}) collective-permute-start(f32[59,32,128]{2,1,0:T(8,128)S(1)} %get-tuple-element.47), channel_id=1, source_target_pairs={{32,64},{64,32},{33,65},{65,33},{34,66},{66,34},{35,67},{67,35},{3... | collective-permute-start | bytes 2899976 | tf_op jit(solution)/shard_map/ppermute | solution.py:653
  19.7 5.0 %copy-start = (bf16[2,4,256,128]{3,2,1,0:T(8,128)(2,1)S(1)}, bf16[2,4,256,128]{3,2,1,0:T(8,128)(2,1)}, u32[]{:S(2)}) copy-start(bf16[2,4,256,128]{3,2,1,0:T(8,128)(2,1)} %constant.4.clone.refs_0_.own_ref) | copy-start | bytes 1572868
  19.7 5.0 %copy-start.1 = (bf16[2,640,128]{2,1,0:T(8,128)(2,1)S(1)}, bf16[2,640,128]{2,1,0:T(8,128)(2,1)}, u32[]{:S(2)}) copy-start(bf16[2,640,128]{2,1,0:T(8,128)(2,1)} %constant.5.clone.refs_1_.halo_ref) | copy-start | bytes 983044
  20.0 4.6 %collective-permute-start.4 = (f32[23,40,128]{2,1,0:T(8,128)S(1)}, f32[23,40,128]{2,1,0:T(8,128)S(1)}, u32[]{:S(2)}, u32[]{:S(2)}) collective-permute-start(f32[23,40,128]{2,1,0:T(8,128)S(1)} %get-tuple-element.54), channel_id=1, source_target_pairs={{0,32},{32,0},{64,96},{96,64},{1,33},{33,1},{65,97},{97,65},{2,34}... | collective-permute-start | bytes 1413128 | tf_op jit(solution)/shard_map/ppermute | solution.py:665
  20.1 15.2 %collective-permute-start.3 = (f32[59,8,128]{2,1,0:T(8,128)S(1)}, f32[59,8,128]{2,1,0:T(8,128)S(1)}, u32[]{:S(2)}, u32[]{:S(2)}) collective-permute-start(f32[59,8,128]{2,1,0:T(8,128)S(1)} %get-tuple-element.53), channel_id=1, source_target_pairs={{32,64},{64,32},{33,65},{65,33},{34,66},{66,34},{35,67},{67,35},{3... | collective-permute-start | bytes 725000 | tf_op jit(solution)/shard_map/ppermute | solution.py:666
  29.0 1.9 %collective-permute-start.5 = (f32[11,40,128]{2,1,0:T(8,128)S(1)}, f32[11,40,128]{2,1,0:T(8,128)S(1)}, u32[]{:S(2)}, u32[]{:S(2)}) collective-permute-start(f32[11,40,128]{2,1,0:T(8,128)S(1)} %get-tuple-element.58), channel_id=1, source_target_pairs={{0,32},{32,0},{64,96},{96,64},{1,33},{33,1},{65,97},{97,65},{2,34}... | collective-permute-start | bytes 675848 | tf_op jit(solution)/shard_map/ppermute | solution.py:674
  29.1 1.8 %collective-permute-start.6 = (f32[10,40,128]{2,1,0:T(8,128)S(1)}, f32[10,40,128]{2,1,0:T(8,128)S(1)}, u32[]{:S(2)}, u32[]{:S(2)}) collective-permute-start(f32[10,40,128]{2,1,0:T(8,128)S(1)} %get-tuple-element.59), channel_id=1, source_target_pairs={{0,32},{32,0},{64,96},{96,64},{1,33},{33,1},{65,97},{97,65},{2,34}... | collective-permute-start | bytes 614408 | tf_op jit(solution)/shard_map/ppermute | solution.py:674
  38.4 15.9 %collective-permute-start.7 = (f32[216,8,128]{2,1,0:T(8,128)S(1)}, f32[216,8,128]{2,1,0:T(8,128)S(1)}, u32[]{:S(2)}, u32[]{:S(2)}) collective-permute-start(f32[216,8,128]{2,1,0:T(8,128)S(1)} %get-tuple-element.66), channel_id=1, source_target_pairs={{32,64},{64,32},{33,65},{65,33},{34,66},{66,34},{35,67},{67,35},{3... | collective-permute-start | bytes 2654216 | tf_op jit(solution)/shard_map/ppermute | solution.py:666
  40.3 2.0 %collective-permute-start.8 = (f32[21,40,128]{2,1,0:T(8,128)S(1)}, f32[21,40,128]{2,1,0:T(8,128)S(1)}, u32[]{:S(2)}, u32[]{:S(2)}) collective-permute-start(f32[21,40,128]{2,1,0:T(8,128)S(1)} %get-tuple-element.67), channel_id=1, source_target_pairs={{0,32},{32,0},{64,96},{96,64},{1,33},{33,1},{65,97},{97,65},{2,34}... | collective-permute-start | bytes 1290248 | tf_op jit(solution)/shard_map/ppermute | solution.py:665
  42.4 4.9 %copy-start.7 = (f32[3,32]{1,0:T(4,128)S(1)}, f32[3,32]{1,0:T(4,128)}, u32[]{:S(2)}) copy-start(f32[3,32]{1,0:T(4,128)} %profile_ref.1) | copy-start | bytes 1156
  42.4 4.9 %copy-start.9 = (s32[1,64]{1,0:T(1,128)S(1)}, s32[1,64]{1,0:T(1,128)}, u32[]{:S(2)}) copy-start(s32[1,64]{1,0:T(1,128)} %influence_ref.1) | copy-start | bytes 772
  45.4 1.9 %collective-permute-start.9 = (f32[21,40,128]{2,1,0:T(8,128)S(1)}, f32[21,40,128]{2,1,0:T(8,128)S(1)}, u32[]{:S(2)}, u32[]{:S(2)}) collective-permute-start(f32[21,40,128]{2,1,0:T(8,128)S(1)} %get-tuple-element.71), channel_id=1, source_target_pairs={{0,32},{32,0},{64,96},{96,64},{1,33},{33,1},{65,97},{97,65},{2,34}... | collective-permute-start | bytes 1290248 | tf_op jit(solution)/shard_map/ppermute | solution.py:674
  47.2 7.0 %copy-start.8 = (f32[3,32]{1,0:T(4,128)S(1)}, f32[3,32]{1,0:T(4,128)}, u32[]{:S(2)}) copy-start(f32[3,32]{1,0:T(4,128)} %observed_ref.1) | copy-start | bytes 1156
  47.2 7.0 %copy-start.10 = (f32[32]{0:T(128)S(1)}, f32[32]{0:T(128)}, u32[]{:S(2)}) copy-start(f32[32]{0:T(128)} %param.18) | copy-start | bytes 388
  47.2 7.0 %copy-start.11 = (s32[32]{0:T(128)S(1)}, s32[32]{0:T(128)}, u32[]{:S(2)}) copy-start(s32[32]{0:T(128)} %param.20) | copy-start | bytes 388
  63.4 8.1 %collective-permute-start.10 = (f32[4,8,128]{2,1,0:T(8,128)S(1)}, f32[4,8,128]{2,1,0:T(8,128)S(1)}, u32[]{:S(2)}, u32[]{:S(2)}) collective-permute-start(f32[4,8,128]{2,1,0:T(8,128)S(1)} %bitcast.16), channel_id=1, source_target_pairs={{0,1},{1,0},{2,3},{3,2},{4,5},{5,4},{6,7},{7,6},{8,9},{9,8},{10,11... | collective-permute-start | bytes 49160 | tf_op jit(solution)/shard_map/ppermute | solution.py:698
  64.4 8.6 %collective-permute-start.11 = (f32[4,8,128]{2,1,0:T(8,128)S(1)}, f32[4,8,128]{2,1,0:T(8,128)S(1)}, u32[]{:S(2)}, u32[]{:S(2)}) collective-permute-start(f32[4,8,128]{2,1,0:T(8,128)S(1)} %bitcast.17), channel_id=1, source_target_pairs={{1,2},{2,1},{3,4},{4,3},{5,6},{6,5},{7,8},{8,7},{9,10},{10,9},{11,... | collective-permute-start | bytes 49160 | tf_op jit(solution)/shard_map/ppermute | solution.py:699

commit v6 on v5

--- a/solution.py
+++ b/solution.py
@@ -50,29 +50,28 @@
 
 def band_matrices():
     taps = {0: ((-1, 1), (0, -27), (1, 27), (2, -1)), 1: ((-2, 1), (-1, -27), (0, 27), (1, -1))}
-    own = np.zeros((2, GROUPS, 256, 128), np.float32)
-    halo = np.zeros((2, 640, 128), np.float32)
+    band = np.zeros((2, GROUPS, 256, 256), np.float32)
     for k in range(2):
         for offset, coef in taps[k]:
             for g in range(GROUPS):
                 for lane in range(128):
                     y = lane + offset
                     if 0 <= y < CY:
-                        own[k, g, y, lane] += coef
+                        band[k, g, y, lane] += coef
                     else:
-                        own[k, g, 128 + 32 * g + HALF + (y if y < 0 else y - CY), lane] += coef
+                        band[k, g, 128 + 32 * g + HALF + (y if y < 0 else y - CY), lane] += coef
                 for spot in range(32):
                     to = spot + offset
-                    out = 32 * g + spot
+                    out = 128 + 32 * g + spot
                     if not 0 <= to < 32:
                         continue
                     if (spot < HALF) == (to < HALF):
-                        halo[k, 512 + 32 * g + to, out] += coef
+                        band[k, g, 128 + 32 * g + to, out] += coef
                     elif spot < HALF:
-                        halo[k, 128 * g + to - HALF, out] += coef
+                        band[k, g, to - HALF, out] += coef
                     else:
-                        halo[k, 128 * g + CY + to - HALF, out] += coef
-    return own, halo
+                        band[k, g, CY + to - HALF, out] += coef
+    return band
 
 
 def two_terms(value):
@@ -80,28 +79,26 @@
     return high, (value - high.astype(jnp.float32)).astype(jnp.bfloat16)
 
 
-def y_differences(items, count, forward, own_ref, halo_ref, out_ref):
-    k = 0 if forward else 1
+def y_differences(items, count, forward, band_ref, out_ref):
     even = count + count % 2
+    size = 8 * even * len(items)
 
     def rows(at):
-        return jnp.concatenate(
+        value = jnp.concatenate(
             [ref[f, x + j, at:at + 8, :] for ref, f, x, _ in items for j in range(even)], axis=0)
-
-    parts = [two_terms(rows(8 + 8 * g)) for g in range(GROUPS)] + [two_terms(rows(56))]
-
-    def product(lhs, rhs):
-        return jnp.dot(lhs, rhs, preferred_element_type=jnp.float32)
-
+        return jnp.concatenate(two_terms(value), axis=0)
+
+    halo = rows(56)
+    halo_out = None
     for g in range(GROUPS + 1):
-        total = 0.0
-        for term in range(2):
-            if g < GROUPS:
-                lhs = jnp.concatenate([parts[g][term], parts[GROUPS][term]], axis=1)
-                total += product(lhs, own_ref[k, g])
-            else:
-                lhs = jnp.concatenate([parts[n][term] for n in range(GROUPS + 1)], axis=1)
-                total += product(lhs, halo_ref[k])
+        if g < GROUPS:
+            both = jnp.dot(jnp.concatenate([rows(8 + 8 * g), halo], axis=1),
+                           band_ref[0 if forward else 1, g], preferred_element_type=jnp.float32)
+            total = both[:size, :128] + both[size:, :128]
+            part = both[:size, 128:] + both[size:, 128:]
+            halo_out = part if g == 0 else halo_out + part
+        else:
+            total = halo_out
         for n, (_, _, _, slot) in enumerate(items):
             for j in range(count):
                 r = 8 * (n * even + j)
@@ -139,10 +136,10 @@
     return combine(*[load(ref, f, x, first + k) for k in range(4)])
 
 
-def velocity_pass(v_ref, t_ref, p_ref, own_ref, halo_ref, d_ref, x_first, y_first, count):
+def velocity_pass(v_ref, t_ref, p_ref, band_ref, d_ref, x_first, y_first, count):
     xa, ya = x_first + LOW, y_first + LOW
-    y_differences([(t_ref, SXY, xa, 0), (t_ref, SYZ, ya, 2)], count, False, own_ref, halo_ref, d_ref)
-    y_differences([(t_ref, SYY, ya, 1)], count, True, own_ref, halo_ref, d_ref)
+    y_differences([(t_ref, SXY, xa, 0), (t_ref, SYZ, ya, 2)], count, False, band_ref, d_ref)
+    y_differences([(t_ref, SYY, ya, 1)], count, True, band_ref, d_ref)
 
     def body(j, _):
         x = xa + j
@@ -163,10 +160,10 @@
         pad_halo(v_ref, VZ, ya + j)
 
 
-def stress_pass(v_ref, t_ref, p_ref, own_ref, halo_ref, d_ref, first, count, pads=True):
+def stress_pass(v_ref, t_ref, p_ref, band_ref, d_ref, first, count, pads=True):
     a = first + LOW
-    y_differences([(v_ref, VX, a, 0), (v_ref, VZ, a, 2)], count, True, own_ref, halo_ref, d_ref)
-    y_differences([(v_ref, VY, a, 1)], count, False, own_ref, halo_ref, d_ref)
+    y_differences([(v_ref, VX, a, 0), (v_ref, VZ, a, 2)], count, True, band_ref, d_ref)
+    y_differences([(v_ref, VY, a, 1)], count, False, band_ref, d_ref)
 
     def body(j, _):
         x = a + j
@@ -438,14 +435,14 @@
     lax.fori_loop(LOW, LOW + CX, pads, 0)
 
 
-def near_step(items, back, odd, read, v_ref, t_ref, p_ref, own_ref, halo_ref, d_ref):
+def near_step(items, back, odd, read, v_ref, t_ref, p_ref, band_ref, d_ref):
     take_halo(items, odd, True, read, v_ref, t_ref, p_ref)
-    mats = (v_ref, t_ref, p_ref, own_ref, halo_ref, d_ref)
+    mats = (v_ref, t_ref, p_ref, band_ref, d_ref)
     velocity_pass(*mats, jnp.where(odd, -2, back + 1), jnp.where(odd, -1, back + 2), CX - back)
     stress_pass(*mats, jnp.where(odd, 0, back + 3), CX - 3 - back)
 
 
-def near_kernel(items, back, gots, gives, own_ref, halo_ref, *refs):
+def near_kernel(items, back, gots, gives, band_ref, *refs):
     got_refs, refs = refs[:gots], refs[gots + 3:]
     v_ref, t_ref, p_ref = refs[:3]
     send_refs, d_ref = refs[3:3 + gives], refs[-1]
@@ -457,7 +454,7 @@
         part = plane_count(INNER[:4])
         return got_refs[0][n] if gots == 1 or n < part else got_refs[1][n - part]
 
-    near_step(items, back, odd, read, v_ref, t_ref, p_ref, own_ref, halo_ref, d_ref)
+    near_step(items, back, odd, read, v_ref, t_ref, p_ref, band_ref, d_ref)
     if gives == 1:
         give_halo(INNER, odd, True, send_refs[0], v_ref, t_ref, p_ref)
     else:
@@ -480,10 +477,10 @@
     return copy
 
 
-def last_near_kernel(influence_ref, count_ref, profile_ref, own_ref, halo_ref, got_ref, v_in, t_in,
+def last_near_kernel(influence_ref, count_ref, profile_ref, band_ref, got_ref, v_in, t_in,
                      p_in, v_ref, t_ref, p_ref, out_ref, used_ref, profile_rows, d_ref, rows_ref, sem):
     odd = is_odd()
-    near_step(INNER, 3, odd, lambda n: got_ref[n], v_ref, t_ref, p_ref, own_ref, halo_ref, d_ref)
+    near_step(INNER, 3, odd, lambda n: got_ref[n], v_ref, t_ref, p_ref, band_ref, d_ref)
     copy = stress_half(jnp.where(odd, 0, 8), t_ref, out_ref, rows_ref, sem)
     lane = lanes(8)
     column = lax.broadcasted_iota(jnp.int32, (8, 128), 0) + lax.axis_index("tile") - 1
@@ -500,9 +497,9 @@
     copy.wait()
 
 
-def far_steps(items, last, odd, read, v_ref, t_ref, p_ref, own_ref, halo_ref, d_ref):
+def far_steps(items, last, odd, read, v_ref, t_ref, p_ref, band_ref, d_ref):
     take_halo(items, odd, False, read, v_ref, t_ref, p_ref)
-    mats = (v_ref, t_ref, p_ref, own_ref, halo_ref, d_ref)
+    mats = (v_ref, t_ref, p_ref, band_ref, d_ref)
     velocity_pass(*mats, jnp.where(odd, 14, -5), jnp.where(odd, 15, -4), 6)
     stress_pass(*mats, jnp.where(odd, 13, -3), 6)
     velocity_pass(*mats, jnp.where(odd, 11, -2), jnp.where(odd, 12, -1), 6)
@@ -510,17 +507,17 @@
         stress_pass(*mats, jnp.where(odd, 10, 0), 6)
 
 
-def far_kernel(own_ref, halo_ref, got_own, got_halo, v_in, t_in, p_in, v_ref, t_ref, p_ref,
+def far_kernel(band_ref, got_own, got_halo, v_in, t_in, p_in, v_ref, t_ref, p_ref,
                outer_ref, d_ref):
     odd = is_odd()
-    far_steps(OUTER_FIRST, False, odd, read_first(got_own, got_halo), v_ref, t_ref, p_ref, own_ref, halo_ref, d_ref)
+    far_steps(OUTER_FIRST, False, odd, read_first(got_own, got_halo), v_ref, t_ref, p_ref, band_ref, d_ref)
     give_second(odd, outer_ref, v_ref, t_ref, p_ref)
 
 
-def station_kernel(count_ref, observed_ref, gain_ref, cell_ref, own_ref, halo_ref,
+def station_kernel(count_ref, observed_ref, gain_ref, cell_ref, band_ref,
                    got_ref, v_in, t_in, p_in, v_ref, t_ref, p_ref, packet_ref, d_ref, slot_ref):
     odd = is_odd()
-    far_steps(OUTER, True, odd, read_second(got_ref), v_ref, t_ref, p_ref, own_ref, halo_ref, d_ref)
+    far_steps(OUTER, True, odd, read_second(got_ref), v_ref, t_ref, p_ref, band_ref, d_ref)
     slot_ref[...] = jnp.zeros((16, 128), jnp.float32)
     slot_ref[0:3, 0:S] = observed_ref[...]
     slot_ref[3:4, 0:S] = gain_ref[...]
@@ -566,10 +563,10 @@
     return cell_x, cell_y
 
 
-def stress_out_kernel(own_ref, halo_ref, here_ref, used_ref, v_ref, t_in, p_ref, out_in, t_ref,
+def stress_out_kernel(band_ref, here_ref, used_ref, v_ref, t_in, p_ref, out_in, t_ref,
                       out_ref, own_part, d_ref, rows_ref, sem):
     odd = is_odd()
-    stress_pass(v_ref, t_ref, p_ref, own_ref, halo_ref, d_ref, jnp.where(odd, 10, 0), 6, pads=False)
+    stress_pass(v_ref, t_ref, p_ref, band_ref, d_ref, jnp.where(odd, 10, 0), 6, pads=False)
     copy = stress_half(jnp.where(odd, 8, 0), t_ref, out_ref, rows_ref, sem)
     own_part[...] = tile_column(here_ref, used_ref[1:2], *cell_places())
     copy.wait()
@@ -633,8 +630,7 @@
 
 def per_device(fields, buoyancy, lame_first, shear_modulus, observed, station_weight, depth_profile,
                station_cell, station_count, influence, influence_count):
-    own, edge = band_matrices()
-    own, edge = jnp.asarray(own, jnp.bfloat16), jnp.asarray(edge, jnp.bfloat16)
+    band = jnp.asarray(band_matrices(), jnp.bfloat16)
     size = NZ * CX
     state = (struct(3, PLANES, ZROWS, 128), struct(6, PLANES, ZROWS, 128),
              struct(3, PLANES, DEPTH, 128))
@@ -659,7 +655,7 @@
     )(got_second, half, v, t, p)
     inner_struct = struct(plane_count(INNER), DEPTH, 128)
     d_scratch = pltpu.VMEM((3, CX, DEPTH, 128), jnp.float32)
-    alias = {3: 0, 4: 1, 5: 2}
+    alias = {2: 0, 3: 1, 4: 2}
     result = struct(9 * NZ, CX, 128)
     for block in range(2):
         got = lax.ppermute(inner, "region", INNER_SWAP)
@@ -668,40 +664,40 @@
         parts = (INNER[:4], INNER[4:]) if block == 0 else (INNER,)
         v, t, p, *inner = call(
             bind(near_kernel, INNER_FIRST if block == 0 else INNER, 0, 1, split),
-            state + tuple(struct(plane_count(part), DEPTH, 128) for part in parts), [VM] * 6,
+            state + tuple(struct(plane_count(part), DEPTH, 128) for part in parts), [VM] * 5,
             [d_scratch], aliases=alias, cost=FREE,
-        )(own, edge, got, v, t, p)
+        )(band, got, v, t, p)
         got = [lax.ppermute(part, "region", INNER_SWAP) for part in inner]
         if block == 0:
             v, t, p, inner = call(
-                bind(near_kernel, INNER, 3, 2, 1), state + (inner_struct,), [VM] * 7,
-                [d_scratch], aliases={4: 0, 5: 1, 6: 2}, cost=FREE,
-            )(own, edge, *got, v, t, p)
+                bind(near_kernel, INNER, 3, 2, 1), state + (inner_struct,), [VM] * 6,
+                [d_scratch], aliases={3: 0, 4: 1, 5: 2}, cost=FREE,
+            )(band, *got, v, t, p)
             v, t, p, outer = call(
                 far_kernel, state + (struct(4 * plane_count(OUTER) + plane_count(OUTER) // 2, 8, 128),),
-                [VM] * 7, [d_scratch], aliases={4: 0, 5: 1, 6: 2},
-            )(own, edge, got_own, got_outer, v, t, p)
+                [VM] * 6, [d_scratch], aliases={3: 0, 4: 1, 5: 2},
+            )(band, got_own, got_outer, v, t, p)
         else:
             v, t, p, out, used, profile_rows = call(
                 last_near_kernel,
                 state + (result, jax.ShapeDtypeStruct((8, 128), jnp.int32), struct(3, NZ, 128)),
-                [SM] * 3 + [VM] * 6,
+                [SM] * 3 + [VM] * 5,
                 [d_scratch, pltpu.VMEM((6 * NZ, 8, 128), jnp.float32), pltpu.SemaphoreType.DMA],
-                out_specs=[VM] * 3 + [HB] + [VM] * 2, aliases={6: 0, 7: 1, 8: 2},
-            )(influence, influence_count, depth_profile, own, edge, *got, v, t, p)
+                out_specs=[VM] * 3 + [HB] + [VM] * 2, aliases={5: 0, 6: 1, 7: 2},
+            )(influence, influence_count, depth_profile, band, *got, v, t, p)
     v, t, p, packet = call(
-        station_kernel, state + (struct(8, 128),), [SM] + [VM] * 9,
-        [d_scratch, pltpu.VMEM((16, 128), jnp.float32)], aliases={7: 0, 8: 1, 9: 2},
+        station_kernel, state + (struct(8, 128),), [SM] + [VM] * 8,
+        [d_scratch, pltpu.VMEM((16, 128), jnp.float32)], aliases={6: 0, 7: 1, 8: 2},
     )(station_count, observed, station_weight.reshape(1, S), station_cell.reshape(1, S),
-      own, edge, got_outer, v, t, p)
+      band, got_outer, v, t, p)
     here = lax.all_gather(packet, "region")
     got_first = lax.ppermute(here, "tile", pairs(0))
     got_second = lax.ppermute(here, "tile", pairs(1))
     _, out, own_part = call(
-        stress_out_kernel, (state[1], result, struct(3 * CX, CY)), [VM] * 7 + [HB],
+        stress_out_kernel, (state[1], result, struct(3 * CX, CY)), [VM] * 6 + [HB],
         [d_scratch, pltpu.VMEM((6 * NZ, 8, 128), jnp.float32), pltpu.SemaphoreType.DMA],
-        out_specs=[VM, HB, VM], aliases={5: 0, 7: 1},
-    )(own, edge, here, used, v, t, p, out)
+        out_specs=[VM, HB, VM], aliases={4: 0, 6: 1},
+    )(band, here, used, v, t, p, out)
     out, = call(
         increment_kernel, (result,), [VM] * 6 + [HB],
         [pltpu.VMEM((3 * NZ, CX, 128), jnp.float32), pltpu.SemaphoreType.DMA((3,))],

time: 74.9 us -> 73.2 us (0.977)
  Pallas kernels: 30.2 us -> 27.5 us
  waiting for transfers between devices: 10.2 us -> 12.2 us
  starting transfers between devices: 23.5 us -> 22.5 us
    ppermute x2, waiting for transfers between devices: 4.68 us -> 6.58 us  [per_device(): got_outer = lax.ppermute(outer, 'region', OUTER_SWAP)]
    pallas_call x2, Pallas kernels: 7.33 us -> 6.32 us  [per_device(): call(bind(near_kernel, INNER_FIRST if block == 0 else INNER, 0, 1, split)...]
    ppermute x1, starting transfers between devices: 0.93 us -> 0.01 us  [per_device(): got_first = lax.ppermute(here, 'tile', pairs(0))]
    pallas_call x3, Pallas kernels: 6.94 us -> 6.15 us  [the longest x1 2.22 us: per_device(): call(station_kernel, state + (struct(8, 128),), [SM] + [VM] * 8, [d_scrat...]
    unnamed x24 -> x22, local copies, waits for them, and re-layouts: 2.37 us -> 2.37 us
  transfers between devices with their start and end apart: 12 -> 12, of which waited for: 7 -> 7; matrix products, arithmetic and copies ran while one was open for 0% -> 0% of each run, Pallas kernels for 25% -> 23%
where the time goes in v6:
time: 73.2 us; the launch traced here: 72.9 us
  Pallas kernels  27.5 us (38%)
  starting transfers between devices  22.5 us (31%)
  waiting for transfers between devices  12.2 us (17%)
  blocking collectives  6.68 us (9%)
  local copies, waits for them, and re-layouts  2.37 us (3%)
  between operations  1.69 us (2%)
    all_gather x1, blocking collectives, per_device(): here = lax.all_gather(packet, 'region')  6.68 us
    ppermute x2, waiting for transfers between devices, per_device(): got_outer = lax.ppermute(outer, 'region', OUTER_SWAP)  6.58 us
    ppermute x2, starting transfers between devices, per_device(): got_outer = lax.ppermute(outer, 'region', OUTER_SWAP)  6.47 us
    ppermute x1, starting transfers between devices, per_device(): got_second = lax.ppermute(second, 'tile', pairs(1))  6.38 us
    pallas_call x2, Pallas kernels, per_device(): call(bind(near_kernel, INNER_FIRST if block == 0 else INNER, 0, 1, split)...  6.32 us
    ppermute x1, starting transfers between devices, per_device(): got_second = lax.ppermute(here, 'tile', pairs(1))  5.22 us
    pallas_call x1, Pallas kernels, per_device(): call(edge_kernel, (packed, packed, struct(8, 128)), [HB] * 4, fetched, vm...  4.61 us
    pallas_call x1, Pallas kernels, per_device(): call(last_near_kernel, state + (result, jax.ShapeDtypeStruct((8, 128), jn...  3.76 us
  transfers between devices with their start and end apart: 12, of which 7 were waited for; matrix products, arithmetic and copies ran while one was open for 0% of the time, Pallas kernels for 23%

profile of v6, /device:TPU:22, one launch (start us, length us, event | category | flops | bytes accessed | tf_op | source)
XLA Modules:
  0.0 72.9 jit_solution(14827522809152902308)
XLA Ops:
  0.0 0.0 copy-start.2
  0.0 0.0 copy-start.3
  0.0 0.0 copy-start.4
  0.0 4.6 %shard_map.118 = (f32[12,6,8,128]{3,2,1,0:T(8,128)}, f32[12,6,8,128]{3,2,1,0:T(8,128)}, f32[8,128]{1,0:T(8,128)}) custom-call(f32[4608,128]{1,0:T(8,128)} %bitcast.8, f32[512,128]{1,0:T(8,128)} %bitcast.10, f32[512,128]{1,0:T(8,128)} %bitcast.12, f32[512,128]{1,0:T(8,128)} %bitcast.14), custom_call_target="tpu_custom_call" | custom-call | tf_op jit(solution)/shard_map/pallas_call | solution.py:641
  4.6 1.4 %collective-permute-start.2 = (f32[12,6,8,128]{3,2,1,0:T(8,128)}, f32[12,6,8,128]{3,2,1,0:T(8,128)S(1)}, u32[]{:S(2)}, u32[]{:S(2)}) collective-permute-start(f32[12,6,8,128]{3,2,1,0:T(8,128)} %get-tuple-element.49), channel_id=1, source_target_pairs={{0,1},{1,0},{2,3},{3,2},{4,5},{5,4},{6,7},{7,6},{8,9},{9,8},{10,11... | collective-permute-start | bytes 884744 | tf_op jit(solution)/shard_map/ppermute | solution.py:643
  6.0 6.4 %collective-permute-start.1 = (f32[12,6,8,128]{3,2,1,0:T(8,128)}, f32[12,6,8,128]{3,2,1,0:T(8,128)S(1)}, u32[]{:S(2)}, u32[]{:S(2)}) collective-permute-start(f32[12,6,8,128]{3,2,1,0:T(8,128)} %get-tuple-element.48), channel_id=1, source_target_pairs={{1,2},{2,1},{3,4},{4,3},{5,6},{6,5},{7,8},{8,7},{9,10},{10,9},{11,... | collective-permute-start | bytes 884744 | tf_op jit(solution)/shard_map/ppermute | solution.py:644
  12.4 0.0 copy-done.2
  12.4 0.0 copy-done.3
  12.4 0.0 copy-done.4
  12.4 0.0 copy-start.1
  12.4 1.7 %copy-done.1 = f32[9,32,16,128]{3,2,1,0:T(8,128)S(1)} copy-done((f32[9,32,16,128]{3,2,1,0:T(8,128)S(1)}, f32[9,32,16,128]{3,2,1,0:T(8,128)}, u32[]{:S(2)}) %copy-start.1) | copy-done | bytes 2359320
  14.1 0.0 copy-start.5
  14.1 0.7 copy-done.5
  14.8 1.2 %shard_map.119 = (f32[3,28,72,128]{3,2,1,0:T(8,128)S(1)}, f32[6,28,72,128]{3,2,1,0:T(8,128)S(1)}, f32[3,28,40,128]{3,2,1,0:T(8,128)S(1)}, f32[59,32,128]{2,1,0:T(8,128)S(1)}) custom-call(f32[4608,128]{1,0:T(8,128)S(1)} %bitcast.9, f32[512,128]{1,0:T(8,128)S(1)} %bitcast.11, f32[512,128]{1,0:T(8,128)S(1)} %bitcast.13, f32[512,128]{1,0:T(8,128)S(1)} %bitcast.15, ...), custom_call_target="tpu_custom_call" | custom-call | bytes 100000000 | tf_op jit(solution)/shard_map/pallas_call | solution.py:646
  16.0 1.9 %collective-permute-start = (f32[59,32,128]{2,1,0:T(8,128)S(1)}, f32[59,32,128]{2,1,0:T(8,128)S(1)}, u32[]{:S(2)}, u32[]{:S(2)}) collective-permute-start(f32[59,32,128]{2,1,0:T(8,128)S(1)} %get-tuple-element.47), channel_id=1, source_target_pairs={{32,64},{64,32},{33,65},{65,33},{34,66},{66,34},{35,67},{67,35},{3... | collective-permute-start | bytes 2899976 | tf_op jit(solution)/shard_map/ppermute | solution.py:649
  17.9 0.0 collective-permute-done.2.got_ref
  17.9 1.1 %shard_map.120.half_ref = f32[12,2,8,8,128]{4,3,2,1,0:T(8,128)S(1)} custom-call(f32[12,6,8,128]{3,2,1,0:T(8,128)S(1)} %collective-permute-done.2.got_ref), custom_call_target="tpu_custom_call" | custom-call | tf_op jit(solution)/shard_map/pallas_call | solution.py:650
  19.0 0.7 collective-permute-done.1.got_ref
  19.7 0.0 copy-start
  19.7 0.3 shard_map.121
  20.0 0.1 collective-permute-start.4
  20.1 4.5 %collective-permute-start.3 = (f32[59,8,128]{2,1,0:T(8,128)S(1)}, f32[59,8,128]{2,1,0:T(8,128)S(1)}, u32[]{:S(2)}, u32[]{:S(2)}) collective-permute-start(f32[59,8,128]{2,1,0:T(8,128)S(1)} %get-tuple-element.53), channel_id=1, source_target_pairs={{32,64},{64,32},{33,65},{65,33},{34,66},{66,34},{35,67},{67,35},{3... | collective-permute-start | bytes 725000 | tf_op jit(solution)/shard_map/ppermute | solution.py:662
  24.6 0.0 collective-permute-done.4.refs_1_
  24.6 0.0 copy-done
  24.7 3.8 %shard_map.122 = (f32[3,28,72,128]{3,2,1,0:T(8,128)S(1)}, f32[6,28,72,128]{3,2,1,0:T(8,128)S(1)}, f32[3,28,40,128]{3,2,1,0:T(8,128)S(1)}, f32[11,40,128]{2,1,0:T(8,128)S(1)}, f32[10,40,128]{2,1,0:T(8,128)S(1)}) custom-call(bf16[2,4,256,256]{3,2,1,0:T(8,128)(2,1)S(1)} %copy-done, ...), custom_call_target="tpu_custom_call", output_to_operand_aliasing={{0}: (2, {}), {1}: (3, {}), {2}: (4, {})} | custom-call | flops 1024 | bytes 1024 | tf_op jit(solution)/shard_map/pallas_call | solution.py:665
  28.5 0.1 collective-permute-start.5
  28.6 0.5 collective-permute-start.6
  29.1 1.3 %collective-permute-done.6.refs_2_ = f32[10,40,128]{2,1,0:T(8,128)S(1)} collective-permute-done((f32[10,40,128]{2,1,0:T(8,128)S(1)}, f32[10,40,128]{2,1,0:T(8,128)S(1)}, u32[]{:S(2)}, u32[]{:S(2)}) %collective-permute-start.6) | collective-permute-done | bytes 204832 | tf_op jit(solution)/shard_map/ppermute | solution.py:670
  30.3 0.0 collective-permute-done.5.refs_1_
  30.3 2.1 %shard_map.123 = (f32[3,28,72,128]{3,2,1,0:T(8,128)S(1)}, f32[6,28,72,128]{3,2,1,0:T(8,128)S(1)}, f32[3,28,40,128]{3,2,1,0:T(8,128)S(1)}, f32[21,40,128]{2,1,0:T(8,128)S(1)}) custom-call(bf16[2,4,256,256]{3,2,1,0:T(8,128)(2,1)S(1)} %copy-done, ...), custom_call_target="tpu_custom_call", output_to_operand_aliasing={{0}: (3, {}), {1}: (4, {}), {2}: (5, {})} | custom-call | flops 1024 | bytes 1024 | tf_op jit(solution)/shard_map/pallas_call | solution.py:672
  32.4 2.9 %collective-permute-done.3.got_halo = f32[59,8,128]{2,1,0:T(8,128)S(1)} collective-permute-done((f32[59,8,128]{2,1,0:T(8,128)S(1)}, f32[59,8,128]{2,1,0:T(8,128)S(1)}, u32[]{:S(2)}, u32[]{:S(2)}) %collective-permute-start.3) | collective-permute-done | bytes 241696 | tf_op jit(solution)/shard_map/ppermute | solution.py:662
  35.3 0.0 collective-permute-done.got_own
  35.3 2.6 %shard_map.124 = (f32[3,28,72,128]{3,2,1,0:T(8,128)S(1)}, f32[6,28,72,128]{3,2,1,0:T(8,128)S(1)}, f32[3,28,40,128]{3,2,1,0:T(8,128)S(1)}, f32[216,8,128]{2,1,0:T(8,128)S(1)}) custom-call(bf16[2,4,256,256]{3,2,1,0:T(8,128)(2,1)S(1)} %copy-done, ...), custom_call_target="tpu_custom_call", output_to_operand_aliasing={{0}: (3, {}), {1}: (4, {}), {2}: (5, {})} | custom-call | tf_op jit(solution)/shard_map/pallas_call | solution.py:676
  37.9 1.9 %collective-permute-start.7 = (f32[216,8,128]{2,1,0:T(8,128)S(1)}, f32[216,8,128]{2,1,0:T(8,128)S(1)}, u32[]{:S(2)}, u32[]{:S(2)}) collective-permute-start(f32[216,8,128]{2,1,0:T(8,128)S(1)} %get-tuple-element.66), channel_id=1, source_target_pairs={{32,64},{64,32},{33,65},{65,33},{34,66},{66,34},{35,67},{67,35},{3... | collective-permute-start | bytes 2654216 | tf_op jit(solution)/shard_map/ppermute | solution.py:662
  39.9 0.1 collective-permute-start.8
  39.9 1.8 %collective-permute-done.8.refs_1_ = f32[21,40,128]{2,1,0:T(8,128)S(1)} collective-permute-done((f32[21,40,128]{2,1,0:T(8,128)S(1)}, f32[21,40,128]{2,1,0:T(8,128)S(1)}, u32[]{:S(2)}, u32[]{:S(2)}) %collective-permute-start.8) | collective-permute-done | bytes 430112 | tf_op jit(solution)/shard_map/ppermute | solution.py:661
  41.7 0.0 copy-start.6
  41.7 0.0 copy-start.8
  41.7 2.5 %shard_map.125 = (f32[3,28,72,128]{3,2,1,0:T(8,128)S(1)}, f32[6,28,72,128]{3,2,1,0:T(8,128)S(1)}, f32[3,28,40,128]{3,2,1,0:T(8,128)S(1)}, f32[21,40,128]{2,1,0:T(8,128)S(1)}) custom-call(bf16[2,4,256,256]{3,2,1,0:T(8,128)(2,1)S(1)} %copy-done, ...), custom_call_target="tpu_custom_call", output_to_operand_aliasing={{0}: (2, {}), {1}: (3, {}), {2}: (4, {})} | custom-call | flops 1024 | bytes 1024 | tf_op jit(solution)/shard_map/pallas_call | solution.py:665
  44.2 0.4 collective-permute-start.9
  45.9 0.4 collective-permute-done.9.got_ref
  46.3 0.0 copy-done.6
  46.3 0.0 copy-done.8
  46.3 0.0 copy-start.7
  46.3 0.0 copy-start.9
  46.3 0.0 copy-start.10
  46.3 3.8 %shard_map.126 = (f32[3,28,72,128]{3,2,1,0:T(8,128)S(1)}, f32[6,28,72,128]{3,2,1,0:T(8,128)S(1)}, f32[3,28,40,128]{3,2,1,0:T(8,128)S(1)}, f32[288,16,128]{2,1,0:...) custom-call(s32[1,64]{1,0:T(1,128)S(1)} %copy-done.8, ...), custom_call_target="tpu_custom_call", output_to_operand_aliasing={{0}: (5, {}), {1}: (6, {}), {2}: (7, {})} | custom-call | tf_op jit(solution)/shard_map/pallas_call | solution.py:681
  50.1 3.7 %collective-permute-done.7.got_ref = f32[216,8,128]{2,1,0:T(8,128)S(1)} collective-permute-done((f32[216,8,128]{2,1,0:T(8,128)S(1)}, f32[216,8,128]{2,1,0:T(8,128)S(1)}, u32[]{:S(2)}, u32[]{:S(2)}) %collective-permute-start.7) | collective-permute-done | bytes 884768 | tf_op jit(solution)/shard_map/ppermute | solution.py:662
  53.8 0.0 copy-done.7
  53.8 0.0 copy-done.9
  53.8 0.0 copy-done.10
  53.8 2.2 %shard_map.127 = (f32[3,28,72,128]{3,2,1,0:T(8,128)S(1)}, f32[6,28,72,128]{3,2,1,0:T(8,128)S(1)}, f32[3,28,40,128]{3,2,1,0:T(8,128)S(1)}, f32[8,128]{1,0:T(8,128)S(1)}) custom-call(s32[1]{0:T(128)S(6)} %copy.61.count_ref, f32[3,32]{1,0:T(4,128)S(1)} %copy-done.7, f32[1,32]{1,0:T(1,128)S(1)} %bitcast.19, ...), custom_call_target="tpu_custom_call", output_to_operand_aliasing={{0}: (6, {}), {1}: (7, {}), {2}: (8, {})} | custom-call | tf_op jit(solution)/shard_map/pallas_call | solution.py:688
  56.0 6.7 %all-gather = f32[32,128]{1,0:T(8,128)S(1)} all-gather(f32[8,128]{1,0:T(8,128)S(1)} %get-tuple-element.79), channel_id=2, replica_groups=mesh['region'=4,'tile'=32] {'region'}, dimensions={0}, use_global_device_ids=true | all-gather | bytes 20480 | tf_op jit(solution)/shard_map/all_gather | solution.py:693
  62.7 0.0 collective-permute-start.10
  62.7 5.2 %collective-permute-start.11 = (f32[4,8,128]{2,1,0:T(8,128)S(1)}, f32[4,8,128]{2,1,0:T(8,128)S(1)}, u32[]{:S(2)}, u32[]{:S(2)}) collective-permute-start(f32[4,8,128]{2,1,0:T(8,128)S(1)} %bitcast.17), channel_id=1, source_target_pairs={{1,2},{2,1},{3,4},{4,3},{5,6},{6,5},{7,8},{8,7},{9,10},{10,9},{11,... | collective-permute-start | bytes 49160 | tf_op jit(solution)/shard_map/ppermute | solution.py:695
  67.9 1.8 %shard_map.128 = (f32[6,28,72,128]{3,2,1,0:T(8,128)S(1)}, f32[288,16,128]{2,1,0:T(8,128)}, f32[48,128]{1,0:T(8,128)S(1)}) custom-call(bf16[2,4,256,256]{3,2,1,0:T(8,128)(2,1)S(1)} %copy-done, f32[4,8,128]{2,1,0:T(8,128)S(1)} %bitcast.18, s32[8,128]{1,0:T(8,128)S(1)} %get-tuple-element.80.used_ref, ...), custom_call_target="tpu_custom_call", output_to_operand_aliasing={{0}: (4, {}), {1}: (6, {})} | custom-call | tf_op jit(solution)/shard_map/pallas_call | solution.py:696
  69.8 0.0 collective-permute-done.10.first_ref
  69.8 1.5 %collective-permute-done.11.second_ref = f32[4,8,128]{2,1,0:T(8,128)S(1)} collective-permute-done((f32[4,8,128]{2,1,0:T(8,128)S(1)}, f32[4,8,128]{2,1,0:T(8,128)S(1)}, u32[]{:S(2)}, u32[]{:S(2)}) %collective-permute-start.11) | collective-permute-done | bytes 16416 | tf_op jit(solution)/shard_map/ppermute | solution.py:695
  71.3 1.4 %shard_map.129 = f32[288,16,128]{2,1,0:T(8,128)} custom-call(f32[3,28,72,128]{3,2,1,0:T(8,128)S(1)} %get-tuple-element.78.v_ref, f32[4,8,128]{2,1,0:T(8,128)S(1)} %collective-permute-done.10.first_ref, f32[4,8,128]{2,1,0:T(8,128)S(1)} %collective-permute-done.11.second_ref, s32[8,128]{1,0:T(8,128)S(1)} %get-tuple-element.80.used_ref, ...), custom_call_target="tpu_custom_call", output_to_operand_aliasing={{}: (6, {})} | custom-call | tf_op jit(solution)/shard_map/pallas_call | solution.py:701
Async XLA Ops:
  0.0 12.4 %copy-start.2 = (f32[32,16,128]{2,1,0:T(8,128)S(1)}, f32[32,16,128]{2,1,0:T(8,128)}, u32[]{:S(2)}) copy-start(f32[32,16,128]{2,1,0:T(8,128)} %param.13) | copy-start | bytes 786436
  0.0 12.4 %copy-start.3 = (f32[32,16,128]{2,1,0:T(8,128)S(1)}, f32[32,16,128]{2,1,0:T(8,128)}, u32[]{:S(2)}) copy-start(f32[32,16,128]{2,1,0:T(8,128)} %param.14) | copy-start | bytes 786436
  0.0 12.4 %copy-start.4 = (f32[32,16,128]{2,1,0:T(8,128)S(1)}, f32[32,16,128]{2,1,0:T(8,128)}, u32[]{:S(2)}) copy-start(f32[32,16,128]{2,1,0:T(8,128)} %param.15) | copy-start | bytes 786436
  4.6 13.3 %collective-permute-start.2 = (f32[12,6,8,128]{3,2,1,0:T(8,128)}, f32[12,6,8,128]{3,2,1,0:T(8,128)S(1)}, u32[]{:S(2)}, u32[]{:S(2)}) collective-permute-start(f32[12,6,8,128]{3,2,1,0:T(8,128)} %get-tuple-element.49), channel_id=1, source_target_pairs={{0,1},{1,0},{2,3},{3,2},{4,5},{5,4},{6,7},{7,6},{8,9},{9,8},{10,11... | collective-permute-start | bytes 884744 | tf_op jit(solution)/shard_map/ppermute | solution.py:643
  6.0 13.7 %collective-permute-start.1 = (f32[12,6,8,128]{3,2,1,0:T(8,128)}, f32[12,6,8,128]{3,2,1,0:T(8,128)S(1)}, u32[]{:S(2)}, u32[]{:S(2)}) collective-permute-start(f32[12,6,8,128]{3,2,1,0:T(8,128)} %get-tuple-element.48), channel_id=1, source_target_pairs={{1,2},{2,1},{3,4},{4,3},{5,6},{6,5},{7,8},{8,7},{9,10},{10,9},{11,... | collective-permute-start | bytes 884744 | tf_op jit(solution)/shard_map/ppermute | solution.py:644
  12.4 1.7 %copy-start.1 = (f32[9,32,16,128]{3,2,1,0:T(8,128)S(1)}, f32[9,32,16,128]{3,2,1,0:T(8,128)}, u32[]{:S(2)}) copy-start(f32[9,32,16,128]{3,2,1,0:T(8,128)} %param.12) | copy-start | bytes 7077892
  14.1 0.7 copy-start.5
  16.0 19.3 %collective-permute-start = (f32[59,32,128]{2,1,0:T(8,128)S(1)}, f32[59,32,128]{2,1,0:T(8,128)S(1)}, u32[]{:S(2)}, u32[]{:S(2)}) collective-permute-start(f32[59,32,128]{2,1,0:T(8,128)S(1)} %get-tuple-element.47), channel_id=1, source_target_pairs={{32,64},{64,32},{33,65},{65,33},{34,66},{66,34},{35,67},{67,35},{3... | collective-permute-start | bytes 2899976 | tf_op jit(solution)/shard_map/ppermute | solution.py:649
  19.7 5.0 %copy-start = (bf16[2,4,256,256]{3,2,1,0:T(8,128)(2,1)S(1)}, bf16[2,4,256,256]{3,2,1,0:T(8,128)(2,1)}, u32[]{:S(2)}) copy-start(bf16[2,4,256,256]{3,2,1,0:T(8,128)(2,1)} %constant.2.clone.refs_0_.band_ref) | copy-start | bytes 3145732
  20.0 4.6 %collective-permute-start.4 = (f32[23,40,128]{2,1,0:T(8,128)S(1)}, f32[23,40,128]{2,1,0:T(8,128)S(1)}, u32[]{:S(2)}, u32[]{:S(2)}) collective-permute-start(f32[23,40,128]{2,1,0:T(8,128)S(1)} %get-tuple-element.54), channel_id=1, source_target_pairs={{0,32},{32,0},{64,96},{96,64},{1,33},{33,1},{65,97},{97,65},{2,34}... | collective-permute-start | bytes 1413128 | tf_op jit(solution)/shard_map/ppermute | solution.py:661
  20.1 15.2 %collective-permute-start.3 = (f32[59,8,128]{2,1,0:T(8,128)S(1)}, f32[59,8,128]{2,1,0:T(8,128)S(1)}, u32[]{:S(2)}, u32[]{:S(2)}) collective-permute-start(f32[59,8,128]{2,1,0:T(8,128)S(1)} %get-tuple-element.53), channel_id=1, source_target_pairs={{32,64},{64,32},{33,65},{65,33},{34,66},{66,34},{35,67},{67,35},{3... | collective-permute-start | bytes 725000 | tf_op jit(solution)/shard_map/ppermute | solution.py:662
  28.5 1.9 %collective-permute-start.5 = (f32[11,40,128]{2,1,0:T(8,128)S(1)}, f32[11,40,128]{2,1,0:T(8,128)S(1)}, u32[]{:S(2)}, u32[]{:S(2)}) collective-permute-start(f32[11,40,128]{2,1,0:T(8,128)S(1)} %get-tuple-element.58), channel_id=1, source_target_pairs={{0,32},{32,0},{64,96},{96,64},{1,33},{33,1},{65,97},{97,65},{2,34}... | collective-permute-start | bytes 675848 | tf_op jit(solution)/shard_map/ppermute | solution.py:670
  28.6 1.8 %collective-permute-start.6 = (f32[10,40,128]{2,1,0:T(8,128)S(1)}, f32[10,40,128]{2,1,0:T(8,128)S(1)}, u32[]{:S(2)}, u32[]{:S(2)}) collective-permute-start(f32[10,40,128]{2,1,0:T(8,128)S(1)} %get-tuple-element.59), channel_id=1, source_target_pairs={{0,32},{32,0},{64,96},{96,64},{1,33},{33,1},{65,97},{97,65},{2,34}... | collective-permute-start | bytes 614408 | tf_op jit(solution)/shard_map/ppermute | solution.py:670
  37.9 15.9 %collective-permute-start.7 = (f32[216,8,128]{2,1,0:T(8,128)S(1)}, f32[216,8,128]{2,1,0:T(8,128)S(1)}, u32[]{:S(2)}, u32[]{:S(2)}) collective-permute-start(f32[216,8,128]{2,1,0:T(8,128)S(1)} %get-tuple-element.66), channel_id=1, source_target_pairs={{32,64},{64,32},{33,65},{65,33},{34,66},{66,34},{35,67},{67,35},{3... | collective-permute-start | bytes 2654216 | tf_op jit(solution)/shard_map/ppermute | solution.py:662
  39.9 1.9 %collective-permute-start.8 = (f32[21,40,128]{2,1,0:T(8,128)S(1)}, f32[21,40,128]{2,1,0:T(8,128)S(1)}, u32[]{:S(2)}, u32[]{:S(2)}) collective-permute-start(f32[21,40,128]{2,1,0:T(8,128)S(1)} %get-tuple-element.67), channel_id=1, source_target_pairs={{0,32},{32,0},{64,96},{96,64},{1,33},{33,1},{65,97},{97,65},{2,34}... | collective-permute-start | bytes 1290248 | tf_op jit(solution)/shard_map/ppermute | solution.py:661
  41.7 4.6 %copy-start.6 = (f32[3,32]{1,0:T(4,128)S(1)}, f32[3,32]{1,0:T(4,128)}, u32[]{:S(2)}) copy-start(f32[3,32]{1,0:T(4,128)} %profile_ref.1) | copy-start | bytes 1156
  41.7 4.6 %copy-start.8 = (s32[1,64]{1,0:T(1,128)S(1)}, s32[1,64]{1,0:T(1,128)}, u32[]{:S(2)}) copy-start(s32[1,64]{1,0:T(1,128)} %influence_ref.1) | copy-start | bytes 772
  44.2 2.0 %collective-permute-start.9 = (f32[21,40,128]{2,1,0:T(8,128)S(1)}, f32[21,40,128]{2,1,0:T(8,128)S(1)}, u32[]{:S(2)}, u32[]{:S(2)}) collective-permute-start(f32[21,40,128]{2,1,0:T(8,128)S(1)} %get-tuple-element.71), channel_id=1, source_target_pairs={{0,32},{32,0},{64,96},{96,64},{1,33},{33,1},{65,97},{97,65},{2,34}... | collective-permute-start | bytes 1290248 | tf_op jit(solution)/shard_map/ppermute | solution.py:670
  46.3 7.5 %copy-start.7 = (f32[3,32]{1,0:T(4,128)S(1)}, f32[3,32]{1,0:T(4,128)}, u32[]{:S(2)}) copy-start(f32[3,32]{1,0:T(4,128)} %observed_ref.1) | copy-start | bytes 1156
  46.3 7.5 %copy-start.9 = (f32[32]{0:T(128)S(1)}, f32[32]{0:T(128)}, u32[]{:S(2)}) copy-start(f32[32]{0:T(128)} %param.17) | copy-start | bytes 388
  46.3 7.5 %copy-start.10 = (s32[32]{0:T(128)S(1)}, s32[32]{0:T(128)}, u32[]{:S(2)}) copy-start(s32[32]{0:T(128)} %param.19) | copy-start | bytes 388
  62.7 7.1 %collective-permute-start.10 = (f32[4,8,128]{2,1,0:T(8,128)S(1)}, f32[4,8,128]{2,1,0:T(8,128)S(1)}, u32[]{:S(2)}, u32[]{:S(2)}) collective-permute-start(f32[4,8,128]{2,1,0:T(8,128)S(1)} %bitcast.16), channel_id=1, source_target_pairs={{0,1},{1,0},{2,3},{3,2},{4,5},{5,4},{6,7},{7,6},{8,9},{9,8},{10,11... | collective-permute-start | bytes 49160 | tf_op jit(solution)/shard_map/ppermute | solution.py:694
  62.7 8.6 %collective-permute-start.11 = (f32[4,8,128]{2,1,0:T(8,128)S(1)}, f32[4,8,128]{2,1,0:T(8,128)S(1)}, u32[]{:S(2)}, u32[]{:S(2)}) collective-permute-start(f32[4,8,128]{2,1,0:T(8,128)S(1)} %bitcast.17), channel_id=1, source_target_pairs={{1,2},{2,1},{3,4},{4,3},{5,6},{6,5},{7,8},{8,7},{9,10},{10,9},{11,... | collective-permute-start | bytes 49160 | tf_op jit(solution)/shard_map/ppermute | solution.py:695

commit v7 on v6

--- a/solution.py
+++ b/solution.py
@@ -12,7 +12,7 @@
 S, LIST = 32, 64
 GROUPS = 4
 HALF = 16
-WIDE = 12
+WIDTHS = (11, 11, 11, 11, 12, 11, 12, 11, 12, 11, 9, 9)
 PACK = NZ // GROUPS
 DEPTH = NZ + PACK
 LOW = 6
@@ -288,17 +288,20 @@
 
 
 def pieces():
-    out = []
-    for u in range(8):
-        for v in range(3):
-            start = WIDE * u - 32 * v
-            a, b = max(0, start), min(32, start + WIDE)
-            if a < b:
-                out.append((u, v, start, a, b))
-    return out
-
-
-PIECES = pieces()
+    out, at = {}, 0
+    for a in range(12):
+        for block in range(2):
+            for u in range(8):
+                unit = []
+                for v in range(at // 32, (at + WIDTHS[a] - 1) // 32 + 1):
+                    start = at - 32 * v
+                    unit.append((v, start, max(0, start), min(32, start + WIDTHS[a])))
+                out[a, block, u] = unit
+                at += WIDTHS[a]
+    return out, -(-at // 32)
+
+
+PIECES, VECTORS = pieces()
 
 
 def fetch(refs, buf_ref, sems):
@@ -312,70 +315,65 @@
     return waits
 
 
-def low_side(first):
-    odd = lax.rem(lax.axis_index("tile"), 2) > 0
-    return jnp.where(odd, HALF - WIDE, HALF) if first else jnp.where(odd, HALF, HALF - WIDE)
-
-
-def pack_units(units, at, put):
-    spot = lanes(PACK) % 32
-    parts = [None] * 3
-    for u, v, start, lo, hi in PIECES:
-        keep = (spot >= lo) & (spot < hi)
-        moved = pltpu.roll(units[u], lax.rem(start - at + 256, 128), 1)
-        parts[v] = moved if parts[v] is None else jnp.where(keep, moved, parts[v])
-    for v in range(3):
-        put(v, parts[v])
-
-
-def edge_kernel(fields_ref, buoy_ref, lame_ref, mu_ref, first_ref, second_ref, token_ref, buf_ref,
-                sems):
+def odd_tile():
+    return lax.rem(lax.axis_index("tile"), 2) > 0
+
+
+def low_side(first, width):
+    below, above = HALF - width, HALF
+    return jnp.where(odd_tile(), below, above) if first else jnp.where(odd_tile(), above, below)
+
+
+def edge_kernel(fields_ref, buoy_ref, lame_ref, mu_ref, first_ref, second_ref, buf_ref, sems):
     size = NZ * CX
     lane = lanes(PACK)
-    token_ref[...] = jnp.zeros((8, 128), jnp.float32)
+    spot = lane % 32
+    open_parts = [{}, {}]
     for a, copy in enumerate(fetch((fields_ref, buoy_ref, lame_ref, mu_ref), buf_ref, sems)):
         copy.wait()
+        last, zero = -WIDTHS[a], 0
+        ats = (jnp.where(odd_tile(), zero, last), jnp.where(odd_tile(), last, zero))
         for block in range(2):
-            units = []
             for u in range(8):
-                out = None
-                for g in range(GROUPS):
-                    row = a * size + (8 * g + u) * CX + 8 * block
-                    moved = pltpu.roll(buf_ref[row:row + 8, :], (HALF + 32 * g) % 128, 1)
-                    out = moved if g == 0 else jnp.where(lane >= 32 * g, moved, out)
-                units.append(out)
-            for ref, is_first in ((first_ref, True), (second_ref, False)):
-                def put(v, value):
-                    ref[a, 3 * block + v] = value
-                pack_units(units, 2 * HALF - WIDE - low_side(is_first), put)
+                rows = [buf_ref[row:row + 8, :] for row in
+                        [a * size + (8 * g + u) * CX + 8 * block for g in range(GROUPS)]]
+                unit = rows[0]
+                for g in range(1, GROUPS):
+                    unit = jnp.where(lane >= 32 * g - 16, pltpu.roll(rows[g], 32 * g, 1), unit)
+                unit = jnp.where(lane >= 112, rows[0], unit)
+                for v, start, lo, hi in PIECES[a, block, u]:
+                    keep = (spot >= lo) & (spot < hi)
+                    for parts, at, ref in zip(open_parts, ats, (first_ref, second_ref)):
+                        moved = pltpu.roll(unit, lax.rem(start - at + 256, 128), 1)
+                        parts[v] = jnp.where(keep, moved, parts[v]) if v in parts else moved
+                        if hi == 32:
+                            ref[v] = parts.pop(v)
+    for parts, ref in zip(open_parts, (first_ref, second_ref)):
+        for v, value in parts.items():
+            ref[v] = value
 
 
 def unpack_units(got_ref, a, block, at, under, put):
     spot = lanes(PACK) % 32
     for u in range(8):
         value = under(u)
-        for w, v, start, lo, hi in PIECES:
-            if w == u:
-                keep = (spot >= lo - start + at) & (spot < hi - start + at)
-                moved = pltpu.roll(got_ref[a, 3 * block + v], lax.rem(at - start + 256, 128), 1)
-                value = jnp.where(keep, moved, value)
+        for v, start, lo, hi in PIECES[a, block, u]:
+            keep = (spot >= lo - start + at) & (spot < hi - start + at)
+            moved = pltpu.roll(got_ref[v], lax.rem(at - start + 256, 128), 1)
+            value = jnp.where(keep, moved, value)
         put(u, value)
 
 
 def first_halo_kernel(got_ref, half_ref):
-    at = low_side(True)
-
-    def body(a, _):
+    for a in range(12):
         for block in range(2):
             def put(u, value):
                 half_ref[a, block, u] = value
-            unpack_units(got_ref, a, block, at, lambda u: jnp.zeros((PACK, 128), jnp.float32), put)
-        return 0
-
-    lax.fori_loop(0, 12, body, 0)
-
-
-def build_kernel(fields_ref, buoy_ref, lame_ref, mu_ref, after_ref, v_ref, t_ref, p_ref, outer_ref):
+            unpack_units(got_ref, a, block, low_side(True, WIDTHS[a]),
+                         lambda u: jnp.zeros((PACK, 128), jnp.float32), put)
+
+
+def build_kernel(fields_ref, buoy_ref, lame_ref, mu_ref, v_ref, t_ref, p_ref, outer_ref):
     size = NZ * CX
     zero = jnp.zeros((8, 128), jnp.float32)
 
@@ -401,7 +399,6 @@
 
 def halo_kernel(got_ref, half_ref, v_in, t_in, p_in, v_ref, t_ref, p_ref, outer_ref, inner_ref):
     odd = is_odd()
-    at = low_side(False)
     v_rows = v_ref.reshape(3 * PLANES * ZROWS, 128)
     t_rows = t_ref.reshape(6 * PLANES * ZROWS, 128)
     p_rows = p_ref.reshape(3 * PLANES * DEPTH, 128)
@@ -411,7 +408,8 @@
             def put(u, value):
                 row = (f * PLANES + LOW + 8 * block) * depth + begin + u
                 rows_ref[pl.ds(row, 8, stride=depth), :] = scale * value if scale else value
-            unpack_units(got_ref, a, block, at, lambda u: half_ref[a, block, u], put)
+            unpack_units(got_ref, a, block, low_side(False, WIDTHS[a]),
+                         lambda u: half_ref[a, block, u], put)
 
     for a in range(12):
         if a < 3:
@@ -637,15 +635,15 @@
     given = (fields.reshape(9 * size, CY), buoyancy.reshape(size, CY),
              lame_first.reshape(size, CY), shear_modulus.reshape(size, CY))
     fetched = [pltpu.VMEM((12 * size, 128), jnp.float32), pltpu.SemaphoreType.DMA((12,))]
-    packed, edges = struct(12, 6, PACK, 128), struct(12, 2, 8, 8, 128)
-    first, second, token = call(edge_kernel, (packed, packed, struct(8, 128)), [HB] * 4, fetched,
+    packed, edges = struct(VECTORS, PACK, 128), struct(12, 2, 8, 8, 128)
+    first, second = call(edge_kernel, (packed, packed), [HB] * 4, fetched,
                          vmem=62 * 2 ** 20)(*given)
     got_first = lax.ppermute(first, "tile", pairs(0))
     got_second = lax.ppermute(second, "tile", pairs(1))
     early, planes = plane_count(OUTER_FIRST[:EARLY_FIELDS]), plane_count(OUTER_FIRST)
-    v, t, p, outer = call(build_kernel, state + (struct(early, NZ, 128),), [VM] * 5, [],
+    v, t, p, outer = call(build_kernel, state + (struct(early, NZ, 128),), [VM] * 4, [],
                           cost=pl.CostEstimate(flops=0, bytes_accessed=10 ** 8, transcendentals=0))(
-        *given, token)
+        *given)
     got_own = lax.ppermute(outer, "region", OUTER_SWAP)
     half, = call(first_halo_kernel, (edges,), [VM], [])(got_first)
     v, t, p, outer, inner = call(

time: 73.2 us -> 72.2 us (0.986)
  waiting for transfers between devices: 12.2 us -> 14.4 us
  starting transfers between devices: 22.5 us -> 21.1 us
  Pallas kernels: 27.5 us -> 26.3 us
    ppermute x2, starting transfers between devices: 6.47 us -> 5.55 us  [per_device(): got_outer = lax.ppermute(outer, 'region', OUTER_SWAP)]
    ppermute x1, waiting for transfers between devices: 0.66 us -> 1.55 us  [per_device(): got_second = lax.ppermute(second, 'tile', pairs(1))]
    ppermute x2, waiting for transfers between devices: 6.58 us -> 7.42 us  [per_device(): got_outer = lax.ppermute(outer, 'region', OUTER_SWAP)]
    pallas_call x1, Pallas kernels: 1.09 us -> 0.35 us  [per_device(): half, = call(first_halo_kernel, (edges,), [VM], [])(got_first)]
    unnamed x22 -> x20, local copies, waits for them, and re-layouts: 2.37 us -> 1.7 us
  transfers between devices with their start and end apart: 12 -> 12, of which waited for: 7 -> 7; matrix products, arithmetic and copies ran while one was open for 0% -> 0% of each run, Pallas kernels for 23% -> 22%
where the time goes in v7:
time: 72.2 us; the launch traced here: 71.9 us
  Pallas kernels  26.3 us (36%)
  starting transfers between devices  21.1 us (29%)
  waiting for transfers between devices  14.4 us (20%)
  blocking collectives  6.68 us (9%)
  local copies, waits for them, and re-layouts  1.7 us (2%)
  between operations  1.69 us (2%)
    ppermute x2, waiting for transfers between devices, per_device(): got_outer = lax.ppermute(outer, 'region', OUTER_SWAP)  7.42 us
    all_gather x1, blocking collectives, per_device(): here = lax.all_gather(packet, 'region')  6.68 us
    ppermute x1, starting transfers between devices, per_device(): got_second = lax.ppermute(second, 'tile', pairs(1))  6.38 us
    pallas_call x2, Pallas kernels, per_device(): call(bind(near_kernel, INNER_FIRST if block == 0 else INNER, 0, 1, split)...  6.3 us
    ppermute x2, starting transfers between devices, per_device(): got_outer = lax.ppermute(outer, 'region', OUTER_SWAP)  5.55 us
    ppermute x1, starting transfers between devices, per_device(): got_second = lax.ppermute(here, 'tile', pairs(1))  4.79 us
    pallas_call x1, Pallas kernels, per_device(): call(edge_kernel, (packed, packed), [HB] * 4, fetched, vmem=62 * 2 ** 20)  4.32 us
    pallas_call x1, Pallas kernels, per_device(): call(last_near_kernel, state + (result, jax.ShapeDtypeStruct((8, 128), jn...  3.72 us
  transfers between devices with their start and end apart: 12, of which 7 were waited for; matrix products, arithmetic and copies ran while one was open for 0% of the time, Pallas kernels for 22%

profile of v7, /device:TPU:22, one launch (start us, length us, event | category | flops | bytes accessed | tf_op | source)
XLA Modules:
  0.0 71.9 jit_solution(8890959800582908361)
XLA Ops:
  0.0 0.0 copy-start.2
  0.0 0.0 copy-start.3
  0.0 0.0 copy-start.4
  0.0 4.3 %shard_map.119 = (f32[66,8,128]{2,1,0:T(8,128)}, f32[66,8,128]{2,1,0:T(8,128)}) custom-call(f32[4608,128]{1,0:T(8,128)} %bitcast.8, f32[512,128]{1,0:T(8,128)} %bitcast.10, f32[512,128]{1,0:T(8,128)} %bitcast.12, f32[512,128]{1,0:T(8,128)} %bitcast.14), custom_call_target="tpu_custom_call" | custom-call | tf_op jit(solution)/shard_map/pallas_call | solution.py:639
  4.3 1.4 %collective-permute-start.2 = (f32[66,8,128]{2,1,0:T(8,128)}, f32[66,8,128]{2,1,0:T(8,128)S(1)}, u32[]{:S(2)}, u32[]{:S(2)}) collective-permute-start(f32[66,8,128]{2,1,0:T(8,128)} %get-tuple-element.47), channel_id=1, source_target_pairs={{0,1},{1,0},{2,3},{3,2},{4,5},{5,4},{6,7},{7,6},{8,9},{9,8},{10,11... | collective-permute-start | bytes 811016 | tf_op jit(solution)/shard_map/ppermute | solution.py:641
  5.7 6.4 %collective-permute-start.1 = (f32[66,8,128]{2,1,0:T(8,128)}, f32[66,8,128]{2,1,0:T(8,128)S(1)}, u32[]{:S(2)}, u32[]{:S(2)}) collective-permute-start(f32[66,8,128]{2,1,0:T(8,128)} %get-tuple-element.46), channel_id=1, source_target_pairs={{1,2},{2,1},{3,4},{4,3},{5,6},{6,5},{7,8},{8,7},{9,10},{10,9},{11,... | collective-permute-start | bytes 811016 | tf_op jit(solution)/shard_map/ppermute | solution.py:642
  12.1 0.0 copy-done.2
  12.1 0.0 copy-done.3
  12.1 0.0 copy-done.4
  12.1 0.0 copy-start.1
  12.1 1.7 %copy-done.1 = f32[9,32,16,128]{3,2,1,0:T(8,128)S(1)} copy-done((f32[9,32,16,128]{3,2,1,0:T(8,128)S(1)}, f32[9,32,16,128]{3,2,1,0:T(8,128)}, u32[]{:S(2)}) %copy-start.1) | copy-done | bytes 2359320
  13.8 1.2 %shard_map.118 = (f32[3,28,72,128]{3,2,1,0:T(8,128)S(1)}, f32[6,28,72,128]{3,2,1,0:T(8,128)S(1)}, f32[3,28,40,128]{3,2,1,0:T(8,128)S(1)}, f32[59,32,128]{2,1,0:T(8,128)S(1)}) custom-call(f32[4608,128]{1,0:T(8,128)S(1)} %bitcast.9, f32[512,128]{1,0:T(8,128)S(1)} %bitcast.11, f32[512,128]{1,0:T(8,128)S(1)} %bitcast.13, f32[512,128]{1,0:T(8,128)S(1)} %bitcast.15), custom_call_target="tpu_custom_call" | custom-call | bytes 100000000 | tf_op jit(solution)/shard_map/pallas_call | solution.py:644
  15.0 1.9 %collective-permute-start = (f32[59,32,128]{2,1,0:T(8,128)S(1)}, f32[59,32,128]{2,1,0:T(8,128)S(1)}, u32[]{:S(2)}, u32[]{:S(2)}) collective-permute-start(f32[59,32,128]{2,1,0:T(8,128)S(1)} %get-tuple-element.45), channel_id=1, source_target_pairs={{32,64},{64,32},{33,65},{65,33},{34,66},{66,34},{35,67},{67,35},{3... | collective-permute-start | bytes 2899976 | tf_op jit(solution)/shard_map/ppermute | solution.py:647
  16.9 0.0 collective-permute-done.2.got_ref
  16.9 0.3 shard_map.120.half_ref
  17.3 1.5 %collective-permute-done.1.got_ref = f32[66,8,128]{2,1,0:T(8,128)S(1)} collective-permute-done((f32[66,8,128]{2,1,0:T(8,128)}, f32[66,8,128]{2,1,0:T(8,128)S(1)}, u32[]{:S(2)}, u32[]{:S(2)}) %collective-permute-start.1) | collective-permute-done | bytes 270368 | tf_op jit(solution)/shard_map/ppermute | solution.py:642
  18.8 0.0 copy-start
  18.8 0.4 shard_map.121
  19.2 0.1 collective-permute-start.4
  19.3 3.6 %collective-permute-start.3 = (f32[59,8,128]{2,1,0:T(8,128)S(1)}, f32[59,8,128]{2,1,0:T(8,128)S(1)}, u32[]{:S(2)}, u32[]{:S(2)}) collective-permute-start(f32[59,8,128]{2,1,0:T(8,128)S(1)} %get-tuple-element.51), channel_id=1, source_target_pairs={{32,64},{64,32},{33,65},{65,33},{34,66},{66,34},{35,67},{67,35},{3... | collective-permute-start | bytes 725000 | tf_op jit(solution)/shard_map/ppermute | solution.py:660
  23.0 0.0 collective-permute-done.4.refs_1_
  23.0 0.0 copy-done
  23.0 3.8 %shard_map.122 = (f32[3,28,72,128]{3,2,1,0:T(8,128)S(1)}, f32[6,28,72,128]{3,2,1,0:T(8,128)S(1)}, f32[3,28,40,128]{3,2,1,0:T(8,128)S(1)}, f32[11,40,128]{2,1,0:T(8,128)S(1)}, f32[10,40,128]{2,1,0:T(8,128)S(1)}) custom-call(bf16[2,4,256,256]{3,2,1,0:T(8,128)(2,1)S(1)} %copy-done, ...), custom_call_target="tpu_custom_call", output_to_operand_aliasing={{0}: (2, {}), {1}: (3, {}), {2}: (4, {})} | custom-call | flops 1024 | bytes 1024 | tf_op jit(solution)/shard_map/pallas_call | solution.py:663
  26.8 0.1 collective-permute-start.5
  26.9 0.5 collective-permute-start.6
  27.4 1.3 %collective-permute-done.6.refs_2_ = f32[10,40,128]{2,1,0:T(8,128)S(1)} collective-permute-done((f32[10,40,128]{2,1,0:T(8,128)S(1)}, f32[10,40,128]{2,1,0:T(8,128)S(1)}, u32[]{:S(2)}, u32[]{:S(2)}) %collective-permute-start.6) | collective-permute-done | bytes 204832 | tf_op jit(solution)/shard_map/ppermute | solution.py:668
  28.6 0.0 collective-permute-done.5.refs_1_
  28.6 2.0 %shard_map.123 = (f32[3,28,72,128]{3,2,1,0:T(8,128)S(1)}, f32[6,28,72,128]{3,2,1,0:T(8,128)S(1)}, f32[3,28,40,128]{3,2,1,0:T(8,128)S(1)}, f32[21,40,128]{2,1,0:T(8,128)S(1)}) custom-call(bf16[2,4,256,256]{3,2,1,0:T(8,128)(2,1)S(1)} %copy-done, ...), custom_call_target="tpu_custom_call", output_to_operand_aliasing={{0}: (3, {}), {1}: (4, {}), {2}: (5, {})} | custom-call | flops 1024 | bytes 1024 | tf_op jit(solution)/shard_map/pallas_call | solution.py:670
  30.7 3.6 %collective-permute-done.3.got_halo = f32[59,8,128]{2,1,0:T(8,128)S(1)} collective-permute-done((f32[59,8,128]{2,1,0:T(8,128)S(1)}, f32[59,8,128]{2,1,0:T(8,128)S(1)}, u32[]{:S(2)}, u32[]{:S(2)}) %collective-permute-start.3) | collective-permute-done | bytes 241696 | tf_op jit(solution)/shard_map/ppermute | solution.py:660
  34.3 0.0 collective-permute-done.got_own
  34.3 2.6 %shard_map.124 = (f32[3,28,72,128]{3,2,1,0:T(8,128)S(1)}, f32[6,28,72,128]{3,2,1,0:T(8,128)S(1)}, f32[3,28,40,128]{3,2,1,0:T(8,128)S(1)}, f32[216,8,128]{2,1,0:T(8,128)S(1)}) custom-call(bf16[2,4,256,256]{3,2,1,0:T(8,128)(2,1)S(1)} %copy-done, ...), custom_call_target="tpu_custom_call", output_to_operand_aliasing={{0}: (3, {}), {1}: (4, {}), {2}: (5, {})} | custom-call | tf_op jit(solution)/shard_map/pallas_call | solution.py:674
  36.9 1.9 %collective-permute-start.7 = (f32[216,8,128]{2,1,0:T(8,128)S(1)}, f32[216,8,128]{2,1,0:T(8,128)S(1)}, u32[]{:S(2)}, u32[]{:S(2)}) collective-permute-start(f32[216,8,128]{2,1,0:T(8,128)S(1)} %get-tuple-element.64), channel_id=1, source_target_pairs={{32,64},{64,32},{33,65},{65,33},{34,66},{66,34},{35,67},{67,35},{3... | collective-permute-start | bytes 2654216 | tf_op jit(solution)/shard_map/ppermute | solution.py:660
  38.8 0.1 collective-permute-start.8
  38.9 1.8 %collective-permute-done.8.refs_1_ = f32[21,40,128]{2,1,0:T(8,128)S(1)} collective-permute-done((f32[21,40,128]{2,1,0:T(8,128)S(1)}, f32[21,40,128]{2,1,0:T(8,128)S(1)}, u32[]{:S(2)}, u32[]{:S(2)}) %collective-permute-start.8) | collective-permute-done | bytes 430112 | tf_op jit(solution)/shard_map/ppermute | solution.py:659
  40.7 0.0 copy-start.5
  40.7 0.0 copy-start.7
  40.7 2.5 %shard_map.125 = (f32[3,28,72,128]{3,2,1,0:T(8,128)S(1)}, f32[6,28,72,128]{3,2,1,0:T(8,128)S(1)}, f32[3,28,40,128]{3,2,1,0:T(8,128)S(1)}, f32[21,40,128]{2,1,0:T(8,128)S(1)}) custom-call(bf16[2,4,256,256]{3,2,1,0:T(8,128)(2,1)S(1)} %copy-done, ...), custom_call_target="tpu_custom_call", output_to_operand_aliasing={{0}: (2, {}), {1}: (3, {}), {2}: (4, {})} | custom-call | flops 1024 | bytes 1024 | tf_op jit(solution)/shard_map/pallas_call | solution.py:663
  43.2 0.4 collective-permute-start.9
  44.9 0.4 collective-permute-done.9.got_ref
  45.2 0.0 copy-done.5
  45.2 0.0 copy-done.7
  45.3 0.0 copy-start.6
  45.3 0.0 copy-start.8
  45.3 0.0 copy-start.9
  45.3 3.7 %shard_map.126 = (f32[3,28,72,128]{3,2,1,0:T(8,128)S(1)}, f32[6,28,72,128]{3,2,1,0:T(8,128)S(1)}, f32[3,28,40,128]{3,2,1,0:T(8,128)S(1)}, f32[288,16,128]{2,1,0:...) custom-call(s32[1,64]{1,0:T(1,128)S(1)} %copy-done.7, ...), custom_call_target="tpu_custom_call", output_to_operand_aliasing={{0}: (5, {}), {1}: (6, {}), {2}: (7, {})} | custom-call | tf_op jit(solution)/shard_map/pallas_call | solution.py:679
  49.0 3.8 %collective-permute-done.7.got_ref = f32[216,8,128]{2,1,0:T(8,128)S(1)} collective-permute-done((f32[216,8,128]{2,1,0:T(8,128)S(1)}, f32[216,8,128]{2,1,0:T(8,128)S(1)}, u32[]{:S(2)}, u32[]{:S(2)}) %collective-permute-start.7) | collective-permute-done | bytes 884768 | tf_op jit(solution)/shard_map/ppermute | solution.py:660
  52.8 0.0 copy-done.6
  52.8 0.0 copy-done.8
  52.8 0.0 copy-done.9
  52.8 2.2 %shard_map.127 = (f32[3,28,72,128]{3,2,1,0:T(8,128)S(1)}, f32[6,28,72,128]{3,2,1,0:T(8,128)S(1)}, f32[3,28,40,128]{3,2,1,0:T(8,128)S(1)}, f32[8,128]{1,0:T(8,128)S(1)}) custom-call(s32[1]{0:T(128)S(6)} %copy.61.count_ref, f32[3,32]{1,0:T(4,128)S(1)} %copy-done.6, f32[1,32]{1,0:T(1,128)S(1)} %bitcast.19, ...), custom_call_target="tpu_custom_call", output_to_operand_aliasing={{0}: (6, {}), {1}: (7, {}), {2}: (8, {})} | custom-call | tf_op jit(solution)/shard_map/pallas_call | solution.py:686
  55.0 6.7 %all-gather = f32[32,128]{1,0:T(8,128)S(1)} all-gather(f32[8,128]{1,0:T(8,128)S(1)} %get-tuple-element.77), channel_id=2, replica_groups=mesh['region'=4,'tile'=32] {'region'}, dimensions={0}, use_global_device_ids=true | all-gather | bytes 20480 | tf_op jit(solution)/shard_map/all_gather | solution.py:691
  61.7 0.0 collective-permute-start.10
  61.7 4.8 %collective-permute-start.11 = (f32[4,8,128]{2,1,0:T(8,128)S(1)}, f32[4,8,128]{2,1,0:T(8,128)S(1)}, u32[]{:S(2)}, u32[]{:S(2)}) collective-permute-start(f32[4,8,128]{2,1,0:T(8,128)S(1)} %bitcast.17), channel_id=1, source_target_pairs={{1,2},{2,1},{3,4},{4,3},{5,6},{6,5},{7,8},{8,7},{9,10},{10,9},{11,... | collective-permute-start | bytes 49160 | tf_op jit(solution)/shard_map/ppermute | solution.py:693
  66.5 1.8 %shard_map.128 = (f32[6,28,72,128]{3,2,1,0:T(8,128)S(1)}, f32[288,16,128]{2,1,0:T(8,128)}, f32[48,128]{1,0:T(8,128)S(1)}) custom-call(bf16[2,4,256,256]{3,2,1,0:T(8,128)(2,1)S(1)} %copy-done, f32[4,8,128]{2,1,0:T(8,128)S(1)} %bitcast.18, s32[8,128]{1,0:T(8,128)S(1)} %get-tuple-element.78.used_ref, ...), custom_call_target="tpu_custom_call", output_to_operand_aliasing={{0}: (4, {}), {1}: (6, {})} | custom-call | tf_op jit(solution)/shard_map/pallas_call | solution.py:694
  68.3 0.0 collective-permute-done.10.first_ref
  68.3 2.0 %collective-permute-done.11.second_ref = f32[4,8,128]{2,1,0:T(8,128)S(1)} collective-permute-done((f32[4,8,128]{2,1,0:T(8,128)S(1)}, f32[4,8,128]{2,1,0:T(8,128)S(1)}, u32[]{:S(2)}, u32[]{:S(2)}) %collective-permute-start.11) | collective-permute-done | bytes 16416 | tf_op jit(solution)/shard_map/ppermute | solution.py:693
  70.3 1.4 %shard_map.129 = f32[288,16,128]{2,1,0:T(8,128)} custom-call(f32[3,28,72,128]{3,2,1,0:T(8,128)S(1)} %get-tuple-element.76.v_ref, f32[4,8,128]{2,1,0:T(8,128)S(1)} %collective-permute-done.10.first_ref, f32[4,8,128]{2,1,0:T(8,128)S(1)} %collective-permute-done.11.second_ref, s32[8,128]{1,0:T(8,128)S(1)} %get-tuple-element.78.used_ref, ...), custom_call_target="tpu_custom_call", output_to_operand_aliasing={{}: (6, {})} | custom-call | tf_op jit(solution)/shard_map/pallas_call | solution.py:699
Async XLA Ops:
  0.0 12.1 %copy-start.2 = (f32[32,16,128]{2,1,0:T(8,128)S(1)}, f32[32,16,128]{2,1,0:T(8,128)}, u32[]{:S(2)}) copy-start(f32[32,16,128]{2,1,0:T(8,128)} %param.13) | copy-start | bytes 786436
  0.0 12.1 %copy-start.3 = (f32[32,16,128]{2,1,0:T(8,128)S(1)}, f32[32,16,128]{2,1,0:T(8,128)}, u32[]{:S(2)}) copy-start(f32[32,16,128]{2,1,0:T(8,128)} %param.14) | copy-start | bytes 786436
  0.0 12.1 %copy-start.4 = (f32[32,16,128]{2,1,0:T(8,128)S(1)}, f32[32,16,128]{2,1,0:T(8,128)}, u32[]{:S(2)}) copy-start(f32[32,16,128]{2,1,0:T(8,128)} %param.15) | copy-start | bytes 786436
  4.3 12.6 %collective-permute-start.2 = (f32[66,8,128]{2,1,0:T(8,128)}, f32[66,8,128]{2,1,0:T(8,128)S(1)}, u32[]{:S(2)}, u32[]{:S(2)}) collective-permute-start(f32[66,8,128]{2,1,0:T(8,128)} %get-tuple-element.47), channel_id=1, source_target_pairs={{0,1},{1,0},{2,3},{3,2},{4,5},{5,4},{6,7},{7,6},{8,9},{9,8},{10,11... | collective-permute-start | bytes 811016 | tf_op jit(solution)/shard_map/ppermute | solution.py:641
  5.7 13.1 %collective-permute-start.1 = (f32[66,8,128]{2,1,0:T(8,128)}, f32[66,8,128]{2,1,0:T(8,128)S(1)}, u32[]{:S(2)}, u32[]{:S(2)}) collective-permute-start(f32[66,8,128]{2,1,0:T(8,128)} %get-tuple-element.46), channel_id=1, source_target_pairs={{1,2},{2,1},{3,4},{4,3},{5,6},{6,5},{7,8},{8,7},{9,10},{10,9},{11,... | collective-permute-start | bytes 811016 | tf_op jit(solution)/shard_map/ppermute | solution.py:642
  12.1 1.7 %copy-start.1 = (f32[9,32,16,128]{3,2,1,0:T(8,128)S(1)}, f32[9,32,16,128]{3,2,1,0:T(8,128)}, u32[]{:S(2)}) copy-start(f32[9,32,16,128]{3,2,1,0:T(8,128)} %param.12) | copy-start | bytes 7077892
  15.0 19.3 %collective-permute-start = (f32[59,32,128]{2,1,0:T(8,128)S(1)}, f32[59,32,128]{2,1,0:T(8,128)S(1)}, u32[]{:S(2)}, u32[]{:S(2)}) collective-permute-start(f32[59,32,128]{2,1,0:T(8,128)S(1)} %get-tuple-element.45), channel_id=1, source_target_pairs={{32,64},{64,32},{33,65},{65,33},{34,66},{66,34},{35,67},{67,35},{3... | collective-permute-start | bytes 2899976 | tf_op jit(solution)/shard_map/ppermute | solution.py:647
  18.8 4.1 %copy-start = (bf16[2,4,256,256]{3,2,1,0:T(8,128)(2,1)S(1)}, bf16[2,4,256,256]{3,2,1,0:T(8,128)(2,1)}, u32[]{:S(2)}) copy-start(bf16[2,4,256,256]{3,2,1,0:T(8,128)(2,1)} %constant.2.clone.refs_0_.band_ref) | copy-start | bytes 3145732
  19.2 3.7 %collective-permute-start.4 = (f32[23,40,128]{2,1,0:T(8,128)S(1)}, f32[23,40,128]{2,1,0:T(8,128)S(1)}, u32[]{:S(2)}, u32[]{:S(2)}) collective-permute-start(f32[23,40,128]{2,1,0:T(8,128)S(1)} %get-tuple-element.52), channel_id=1, source_target_pairs={{0,32},{32,0},{64,96},{96,64},{1,33},{33,1},{65,97},{97,65},{2,34}... | collective-permute-start | bytes 1413128 | tf_op jit(solution)/shard_map/ppermute | solution.py:659
  19.3 15.0 %collective-permute-start.3 = (f32[59,8,128]{2,1,0:T(8,128)S(1)}, f32[59,8,128]{2,1,0:T(8,128)S(1)}, u32[]{:S(2)}, u32[]{:S(2)}) collective-permute-start(f32[59,8,128]{2,1,0:T(8,128)S(1)} %get-tuple-element.51), channel_id=1, source_target_pairs={{32,64},{64,32},{33,65},{65,33},{34,66},{66,34},{35,67},{67,35},{3... | collective-permute-start | bytes 725000 | tf_op jit(solution)/shard_map/ppermute | solution.py:660
  26.8 1.9 %collective-permute-start.5 = (f32[11,40,128]{2,1,0:T(8,128)S(1)}, f32[11,40,128]{2,1,0:T(8,128)S(1)}, u32[]{:S(2)}, u32[]{:S(2)}) collective-permute-start(f32[11,40,128]{2,1,0:T(8,128)S(1)} %get-tuple-element.56), channel_id=1, source_target_pairs={{0,32},{32,0},{64,96},{96,64},{1,33},{33,1},{65,97},{97,65},{2,34}... | collective-permute-start | bytes 675848 | tf_op jit(solution)/shard_map/ppermute | solution.py:668
  26.9 1.8 %collective-permute-start.6 = (f32[10,40,128]{2,1,0:T(8,128)S(1)}, f32[10,40,128]{2,1,0:T(8,128)S(1)}, u32[]{:S(2)}, u32[]{:S(2)}) collective-permute-start(f32[10,40,128]{2,1,0:T(8,128)S(1)} %get-tuple-element.57), channel_id=1, source_target_pairs={{0,32},{32,0},{64,96},{96,64},{1,33},{33,1},{65,97},{97,65},{2,34}... | collective-permute-start | bytes 614408 | tf_op jit(solution)/shard_map/ppermute | solution.py:668
  36.9 15.9 %collective-permute-start.7 = (f32[216,8,128]{2,1,0:T(8,128)S(1)}, f32[216,8,128]{2,1,0:T(8,128)S(1)}, u32[]{:S(2)}, u32[]{:S(2)}) collective-permute-start(f32[216,8,128]{2,1,0:T(8,128)S(1)} %get-tuple-element.64), channel_id=1, source_target_pairs={{32,64},{64,32},{33,65},{65,33},{34,66},{66,34},{35,67},{67,35},{3... | collective-permute-start | bytes 2654216 | tf_op jit(solution)/shard_map/ppermute | solution.py:660
  38.8 1.9 %collective-permute-start.8 = (f32[21,40,128]{2,1,0:T(8,128)S(1)}, f32[21,40,128]{2,1,0:T(8,128)S(1)}, u32[]{:S(2)}, u32[]{:S(2)}) collective-permute-start(f32[21,40,128]{2,1,0:T(8,128)S(1)} %get-tuple-element.65), channel_id=1, source_target_pairs={{0,32},{32,0},{64,96},{96,64},{1,33},{33,1},{65,97},{97,65},{2,34}... | collective-permute-start | bytes 1290248 | tf_op jit(solution)/shard_map/ppermute | solution.py:659
  40.7 4.6 %copy-start.5 = (f32[3,32]{1,0:T(4,128)S(1)}, f32[3,32]{1,0:T(4,128)}, u32[]{:S(2)}) copy-start(f32[3,32]{1,0:T(4,128)} %profile_ref.1) | copy-start | bytes 1156
  40.7 4.6 %copy-start.7 = (s32[1,64]{1,0:T(1,128)S(1)}, s32[1,64]{1,0:T(1,128)}, u32[]{:S(2)}) copy-start(s32[1,64]{1,0:T(1,128)} %influence_ref.1) | copy-start | bytes 772
  43.2 2.0 %collective-permute-start.9 = (f32[21,40,128]{2,1,0:T(8,128)S(1)}, f32[21,40,128]{2,1,0:T(8,128)S(1)}, u32[]{:S(2)}, u32[]{:S(2)}) collective-permute-start(f32[21,40,128]{2,1,0:T(8,128)S(1)} %get-tuple-element.69), channel_id=1, source_target_pairs={{0,32},{32,0},{64,96},{96,64},{1,33},{33,1},{65,97},{97,65},{2,34}... | collective-permute-start | bytes 1290248 | tf_op jit(solution)/shard_map/ppermute | solution.py:668
  45.3 7.5 %copy-start.6 = (f32[3,32]{1,0:T(4,128)S(1)}, f32[3,32]{1,0:T(4,128)}, u32[]{:S(2)}) copy-start(f32[3,32]{1,0:T(4,128)} %observed_ref.1) | copy-start | bytes 1156
  45.3 7.5 %copy-start.8 = (f32[32]{0:T(128)S(1)}, f32[32]{0:T(128)}, u32[]{:S(2)}) copy-start(f32[32]{0:T(128)} %param.17) | copy-start | bytes 388
  45.3 7.5 %copy-start.9 = (s32[32]{0:T(128)S(1)}, s32[32]{0:T(128)}, u32[]{:S(2)}) copy-start(s32[32]{0:T(128)} %param.19) | copy-start | bytes 388
  61.7 6.6 %collective-permute-start.10 = (f32[4,8,128]{2,1,0:T(8,128)S(1)}, f32[4,8,128]{2,1,0:T(8,128)S(1)}, u32[]{:S(2)}, u32[]{:S(2)}) collective-permute-start(f32[4,8,128]{2,1,0:T(8,128)S(1)} %bitcast.16), channel_id=1, source_target_pairs={{0,1},{1,0},{2,3},{3,2},{4,5},{5,4},{6,7},{7,6},{8,9},{9,8},{10,11... | collective-permute-start | bytes 49160 | tf_op jit(solution)/shard_map/ppermute | solution.py:692
  61.7 8.6 %collective-permute-start.11 = (f32[4,8,128]{2,1,0:T(8,128)S(1)}, f32[4,8,128]{2,1,0:T(8,128)S(1)}, u32[]{:S(2)}, u32[]{:S(2)}) collective-permute-start(f32[4,8,128]{2,1,0:T(8,128)S(1)} %bitcast.17), channel_id=1, source_target_pairs={{1,2},{2,1},{3,4},{4,3},{5,6},{6,5},{7,8},{8,7},{9,10},{10,9},{11,... | collective-permute-start | bytes 49160 | tf_op jit(solution)/shard_map/ppermute | solution.py:693

commit v8 on v7

--- a/solution.py
+++ b/solution.py
@@ -430,7 +430,7 @@
             pad_halo(t_ref, f, x)
         return 0
 
-    lax.fori_loop(LOW, LOW + CX, pads, 0)
+    lax.fori_loop(LOW, LOW + CX, pads, 0, unroll=4)
 
 
 def near_step(items, back, odd, read, v_ref, t_ref, p_ref, band_ref, d_ref):

time: 72.2 us -> 72.2 us (level)
  Pallas kernels: 26.3 us -> 25.5 us
  waiting for transfers between devices: 14.4 us -> 15.2 us
    pallas_call x2, Pallas kernels: 6.3 us -> 5.47 us  [per_device(): call(bind(near_kernel, INNER_FIRST if block == 0 else INNER, 0, 1, split)...]
    ppermute x2, waiting for transfers between devices: 7.42 us -> 8.25 us  [per_device(): got_outer = lax.ppermute(outer, 'region', OUTER_SWAP)]
  transfers between devices with their start and end apart: 12 -> 12, of which waited for: 7 -> 7; matrix products, arithmetic and copies ran while one was open for 0% -> 0% of each run, Pallas kernels for 22% -> 21%
where the time goes in v8:
time: 72.2 us; the launch traced here: 71.9 us
  Pallas kernels  25.5 us (35%)
  starting transfers between devices  21.1 us (29%)
  waiting for transfers between devices  15.2 us (21%)
  blocking collectives  6.68 us (9%)
  local copies, waits for them, and re-layouts  1.7 us (2%)
  between operations  1.69 us (2%)
    ppermute x2, waiting for transfers between devices, per_device(): got_outer = lax.ppermute(outer, 'region', OUTER_SWAP)  8.25 us
    all_gather x1, blocking collectives, per_device(): here = lax.all_gather(packet, 'region')  6.68 us
    ppermute x1, starting transfers between devices, per_device(): got_second = lax.ppermute(second, 'tile', pairs(1))  6.38 us
    ppermute x2, starting transfers between devices, per_device(): got_outer = lax.ppermute(outer, 'region', OUTER_SWAP)  5.55 us
    pallas_call x2, Pallas kernels, per_device(): call(bind(near_kernel, INNER_FIRST if block == 0 else INNER, 0, 1, split)...  5.47 us
    ppermute x1, starting transfers between devices, per_device(): got_second = lax.ppermute(here, 'tile', pairs(1))  4.79 us
    pallas_call x1, Pallas kernels, per_device(): call(edge_kernel, (packed, packed), [HB] * 4, fetched, vmem=62 * 2 ** 20)  4.32 us
    pallas_call x1, Pallas kernels, per_device(): call(last_near_kernel, state + (result, jax.ShapeDtypeStruct((8, 128), jn...  3.72 us
  transfers between devices with their start and end apart: 12, of which 7 were waited for; matrix products, arithmetic and copies ran while one was open for 0% of the time, Pallas kernels for 21%

profile of v8, /device:TPU:22, one launch (start us, length us, event | category | flops | bytes accessed | tf_op | source)
XLA Modules:
  0.0 71.9 jit_solution(2410754222626449546)
XLA Ops:
  0.0 0.0 copy-start.2
  0.0 0.0 copy-start.3
  0.0 0.0 copy-start.4
  0.0 4.3 %shard_map.119 = (f32[66,8,128]{2,1,0:T(8,128)}, f32[66,8,128]{2,1,0:T(8,128)}) custom-call(f32[4608,128]{1,0:T(8,128)} %bitcast.8, f32[512,128]{1,0:T(8,128)} %bitcast.10, f32[512,128]{1,0:T(8,128)} %bitcast.12, f32[512,128]{1,0:T(8,128)} %bitcast.14), custom_call_target="tpu_custom_call" | custom-call | tf_op jit(solution)/shard_map/pallas_call | solution.py:639
  4.3 1.4 %collective-permute-start.2 = (f32[66,8,128]{2,1,0:T(8,128)}, f32[66,8,128]{2,1,0:T(8,128)S(1)}, u32[]{:S(2)}, u32[]{:S(2)}) collective-permute-start(f32[66,8,128]{2,1,0:T(8,128)} %get-tuple-element.47), channel_id=1, source_target_pairs={{0,1},{1,0},{2,3},{3,2},{4,5},{5,4},{6,7},{7,6},{8,9},{9,8},{10,11... | collective-permute-start | bytes 811016 | tf_op jit(solution)/shard_map/ppermute | solution.py:641
  5.7 6.4 %collective-permute-start.1 = (f32[66,8,128]{2,1,0:T(8,128)}, f32[66,8,128]{2,1,0:T(8,128)S(1)}, u32[]{:S(2)}, u32[]{:S(2)}) collective-permute-start(f32[66,8,128]{2,1,0:T(8,128)} %get-tuple-element.46), channel_id=1, source_target_pairs={{1,2},{2,1},{3,4},{4,3},{5,6},{6,5},{7,8},{8,7},{9,10},{10,9},{11,... | collective-permute-start | bytes 811016 | tf_op jit(solution)/shard_map/ppermute | solution.py:642
  12.1 0.0 copy-done.2
  12.1 0.0 copy-done.3
  12.1 0.0 copy-done.4
  12.1 0.0 copy-start.1
  12.1 1.7 %copy-done.1 = f32[9,32,16,128]{3,2,1,0:T(8,128)S(1)} copy-done((f32[9,32,16,128]{3,2,1,0:T(8,128)S(1)}, f32[9,32,16,128]{3,2,1,0:T(8,128)}, u32[]{:S(2)}) %copy-start.1) | copy-done | bytes 2359320
  13.8 1.2 %shard_map.118 = (f32[3,28,72,128]{3,2,1,0:T(8,128)S(1)}, f32[6,28,72,128]{3,2,1,0:T(8,128)S(1)}, f32[3,28,40,128]{3,2,1,0:T(8,128)S(1)}, f32[59,32,128]{2,1,0:T(8,128)S(1)}) custom-call(f32[4608,128]{1,0:T(8,128)S(1)} %bitcast.9, f32[512,128]{1,0:T(8,128)S(1)} %bitcast.11, f32[512,128]{1,0:T(8,128)S(1)} %bitcast.13, f32[512,128]{1,0:T(8,128)S(1)} %bitcast.15), custom_call_target="tpu_custom_call" | custom-call | bytes 100000000 | tf_op jit(solution)/shard_map/pallas_call | solution.py:644
  15.0 1.9 %collective-permute-start = (f32[59,32,128]{2,1,0:T(8,128)S(1)}, f32[59,32,128]{2,1,0:T(8,128)S(1)}, u32[]{:S(2)}, u32[]{:S(2)}) collective-permute-start(f32[59,32,128]{2,1,0:T(8,128)S(1)} %get-tuple-element.45), channel_id=1, source_target_pairs={{32,64},{64,32},{33,65},{65,33},{34,66},{66,34},{35,67},{67,35},{3... | collective-permute-start | bytes 2899976 | tf_op jit(solution)/shard_map/ppermute | solution.py:647
  16.9 0.0 collective-permute-done.2.got_ref
  16.9 0.3 shard_map.120.half_ref
  17.3 1.5 %collective-permute-done.1.got_ref = f32[66,8,128]{2,1,0:T(8,128)S(1)} collective-permute-done((f32[66,8,128]{2,1,0:T(8,128)}, f32[66,8,128]{2,1,0:T(8,128)S(1)}, u32[]{:S(2)}, u32[]{:S(2)}) %collective-permute-start.1) | collective-permute-done | bytes 270368 | tf_op jit(solution)/shard_map/ppermute | solution.py:642
  18.8 0.0 copy-start
  18.8 0.4 shard_map.121
  19.2 0.1 collective-permute-start.4
  19.3 3.6 %collective-permute-start.3 = (f32[59,8,128]{2,1,0:T(8,128)S(1)}, f32[59,8,128]{2,1,0:T(8,128)S(1)}, u32[]{:S(2)}, u32[]{:S(2)}) collective-permute-start(f32[59,8,128]{2,1,0:T(8,128)S(1)} %get-tuple-element.51), channel_id=1, source_target_pairs={{32,64},{64,32},{33,65},{65,33},{34,66},{66,34},{35,67},{67,35},{3... | collective-permute-start | bytes 725000 | tf_op jit(solution)/shard_map/ppermute | solution.py:660
  23.0 0.0 collective-permute-done.4.refs_1_
  23.0 0.0 copy-done
  23.0 3.0 %shard_map.122 = (f32[3,28,72,128]{3,2,1,0:T(8,128)S(1)}, f32[6,28,72,128]{3,2,1,0:T(8,128)S(1)}, f32[3,28,40,128]{3,2,1,0:T(8,128)S(1)}, f32[11,40,128]{2,1,0:T(8,128)S(1)}, f32[10,40,128]{2,1,0:T(8,128)S(1)}) custom-call(bf16[2,4,256,256]{3,2,1,0:T(8,128)(2,1)S(1)} %copy-done, ...), custom_call_target="tpu_custom_call", output_to_operand_aliasing={{0}: (2, {}), {1}: (3, {}), {2}: (4, {})} | custom-call | flops 1024 | bytes 1024 | tf_op jit(solution)/shard_map/pallas_call | solution.py:663
  26.0 0.1 collective-permute-start.5
  26.1 0.5 collective-permute-start.6
  26.5 1.3 %collective-permute-done.6.refs_2_ = f32[10,40,128]{2,1,0:T(8,128)S(1)} collective-permute-done((f32[10,40,128]{2,1,0:T(8,128)S(1)}, f32[10,40,128]{2,1,0:T(8,128)S(1)}, u32[]{:S(2)}, u32[]{:S(2)}) %collective-permute-start.6) | collective-permute-done | bytes 204832 | tf_op jit(solution)/shard_map/ppermute | solution.py:668
  27.8 0.0 collective-permute-done.5.refs_1_
  27.8 2.0 %shard_map.123 = (f32[3,28,72,128]{3,2,1,0:T(8,128)S(1)}, f32[6,28,72,128]{3,2,1,0:T(8,128)S(1)}, f32[3,28,40,128]{3,2,1,0:T(8,128)S(1)}, f32[21,40,128]{2,1,0:T(8,128)S(1)}) custom-call(bf16[2,4,256,256]{3,2,1,0:T(8,128)(2,1)S(1)} %copy-done, ...), custom_call_target="tpu_custom_call", output_to_operand_aliasing={{0}: (3, {}), {1}: (4, {}), {2}: (5, {})} | custom-call | flops 1024 | bytes 1024 | tf_op jit(solution)/shard_map/pallas_call | solution.py:670
  29.9 4.5 %collective-permute-done.3.got_halo = f32[59,8,128]{2,1,0:T(8,128)S(1)} collective-permute-done((f32[59,8,128]{2,1,0:T(8,128)S(1)}, f32[59,8,128]{2,1,0:T(8,128)S(1)}, u32[]{:S(2)}, u32[]{:S(2)}) %collective-permute-start.3) | collective-permute-done | bytes 241696 | tf_op jit(solution)/shard_map/ppermute | solution.py:660
  34.3 0.0 collective-permute-done.got_own
  34.3 2.6 %shard_map.124 = (f32[3,28,72,128]{3,2,1,0:T(8,128)S(1)}, f32[6,28,72,128]{3,2,1,0:T(8,128)S(1)}, f32[3,28,40,128]{3,2,1,0:T(8,128)S(1)}, f32[216,8,128]{2,1,0:T(8,128)S(1)}) custom-call(bf16[2,4,256,256]{3,2,1,0:T(8,128)(2,1)S(1)} %copy-done, ...), custom_call_target="tpu_custom_call", output_to_operand_aliasing={{0}: (3, {}), {1}: (4, {}), {2}: (5, {})} | custom-call | tf_op jit(solution)/shard_map/pallas_call | solution.py:674
  36.9 1.9 %collective-permute-start.7 = (f32[216,8,128]{2,1,0:T(8,128)S(1)}, f32[216,8,128]{2,1,0:T(8,128)S(1)}, u32[]{:S(2)}, u32[]{:S(2)}) collective-permute-start(f32[216,8,128]{2,1,0:T(8,128)S(1)} %get-tuple-element.64), channel_id=1, source_target_pairs={{32,64},{64,32},{33,65},{65,33},{34,66},{66,34},{35,67},{67,35},{3... | collective-permute-start | bytes 2654216 | tf_op jit(solution)/shard_map/ppermute | solution.py:660
  38.8 0.1 collective-permute-start.8
  38.9 1.8 %collective-permute-done.8.refs_1_ = f32[21,40,128]{2,1,0:T(8,128)S(1)} collective-permute-done((f32[21,40,128]{2,1,0:T(8,128)S(1)}, f32[21,40,128]{2,1,0:T(8,128)S(1)}, u32[]{:S(2)}, u32[]{:S(2)}) %collective-permute-start.8) | collective-permute-done | bytes 430112 | tf_op jit(solution)/shard_map/ppermute | solution.py:659
  40.7 0.0 copy-start.5
  40.7 0.0 copy-start.7
  40.7 2.5 %shard_map.125 = (f32[3,28,72,128]{3,2,1,0:T(8,128)S(1)}, f32[6,28,72,128]{3,2,1,0:T(8,128)S(1)}, f32[3,28,40,128]{3,2,1,0:T(8,128)S(1)}, f32[21,40,128]{2,1,0:T(8,128)S(1)}) custom-call(bf16[2,4,256,256]{3,2,1,0:T(8,128)(2,1)S(1)} %copy-done, ...), custom_call_target="tpu_custom_call", output_to_operand_aliasing={{0}: (2, {}), {1}: (3, {}), {2}: (4, {})} | custom-call | flops 1024 | bytes 1024 | tf_op jit(solution)/shard_map/pallas_call | solution.py:663
  43.2 0.4 collective-permute-start.9
  44.9 0.4 collective-permute-done.9.got_ref
  45.2 0.0 copy-done.5
  45.2 0.0 copy-done.7
  45.3 0.0 copy-start.6
  45.3 0.0 copy-start.8
  45.3 0.0 copy-start.9
  45.3 3.7 %shard_map.126 = (f32[3,28,72,128]{3,2,1,0:T(8,128)S(1)}, f32[6,28,72,128]{3,2,1,0:T(8,128)S(1)}, f32[3,28,40,128]{3,2,1,0:T(8,128)S(1)}, f32[288,16,128]{2,1,0:...) custom-call(s32[1,64]{1,0:T(1,128)S(1)} %copy-done.7, ...), custom_call_target="tpu_custom_call", output_to_operand_aliasing={{0}: (5, {}), {1}: (6, {}), {2}: (7, {})} | custom-call | tf_op jit(solution)/shard_map/pallas_call | solution.py:679
  49.0 3.8 %collective-permute-done.7.got_ref = f32[216,8,128]{2,1,0:T(8,128)S(1)} collective-permute-done((f32[216,8,128]{2,1,0:T(8,128)S(1)}, f32[216,8,128]{2,1,0:T(8,128)S(1)}, u32[]{:S(2)}, u32[]{:S(2)}) %collective-permute-start.7) | collective-permute-done | bytes 884768 | tf_op jit(solution)/shard_map/ppermute | solution.py:660
  52.8 0.0 copy-done.6
  52.8 0.0 copy-done.8
  52.8 0.0 copy-done.9
  52.8 2.2 %shard_map.127 = (f32[3,28,72,128]{3,2,1,0:T(8,128)S(1)}, f32[6,28,72,128]{3,2,1,0:T(8,128)S(1)}, f32[3,28,40,128]{3,2,1,0:T(8,128)S(1)}, f32[8,128]{1,0:T(8,128)S(1)}) custom-call(s32[1]{0:T(128)S(6)} %copy.61.count_ref, f32[3,32]{1,0:T(4,128)S(1)} %copy-done.6, f32[1,32]{1,0:T(1,128)S(1)} %bitcast.19, ...), custom_call_target="tpu_custom_call", output_to_operand_aliasing={{0}: (6, {}), {1}: (7, {}), {2}: (8, {})} | custom-call | tf_op jit(solution)/shard_map/pallas_call | solution.py:686
  55.0 6.7 %all-gather = f32[32,128]{1,0:T(8,128)S(1)} all-gather(f32[8,128]{1,0:T(8,128)S(1)} %get-tuple-element.77), channel_id=2, replica_groups=mesh['region'=4,'tile'=32] {'region'}, dimensions={0}, use_global_device_ids=true | all-gather | bytes 20480 | tf_op jit(solution)/shard_map/all_gather | solution.py:691
  61.7 0.0 collective-permute-start.10
  61.7 4.8 %collective-permute-start.11 = (f32[4,8,128]{2,1,0:T(8,128)S(1)}, f32[4,8,128]{2,1,0:T(8,128)S(1)}, u32[]{:S(2)}, u32[]{:S(2)}) collective-permute-start(f32[4,8,128]{2,1,0:T(8,128)S(1)} %bitcast.17), channel_id=1, source_target_pairs={{1,2},{2,1},{3,4},{4,3},{5,6},{6,5},{7,8},{8,7},{9,10},{10,9},{11,... | collective-permute-start | bytes 49160 | tf_op jit(solution)/shard_map/ppermute | solution.py:693
  66.5 1.8 %shard_map.128 = (f32[6,28,72,128]{3,2,1,0:T(8,128)S(1)}, f32[288,16,128]{2,1,0:T(8,128)}, f32[48,128]{1,0:T(8,128)S(1)}) custom-call(bf16[2,4,256,256]{3,2,1,0:T(8,128)(2,1)S(1)} %copy-done, f32[4,8,128]{2,1,0:T(8,128)S(1)} %bitcast.18, s32[8,128]{1,0:T(8,128)S(1)} %get-tuple-element.78.used_ref, ...), custom_call_target="tpu_custom_call", output_to_operand_aliasing={{0}: (4, {}), {1}: (6, {})} | custom-call | tf_op jit(solution)/shard_map/pallas_call | solution.py:694
  68.3 0.0 collective-permute-done.10.first_ref
  68.3 2.0 %collective-permute-done.11.second_ref = f32[4,8,128]{2,1,0:T(8,128)S(1)} collective-permute-done((f32[4,8,128]{2,1,0:T(8,128)S(1)}, f32[4,8,128]{2,1,0:T(8,128)S(1)}, u32[]{:S(2)}, u32[]{:S(2)}) %collective-permute-start.11) | collective-permute-done | bytes 16416 | tf_op jit(solution)/shard_map/ppermute | solution.py:693
  70.3 1.4 %shard_map.129 = f32[288,16,128]{2,1,0:T(8,128)} custom-call(f32[3,28,72,128]{3,2,1,0:T(8,128)S(1)} %get-tuple-element.76.v_ref, f32[4,8,128]{2,1,0:T(8,128)S(1)} %collective-permute-done.10.first_ref, f32[4,8,128]{2,1,0:T(8,128)S(1)} %collective-permute-done.11.second_ref, s32[8,128]{1,0:T(8,128)S(1)} %get-tuple-element.78.used_ref, ...), custom_call_target="tpu_custom_call", output_to_operand_aliasing={{}: (6, {})} | custom-call | tf_op jit(solution)/shard_map/pallas_call | solution.py:699
Async XLA Ops:
  0.0 12.1 %copy-start.2 = (f32[32,16,128]{2,1,0:T(8,128)S(1)}, f32[32,16,128]{2,1,0:T(8,128)}, u32[]{:S(2)}) copy-start(f32[32,16,128]{2,1,0:T(8,128)} %param.13) | copy-start | bytes 786436
  0.0 12.1 %copy-start.3 = (f32[32,16,128]{2,1,0:T(8,128)S(1)}, f32[32,16,128]{2,1,0:T(8,128)}, u32[]{:S(2)}) copy-start(f32[32,16,128]{2,1,0:T(8,128)} %param.14) | copy-start | bytes 786436
  0.0 12.1 %copy-start.4 = (f32[32,16,128]{2,1,0:T(8,128)S(1)}, f32[32,16,128]{2,1,0:T(8,128)}, u32[]{:S(2)}) copy-start(f32[32,16,128]{2,1,0:T(8,128)} %param.15) | copy-start | bytes 786436
  4.3 12.6 %collective-permute-start.2 = (f32[66,8,128]{2,1,0:T(8,128)}, f32[66,8,128]{2,1,0:T(8,128)S(1)}, u32[]{:S(2)}, u32[]{:S(2)}) collective-permute-start(f32[66,8,128]{2,1,0:T(8,128)} %get-tuple-element.47), channel_id=1, source_target_pairs={{0,1},{1,0},{2,3},{3,2},{4,5},{5,4},{6,7},{7,6},{8,9},{9,8},{10,11... | collective-permute-start | bytes 811016 | tf_op jit(solution)/shard_map/ppermute | solution.py:641
  5.7 13.1 %collective-permute-start.1 = (f32[66,8,128]{2,1,0:T(8,128)}, f32[66,8,128]{2,1,0:T(8,128)S(1)}, u32[]{:S(2)}, u32[]{:S(2)}) collective-permute-start(f32[66,8,128]{2,1,0:T(8,128)} %get-tuple-element.46), channel_id=1, source_target_pairs={{1,2},{2,1},{3,4},{4,3},{5,6},{6,5},{7,8},{8,7},{9,10},{10,9},{11,... | collective-permute-start | bytes 811016 | tf_op jit(solution)/shard_map/ppermute | solution.py:642
  12.1 1.7 %copy-start.1 = (f32[9,32,16,128]{3,2,1,0:T(8,128)S(1)}, f32[9,32,16,128]{3,2,1,0:T(8,128)}, u32[]{:S(2)}) copy-start(f32[9,32,16,128]{3,2,1,0:T(8,128)} %param.12) | copy-start | bytes 7077892
  15.0 19.3 %collective-permute-start = (f32[59,32,128]{2,1,0:T(8,128)S(1)}, f32[59,32,128]{2,1,0:T(8,128)S(1)}, u32[]{:S(2)}, u32[]{:S(2)}) collective-permute-start(f32[59,32,128]{2,1,0:T(8,128)S(1)} %get-tuple-element.45), channel_id=1, source_target_pairs={{32,64},{64,32},{33,65},{65,33},{34,66},{66,34},{35,67},{67,35},{3... | collective-permute-start | bytes 2899976 | tf_op jit(solution)/shard_map/ppermute | solution.py:647
  18.8 4.1 %copy-start = (bf16[2,4,256,256]{3,2,1,0:T(8,128)(2,1)S(1)}, bf16[2,4,256,256]{3,2,1,0:T(8,128)(2,1)}, u32[]{:S(2)}) copy-start(bf16[2,4,256,256]{3,2,1,0:T(8,128)(2,1)} %constant.2.clone.refs_0_.band_ref) | copy-start | bytes 3145732
  19.2 3.7 %collective-permute-start.4 = (f32[23,40,128]{2,1,0:T(8,128)S(1)}, f32[23,40,128]{2,1,0:T(8,128)S(1)}, u32[]{:S(2)}, u32[]{:S(2)}) collective-permute-start(f32[23,40,128]{2,1,0:T(8,128)S(1)} %get-tuple-element.52), channel_id=1, source_target_pairs={{0,32},{32,0},{64,96},{96,64},{1,33},{33,1},{65,97},{97,65},{2,34}... | collective-permute-start | bytes 1413128 | tf_op jit(solution)/shard_map/ppermute | solution.py:659
  19.3 15.0 %collective-permute-start.3 = (f32[59,8,128]{2,1,0:T(8,128)S(1)}, f32[59,8,128]{2,1,0:T(8,128)S(1)}, u32[]{:S(2)}, u32[]{:S(2)}) collective-permute-start(f32[59,8,128]{2,1,0:T(8,128)S(1)} %get-tuple-element.51), channel_id=1, source_target_pairs={{32,64},{64,32},{33,65},{65,33},{34,66},{66,34},{35,67},{67,35},{3... | collective-permute-start | bytes 725000 | tf_op jit(solution)/shard_map/ppermute | solution.py:660
  26.0 1.9 %collective-permute-start.5 = (f32[11,40,128]{2,1,0:T(8,128)S(1)}, f32[11,40,128]{2,1,0:T(8,128)S(1)}, u32[]{:S(2)}, u32[]{:S(2)}) collective-permute-start(f32[11,40,128]{2,1,0:T(8,128)S(1)} %get-tuple-element.56), channel_id=1, source_target_pairs={{0,32},{32,0},{64,96},{96,64},{1,33},{33,1},{65,97},{97,65},{2,34}... | collective-permute-start | bytes 675848 | tf_op jit(solution)/shard_map/ppermute | solution.py:668
  26.1 1.8 %collective-permute-start.6 = (f32[10,40,128]{2,1,0:T(8,128)S(1)}, f32[10,40,128]{2,1,0:T(8,128)S(1)}, u32[]{:S(2)}, u32[]{:S(2)}) collective-permute-start(f32[10,40,128]{2,1,0:T(8,128)S(1)} %get-tuple-element.57), channel_id=1, source_target_pairs={{0,32},{32,0},{64,96},{96,64},{1,33},{33,1},{65,97},{97,65},{2,34}... | collective-permute-start | bytes 614408 | tf_op jit(solution)/shard_map/ppermute | solution.py:668
  36.9 15.9 %collective-permute-start.7 = (f32[216,8,128]{2,1,0:T(8,128)S(1)}, f32[216,8,128]{2,1,0:T(8,128)S(1)}, u32[]{:S(2)}, u32[]{:S(2)}) collective-permute-start(f32[216,8,128]{2,1,0:T(8,128)S(1)} %get-tuple-element.64), channel_id=1, source_target_pairs={{32,64},{64,32},{33,65},{65,33},{34,66},{66,34},{35,67},{67,35},{3... | collective-permute-start | bytes 2654216 | tf_op jit(solution)/shard_map/ppermute | solution.py:660
  38.8 1.9 %collective-permute-start.8 = (f32[21,40,128]{2,1,0:T(8,128)S(1)}, f32[21,40,128]{2,1,0:T(8,128)S(1)}, u32[]{:S(2)}, u32[]{:S(2)}) collective-permute-start(f32[21,40,128]{2,1,0:T(8,128)S(1)} %get-tuple-element.65), channel_id=1, source_target_pairs={{0,32},{32,0},{64,96},{96,64},{1,33},{33,1},{65,97},{97,65},{2,34}... | collective-permute-start | bytes 1290248 | tf_op jit(solution)/shard_map/ppermute | solution.py:659
  40.7 4.6 %copy-start.5 = (f32[3,32]{1,0:T(4,128)S(1)}, f32[3,32]{1,0:T(4,128)}, u32[]{:S(2)}) copy-start(f32[3,32]{1,0:T(4,128)} %profile_ref.1) | copy-start | bytes 1156
  40.7 4.6 %copy-start.7 = (s32[1,64]{1,0:T(1,128)S(1)}, s32[1,64]{1,0:T(1,128)}, u32[]{:S(2)}) copy-start(s32[1,64]{1,0:T(1,128)} %influence_ref.1) | copy-start | bytes 772
  43.2 2.0 %collective-permute-start.9 = (f32[21,40,128]{2,1,0:T(8,128)S(1)}, f32[21,40,128]{2,1,0:T(8,128)S(1)}, u32[]{:S(2)}, u32[]{:S(2)}) collective-permute-start(f32[21,40,128]{2,1,0:T(8,128)S(1)} %get-tuple-element.69), channel_id=1, source_target_pairs={{0,32},{32,0},{64,96},{96,64},{1,33},{33,1},{65,97},{97,65},{2,34}... | collective-permute-start | bytes 1290248 | tf_op jit(solution)/shard_map/ppermute | solution.py:668
  45.3 7.5 %copy-start.6 = (f32[3,32]{1,0:T(4,128)S(1)}, f32[3,32]{1,0:T(4,128)}, u32[]{:S(2)}) copy-start(f32[3,32]{1,0:T(4,128)} %observed_ref.1) | copy-start | bytes 1156
  45.3 7.5 %copy-start.8 = (f32[32]{0:T(128)S(1)}, f32[32]{0:T(128)}, u32[]{:S(2)}) copy-start(f32[32]{0:T(128)} %param.17) | copy-start | bytes 388
  45.3 7.5 %copy-start.9 = (s32[32]{0:T(128)S(1)}, s32[32]{0:T(128)}, u32[]{:S(2)}) copy-start(s32[32]{0:T(128)} %param.19) | copy-start | bytes 388
  61.7 6.6 %collective-permute-start.10 = (f32[4,8,128]{2,1,0:T(8,128)S(1)}, f32[4,8,128]{2,1,0:T(8,128)S(1)}, u32[]{:S(2)}, u32[]{:S(2)}) collective-permute-start(f32[4,8,128]{2,1,0:T(8,128)S(1)} %bitcast.16), channel_id=1, source_target_pairs={{0,1},{1,0},{2,3},{3,2},{4,5},{5,4},{6,7},{7,6},{8,9},{9,8},{10,11... | collective-permute-start | bytes 49160 | tf_op jit(solution)/shard_map/ppermute | solution.py:692
  61.7 8.6 %collective-permute-start.11 = (f32[4,8,128]{2,1,0:T(8,128)S(1)}, f32[4,8,128]{2,1,0:T(8,128)S(1)}, u32[]{:S(2)}, u32[]{:S(2)}) collective-permute-start(f32[4,8,128]{2,1,0:T(8,128)S(1)} %bitcast.17), channel_id=1, source_target_pairs={{1,2},{2,1},{3,4},{4,3},{5,6},{6,5},{7,8},{8,7},{9,10},{10,9},{11,... | collective-permute-start | bytes 49160 | tf_op jit(solution)/shard_map/ppermute | solution.py:693
